TPU v7x, 32 devices: a whole 2x2x4 slice. The times are simulated.
32 devices in a mesh: group: 4 (over y, x), sub: 8 (over z, core).
Axes of the slice: x: 2, y: 2, z: 4, core: 2. Of those that a mesh axis runs over, the one named last changes fastest.
Arguments:
- points: float32 [3, 262144], P(None, ('group', 'sub')), as said below
- probes: float32 [32, 262144], P(None, ('group', 'sub')), may hold values from -6 to 6
- morton: int32 [262144], P(('group', 'sub')), may hold values from 0 to 8191, as said below
- near_list: int32 [2048, 27], P(('group', 'sub')), may hold values from -1 to 2047, as said below
- leaf_far: int32 [2048, 24], P(('group', 'sub')), may hold values from -1 to 2047, as said below
- box_far: int32 [256, 4], P(('group', 'sub')), may hold values from -1 to 255, as said below
- subtree_far: int32 [32, 4], P(('group', 'sub')), may hold values from -1 to 31, as said below
- leaf_skeleton: float32 [2048, 3, 64], P(('group', 'sub')), as said below
- box_skeleton: float32 [256, 3, 128], P(('group', 'sub')), as said below
- subtree_skeleton: float32 [32, 3, 256], P(('group', 'sub')), as said below
- group_skeleton: float32 [4, 3, 256], replicated, as said below
- leaf_basis: float32 [2048, 64, 128], P(('group', 'sub')), may hold values from -0.5 to 0.5
- leaf_transfer: float32 [2048, 64, 128], P(('group', 'sub')), may hold values from -0.25 to 0.25
- box_transfer: float32 [256, 128, 256], P(('group', 'sub')), may hold values from -0.1875 to 0.1875
- subtree_transfer: float32 [32, 256, 256], P(('group', 'sub')), may hold values from -0.375 to 0.375
Outputs:
- kernel_product: float32 [32, 262144], P(None, ('group', 'sub'))
Inputs may be any that keep to these rules, and one draw needn't show every extreme that they name: `morton`: each block of 8192 entries is a permutation of 0 to 8191. `near_list`: row l starts with l, then distinct leaves within 32 of l; -1 marks an empty slot. `leaf_far`: row l holds distinct leaves within 32 of l, none in its near list; -1 marks an empty slot. `box_far`: row b holds distinct other boxes of the same subtree; -1 marks an empty slot. `subtree_far`: row c holds distinct other subtrees of the same group; -1 marks an empty slot. `points`: coordinates in leaf-cell units. `leaf_skeleton`: coordinates in leaf-cell units. `box_skeleton`: coordinates in leaf-cell units. `subtree_skeleton`: coordinates in leaf-cell units. `group_skeleton`: coordinates in leaf-cell units.
All inputs are finite; a program needn't handle non-finite values.
Results may differ from a plain program's by a relative error of at most 0.0003.
Values sent between devices are 32-bit elements; how exact they have to be, the bound alone decides.
A program may use at most 128 MiB of HBM per device.

v0:
```python
import functools
import math

import jax
import jax.numpy as jnp
from jax import lax
from jax.experimental import pallas as pl
from jax.experimental.pallas import tpu as pltpu
from jax.sharding import PartitionSpec as P

P_SIZE = 128
CH = 8
HALO = 32
NEAR_STEP = 3
FAR_STEP = 4

highest = lax.Precision.HIGHEST
scale = math.sqrt(3.0) / 12.0 * math.log2(math.e)
soft = 0.0001 * scale * scale
ln2 = math.log(2.0)
f32 = jnp.float32
bf16 = jnp.bfloat16
NT = (((1,), (1,)), ((), ()))


def hdot(a, b):
    return jnp.dot(a, b, precision=highest, preferred_element_type=f32)


def hdot_nt(a, b):
    return lax.dot_general(a, b, NT, precision=highest, preferred_element_type=f32)


def profile(squared):
    squared = jnp.maximum(squared, soft)
    u = squared * lax.rsqrt(squared)
    return (1.0 + ln2 * u) * jnp.exp2(-u)


def split3(v):
    high = v.astype(bf16).astype(f32)
    rest = v - high
    mid = rest.astype(bf16).astype(f32)
    return high, mid, rest - mid


def augmented(x):
    row = lax.broadcasted_iota(jnp.int32, x.shape, 0)
    norm = jnp.sum(x * x, axis=0, keepdims=True)
    source = jnp.where(row < 3, -2.0 * x, jnp.where(row == 3, 1.0, jnp.where(row == 4, norm + soft, 0.0)))
    target = jnp.where(row < 3, x, jnp.where(row == 3, norm, jnp.where(row == 4, 1.0, 0.0)))
    return source, target


def source_rows(v):
    h, m, lo = split3(v)
    return jnp.concatenate([h, m, h, m, lo, h, lo, m], axis=0)


def target_rows(v):
    h, m, lo = split3(v)
    return jnp.concatenate([h, h, m, m, h, lo, m, lo], axis=0)


def coords(block, centre):
    row = lax.broadcasted_iota(jnp.int32, block.shape, 0)
    return jnp.where(row < 3, (block - centre) * scale, 0.0)


def arrange_kernel(
    morton, points, probes, skel, basis, leaf_tr, box_tr, sub_tr,
    geo, q1_out, q2_out, q3_out, rows, pad, got,
):
    leaves = geo.shape[0]
    boxes = q1_out.shape[0]
    pad[...] = jnp.zeros_like(pad)

    def flip(g, c):
        for j in range(4):
            at = pl.ds(pl.multiple_of((4 * g + j) * P_SIZE, P_SIZE), P_SIZE)
            pad[j, 0:32, :] = probes[:, at]
            pad[j, 32:35, :] = points[:, at]
        for j in range(4):
            at = pl.ds(pl.multiple_of((4 * g + j) * P_SIZE, P_SIZE), P_SIZE)
            rows[at, :] = pad[j].T
        return c

    lax.fori_loop(0, leaves // 4, flip, 0)

    def one_box(b, q2):
        for j in range(CH):
            base = (b * CH + j) * P_SIZE
            for k in range(P_SIZE):
                got[j, k : k + 1, :] = rows[pl.ds(morton[base + k], 1), :]
        turned = [got[j].T for j in range(CH)]
        parts = []
        for j in range(CH):
            i = b * CH + j
            geo[i, 0:40, :] = turned[j][0:40]
            geo[i, 35:38, 0:64] = skel[i]
            q0 = hdot_nt(turned[j][0:32], basis[i])
            geo[i, 40:56, 0:64] = q0[0:16]
            geo[i, 40:56, 64:128] = q0[16:32]
            parts.append(q0)
        q1 = jnp.zeros(q1_out.shape[1:], f32)
        for j in range(0, CH, 2):
            two = jnp.concatenate([leaf_tr[b * CH + j], leaf_tr[b * CH + j + 1]], axis=0)
            q1 = q1 + hdot(jnp.concatenate(parts[j : j + 2], axis=1), two)
        q1_out[b] = q1
        return q2 + hdot(q1, box_tr[b])

    q2 = lax.fori_loop(0, boxes, one_box, jnp.zeros(q2_out.shape, f32))
    q2_out[...] = q2
    q3_out[...] = hdot(q2, sub_tr[0])


def couple_kernel(
    near_ids, near_trips, far_ids, far_trips, left, own, right,
    near_out, far_out, src, tgt, xw, src_lo, src_hi, tgt2, qw,
    *, near_width, far_width, near_factor, far_factor,
):
    leaves = own.shape[0]
    total = leaves + 2 * HALO
    first = own[0, 32:40, 0:1]
    centre_pt = first
    centre_sk = jnp.concatenate([first[3:8], first[0:3]], axis=0)

    def prepare(ref, i, at, local):
        block = ref[i, 32:40, :]
        s8, t8 = augmented(coords(block, centre_pt))
        src[at] = source_rows(s8).T.astype(bf16)
        lane = lax.broadcasted_iota(jnp.int32, (8, P_SIZE), 1)
        turned = jnp.concatenate([block[3:8], block[0:3]], axis=0)
        ks8, kt8 = augmented(coords(turned, centre_sk))
        both = source_rows(ks8)
        zero = jnp.zeros_like(both)
        src_lo[at] = jnp.concatenate([both, zero], axis=0).T[0:64].astype(bf16)
        src_hi[at] = jnp.concatenate([zero, both], axis=0).T[0:64].astype(bf16)
        x = ref[i, 0:32, :]
        hi = x.astype(bf16)
        lo = (x - hi.astype(f32)).astype(bf16)
        xw[at, :, 0:128] = jnp.concatenate([hi, lo], axis=0)
        xw[at, :, 128:256] = jnp.concatenate([hi, jnp.zeros_like(lo)], axis=0)
        q = ref[i, 40:56, :]
        qr = pltpu.roll(q, 64, 1)
        low = lax.broadcasted_iota(jnp.int32, (16, P_SIZE), 1) < 64
        twice = jnp.concatenate([jnp.where(low, q, qr), jnp.where(low, qr, q)], axis=0)
        qhi = twice.astype(bf16)
        low2 = lax.broadcasted_iota(jnp.int32, (32, P_SIZE), 1) < 64
        qlo = jnp.where(low2, twice - qhi.astype(f32), 0.0).astype(bf16)
        qw[at] = jnp.concatenate([qhi, qlo], axis=0)
        if local is not None:
            tgt[i] = target_rows(t8).astype(bf16)
            kt8 = jnp.where(lane < 64, kt8, 0.0)
            if local == 1:
                kt8 = pltpu.roll(kt8, 64, 1)
            return target_rows(kt8).astype(bf16)
        return None

    def halo(g, c):
        for j in range(4):
            i = g * 4 + j
            prepare(left, i, i, None)
            prepare(right, i, i + HALO + leaves, None)
        return c

    lax.fori_loop(0, HALO // 4, halo, 0)

    def middle(g, c):
        for j in range(8):
            i = g * 8 + j
            half = j % 2
            tgt2[g * 4 + j // 2, half * 64 : half * 64 + 64, :] = prepare(
                own, i, i + HALO, half
            )
        return c

    lax.fori_loop(0, leaves // 8, middle, 0)
    src[total] = jnp.zeros(src.shape[1:], bf16)
    xw[total] = jnp.zeros(xw.shape[1:], bf16)
    src_lo[total] = jnp.zeros(src_lo.shape[1:], bf16)
    src_hi[total] = jnp.zeros(src_hi.shape[1:], bf16)
    qw[total] = jnp.zeros(qw.shape[1:], bf16)

    def near_leaf(l, c):
        target = tgt[l]

        def steps(count):
            def run():
                tiles, values = [], []
                for u in range(count):
                    m = near_ids[l * near_width + u]
                    k = profile(jnp.dot(src[m], target, preferred_element_type=f32))
                    hi = k.astype(bf16)
                    tiles += [hi, (k - hi.astype(f32)).astype(bf16)]
                    values.append(xw[m])
                return jnp.dot(
                    jnp.concatenate(values, axis=1),
                    jnp.concatenate(tiles, axis=0),
                    preferred_element_type=f32,
                )

            return run

        acc = lax.switch(
            jnp.maximum(near_trips[l], 1) - 1,
            [steps(n) for n in range(NEAR_STEP, near_width + 1, NEAR_STEP)],
        )
        near_out[l] = (acc[0:32] + acc[32:64]) * near_factor
        return c

    lax.fori_loop(0, leaves, near_leaf, 0)

    def far_pair(p, c):
        target = tgt2[p]

        def steps(count):
            def run():
                tiles, values = [], []
                for at in range(count):
                    a = far_ids[2 * p * far_width + at]
                    b = far_ids[(2 * p + 1) * far_width + at]
                    k = profile(
                        jnp.dot(src_lo[a] + src_hi[b], target, preferred_element_type=f32)
                    )
                    hi = k.astype(bf16)
                    tiles += [hi, (k - hi.astype(f32)).astype(bf16)]
                    values.append(jnp.concatenate([qw[a], qw[b]], axis=0))
                return jnp.dot(
                    jnp.concatenate(values, axis=1),
                    jnp.concatenate(tiles, axis=0),
                    preferred_element_type=f32,
                )

            return run

        acc = lax.switch(
            jnp.maximum(far_trips[p], 1) - 1,
            [steps(n) for n in range(FAR_STEP, far_width + 1, FAR_STEP)],
        )
        low = lax.broadcasted_iota(jnp.int32, (32, P_SIZE), 1) < 64
        far_out[p] = (
            jnp.where(low, acc[0:32] + acc[32:64], acc[64:96] + acc[96:128]) * far_factor
        )
        return c

    lax.fori_loop(0, leaves // 2, far_pair, 0)


def centred(block, centre):
    return augmented(coords(block, centre))


def finish_kernel(
    morton, box_far, sub_far, place,
    near, far, q1, gathered, box_skel, group_skel,
    basis, leaf_tr, box_tr, sub_tr,
    out, rows, pad, l1s,
    *, subs, groups, box_width, sub_width, f1, f2, f3,
):
    boxes = q1.shape[0]
    leaves = near.shape[0]
    device, group = place[0], place[1]

    def tile(source8, target8):
        return profile(
            jnp.dot(
                source_rows(source8).T.astype(bf16),
                target_rows(target8).astype(bf16),
                preferred_element_type=f32,
            )
        )

    own = gathered[device, 64:72, :]
    centre = own[:, 0:1]
    target = centred(own, centre)[1]

    def sub_term(j, acc):
        entry = sub_far[j]
        m = jnp.maximum(entry, 0)
        source = centred(gathered[m, 64:72, :], centre)[0]
        term = hdot(gathered[m, 0:32, :], tile(source, target))
        return acc + jnp.where(entry >= 0, term, 0.0)

    many = 4 if sub_width % 4 == 0 else 1

    def sub_terms(g, acc):
        for j in range(many):
            acc = sub_term(g * many + j, acc)
        return acc

    z2 = lax.fori_loop(0, sub_width // many, sub_terms, jnp.zeros(gathered[0, 0:32, :].shape, f32))
    g_own = group_skel[group]
    g_centre = g_own[:, 0:1]
    g_target = centred(g_own, g_centre)[1]

    def group_term(h, acc):
        q3 = lax.fori_loop(
            0, subs, lambda s, t: t + gathered[h * subs + s, 32:64, :], jnp.zeros(z2.shape, f32)
        )
        source = centred(group_skel[h], g_centre)[0]
        return acc + jnp.where(h != group, hdot(q3, tile(source, g_target)), 0.0)

    z3 = jnp.zeros(z2.shape, f32)
    for h in range(groups):
        z3 = group_term(h, z3)
    l2 = z2 * f2 + hdot_nt(z3 * f3, sub_tr[0])

    def box_level(b, c):
        mine = box_skel[b]
        b_centre = mine[:, 0:1]
        b_target = centred(mine, b_centre)[1]

        def box_term(j, acc):
            entry = box_far[b * box_width + j]
            m = jnp.maximum(entry - device * boxes, 0)
            source = centred(box_skel[m], b_centre)[0]
            return acc + jnp.where(entry >= 0, hdot(q1[m], tile(source, b_target)), 0.0)

        z1 = jnp.zeros((32, P_SIZE), f32)
        for j in range(box_width):
            z1 = box_term(j, z1)
        l1s[b] = z1 * f1 + hdot_nt(l2, box_tr[b])
        return c

    def box_pair(g, c):
        for j in range(2):
            box_level(2 * g + j, c)
        return c

    lax.fori_loop(0, boxes // 2, box_pair, 0)

    pad[...] = jnp.zeros_like(pad)

    def down(b, c):
        l1 = l1s[b]
        for j in range(CH):
            i = b * CH + j
            half = 64 * (j % 2)
            l0 = far[b * (CH // 2) + j // 2, :, half : half + 64] + hdot_nt(l1, leaf_tr[i])
            pad[j, 0:32, :] = near[i] + hdot(l0, basis[i])
        for j in range(CH):
            pad[CH + j] = pad[j].T
        for j in range(CH):
            base = (b * CH + j) * P_SIZE
            for k in range(P_SIZE):
                rows[pl.ds(morton[base + k], 1), :] = pad[CH + j, k : k + 1, :]
        return c

    lax.fori_loop(0, boxes, down, 0)

    def flip(g, c):
        for j in range(4):
            at = pl.ds(pl.multiple_of((4 * g + j) * P_SIZE, P_SIZE), P_SIZE)
            out[:, at] = rows[at, :].T[0:32]
        return c

    lax.fori_loop(0, leaves // 4, flip, 0)


VMEM = pl.BlockSpec(memory_space=pltpu.VMEM)
SMEM = pl.BlockSpec(memory_space=pltpu.SMEM)
params = pltpu.CompilerParams(vmem_limit_bytes=56 * 2**20)


def slots(ids, base, total, step):
    width = ids.shape[1]
    usable = ids >= 0
    local = jnp.where(usable, ids - base, total)
    more = -width % step
    local = jnp.pad(local, ((0, 0), (0, more)), constant_values=total)
    last = jnp.max(jnp.where(usable, jnp.arange(1, width + 1, dtype=jnp.int32)[None], 0), axis=1)
    return local.reshape(-1), (last + step - 1) // step, width + more


def body(
    points, probes, morton, near_list, leaf_far, box_far, subtree_far,
    leaf_skeleton, box_skeleton, subtree_skeleton, group_skeleton,
    leaf_basis, leaf_transfer, box_transfer, subtree_transfer,
):
    leaves = near_list.shape[0]
    count = points.shape[1]
    nv = probes.shape[0]
    boxes = box_far.shape[0]
    r0, r1 = leaf_basis.shape[1], box_transfer.shape[1]
    r2, r3 = subtree_transfer.shape[1:]
    device = lax.axis_index(("group", "sub"))
    group = lax.axis_index("group")
    subs, groups = lax.axis_size("sub"), lax.axis_size("group")
    total = leaves + 2 * HALO

    geo, q1, q2, q3 = pl.pallas_call(
        arrange_kernel,
        out_shape=(
            jax.ShapeDtypeStruct((leaves, 56, P_SIZE), f32),
            jax.ShapeDtypeStruct((boxes, nv, r1), f32),
            jax.ShapeDtypeStruct((nv, r2), f32),
            jax.ShapeDtypeStruct((nv, r3), f32),
        ),
        in_specs=[SMEM] + [VMEM] * 7,
        out_specs=(VMEM,) * 4,
        scratch_shapes=[
            pltpu.VMEM((count, P_SIZE), f32),
            pltpu.VMEM((4, P_SIZE, P_SIZE), f32),
            pltpu.VMEM((CH, P_SIZE, P_SIZE), f32),
        ],
        compiler_params=params,
        name="arrange",
    )(morton, points, probes, leaf_skeleton, leaf_basis, leaf_transfer, box_transfer, subtree_transfer)

    both = ("group", "sub")
    ends = subs * groups - 1
    left = lax.ppermute(geo[leaves - HALO :], both, [(i, i + 1) for i in range(ends)])
    right = lax.ppermute(geo[:HALO], both, [(i + 1, i) for i in range(ends)])
    packed = jnp.concatenate(
        [q2, q3, subtree_skeleton[0], jnp.zeros((5, r2), f32)], axis=0
    )
    gathered = lax.all_gather(packed, both, axis=0)

    base = device * leaves - HALO
    near_ids, near_trips, near_width = slots(near_list, base, total, NEAR_STEP)
    far_ids, far_trips, far_width = slots(leaf_far, base, total, FAR_STEP)
    far_trips = jnp.max(far_trips.reshape(-1, 2), axis=1)
    near, far = pl.pallas_call(
        functools.partial(
            couple_kernel,
            near_width=near_width,
            far_width=far_width,
            near_factor=(P_SIZE * near_list.shape[1]) ** -0.5,
            far_factor=(r0 * leaf_far.shape[1]) ** -0.5,
        ),
        out_shape=(
            jax.ShapeDtypeStruct((leaves, nv, P_SIZE), f32),
            jax.ShapeDtypeStruct((leaves // 2, nv, P_SIZE), f32),
        ),
        in_specs=[SMEM] * 4 + [VMEM] * 3,
        out_specs=(VMEM,) * 2,
        scratch_shapes=[
            pltpu.VMEM((total + 1, P_SIZE, 64), bf16),
            pltpu.VMEM((leaves, 64, P_SIZE), bf16),
            pltpu.VMEM((total + 1, 64, 256), bf16),
            pltpu.VMEM((total + 1, 64, P_SIZE), bf16),
            pltpu.VMEM((total + 1, 64, P_SIZE), bf16),
            pltpu.VMEM((leaves // 2, P_SIZE, P_SIZE), bf16),
            pltpu.VMEM((total + 1, 64, P_SIZE), bf16),
        ],
        compiler_params=params,
        cost_estimate=pl.CostEstimate(flops=2 * 10**10, bytes_accessed=10**7, transcendentals=5 * 10**7),
        name="couple",
    )(near_ids, near_trips, far_ids, far_trips, left, geo, right)

    pad8 = lambda a: jnp.pad(a, ((0, 0), (0, 5), (0, 0)))
    return pl.pallas_call(
        functools.partial(
            finish_kernel,
            subs=subs,
            groups=groups,
            box_width=box_far.shape[1],
            sub_width=subtree_far.shape[1],
            f1=(r1 * box_far.shape[1]) ** -0.5,
            f2=(r2 * subtree_far.shape[1]) ** -0.5,
            f3=r3**-0.5,
        ),
        out_shape=jax.ShapeDtypeStruct((nv, count), f32),
        in_specs=[SMEM] * 4 + [VMEM] * 10,
        out_specs=VMEM,
        scratch_shapes=[
            pltpu.VMEM((count, P_SIZE), f32),
            pltpu.VMEM((2 * CH, P_SIZE, P_SIZE), f32),
            pltpu.VMEM((boxes, nv, P_SIZE), f32),
        ],
        compiler_params=params,
        name="finish",
    )(
        morton, box_far.reshape(-1), subtree_far.reshape(-1),
        jnp.stack([device, group]).astype(jnp.int32),
        near, far, q1, gathered, pad8(box_skeleton), pad8(group_skeleton),
        leaf_basis, leaf_transfer, box_transfer, subtree_transfer,
    )


def solution(mesh):
    two = ("group", "sub")
    placed = (
        (P(None, two),) * 2
        + (P(two),)
        + (P(two, None),) * 4
        + (P(two, None, None),) * 3
        + (P(),)
        + (P(two, None, None),) * 4
    )
    return jax.shard_map(
        body, mesh=mesh, in_specs=placed, out_specs=P(None, two), check_vma=False
    )
```

profile of v0, /device:TPU:1, one launch (start us, length us, event | category | flops | bytes accessed | tf_op | source)
XLA Modules:
  0.0 209.1 jit_solution(16680867319419483251)
XLA Ops:
  6.5 0.0 all-gather.3.cloned.1.call-start
  6.5 1.6 copy.23.skel
  8.2 0.7 copy.28
  8.8 0.1 pad.13.clone
  8.9 20.7 %arrange.1 = (f32[64,56,128]{2,1,0:T(8,128)}, f32[8,32,128]{2,1,0:T(8,128)}, f32[32,256]{1,0:T(8,128)}, f32[32,256]{1,0:T(8,128)}) custom-call(s32[8192]{0:T(1024)} %morton.3, f32[3,8192]{1,0:T(4,128)} %points.1, f32[32,8192]{1,0:T(8,128)} %probes.1, f32[64,3,64]{2,1,0:T(4,128)} %copy.23.skel, f32[64,64,128]{2,1,0:T(8,128)} %basis.3, ...), custom_call_target="tpu_custom_call" | custom-call | tf_op jit(solution)/shard_map/arrange/pallas_call | solution.py:392
  29.6 0.0 copy-start
  29.6 0.0 copy-start.3
  29.6 0.0 copy-start.1
  29.6 0.0 copy-start.2
  29.6 1.5 maximum_maximum_fusion
  31.1 0.0 copy-start.4
  31.1 0.0 all-gather.3.cloned.1.call-update
  31.2 1.6 fusion.3
  32.7 4.6 %collective-permute-start = (f32[32,56,128]{2,1,0:T(8,128)S(1)}, f32[32,56,128]{2,1,0:T(8,128)S(1)}, u32[]{:S(2)}, u32[]{:S(2)}) collective-permute-start(f32[32,56,128]{2,1,0:T(8,128)S(1)} %get-tuple-element.18), channel_id=1, source_target_pairs={{0,1},{1,2},{2,3},{3,4},{4,5},{5,6},{6,7},{7,8},{8,9},{9,10},{10,1... | collective-permute-start | bytes 2752520 | tf_op jit(solution)/shard_map/ppermute | solution.py:413
  37.3 2.1 %collective-permute-start.1 = (f32[32,56,128]{2,1,0:T(8,128)S(1)}, f32[32,56,128]{2,1,0:T(8,128)}, u32[]{:S(2)}, u32[]{:S(2)}) collective-permute-start(f32[32,56,128]{2,1,0:T(8,128)S(1)} %get-tuple-element.17), channel_id=1, source_target_pairs={{1,0},{2,1},{3,2},{4,3},{5,4},{6,5},{7,6},{8,7},{9,8},{10,9},{11,1... | collective-permute-start | bytes 2752520 | tf_op jit(solution)/shard_map/ppermute | solution.py:414
  39.5 0.0 copy-done
  39.5 0.1 select_reduce_fusion
  39.6 0.1 copy.21
  39.7 0.7 reshape.26.near_ids
  40.4 0.0 copy-done.3
  40.4 0.1 select_reduce_fusion.1
  40.5 0.1 copy.22
  40.6 0.7 reshape.27.far_ids
  41.3 0.1 sub.46
  41.4 0.0 copy-done.1
  41.4 0.6 pad.8.box_skel
  42.0 0.0 copy-done.2
  42.0 0.6 pad.9.group_skel
  42.6 0.0 copy-done.4
  42.6 0.1 copy.20
  42.7 0.7 reshape.24.box_far
  43.4 0.7 pad_add_fusion.place
  44.1 0.7 fusion.1.far_trips
  44.7 0.6 and_select_fusion.near_trips
  45.3 3.3 %collective-permute-done.left = f32[32,56,128]{2,1,0:T(8,128)S(1)} collective-permute-done((f32[32,56,128]{2,1,0:T(8,128)S(1)}, f32[32,56,128]{2,1,0:T(8,128)S(1)}, u32[]{:S(2)}, u32[]{:S(2)}) %collective-permute-start) | collective-permute-done | bytes 917536 | tf_op jit(solution)/shard_map/ppermute | solution.py:413
  48.6 0.0 copy-start.5
  48.6 15.1 %collective-permute-done.1.right = f32[32,56,128]{2,1,0:T(8,128)} collective-permute-done((f32[32,56,128]{2,1,0:T(8,128)S(1)}, f32[32,56,128]{2,1,0:T(8,128)}, u32[]{:S(2)}, u32[]{:S(2)}) %collective-permute-start.1) | collective-permute-done | bytes 917536 | tf_op jit(solution)/shard_map/ppermute | solution.py:414
  63.7 0.0 copy-done.5
  63.7 94.9 %couple.1 = (f32[64,32,128]{2,1,0:T(8,128)}, f32[32,32,128]{2,1,0:T(8,128)}) custom-call(s32[1728]{0:T(1024)} %reshape.26.near_ids, s32[64]{0:T(128)} %and_select_fusion.near_trips, s32[1536]{0:T(1024)} %reshape.27.far_ids, s32[32]{0:T(128)} %fusion.1.far_trips, f32[32,56,128]{2,1,0:T(8,128)} %copy-done.5, f32[64,56,128]{2,1,0:T(8,128)} %get-tuple-element.11.own, ...), custom_call_target="tpu_custom_call" | custom-call | flops 20000000000 | bytes 10000000 | tf_op jit(solution)/shard_map/couple/pallas_call | solution.py:424
  158.6 0.0 all-gather.3.cloned.1.call-done
  158.6 43.6 %finish.1 = f32[32,8192]{1,0:T(8,128)} custom-call(s32[8192]{0:T(1024)} %morton.3, s32[32]{0:T(128)} %reshape.24.box_far, s32[4]{0:T(128)} %bitcast.9, s32[2]{0:T(128)} %pad_add_fusion.place, f32[64,32,128]{2,1,0:T(8,128)} %get-tuple-element.12.near, f32[32,32,128]{2,1,0:T(8,128)} %get-tuple-element.13.far, f32[8,32,128]{2,1,0:T(8,128)} %get-tuple-element.14.q1, ...), custom_call_target="tpu_custom_call" | custom-call | tf_op jit(solution)/shard_map/finish/pallas_call | solution.py:453
  (6 shorter events, 0.0 us)
Async XLA Ops:
  6.5 152.1 %all-gather.3.cloned.1.call-start = ((), (), s32[]{:S(2)}) async-start(), calls=%async_computation | async-start | bytes 2433024 | tf_op jit(solution)/shard_map/all_gather | solution.py:418
  29.6 9.9 %copy-start = (s32[64,27]{0,1:T(8,128)S(1)}, s32[64,27]{0,1:T(8,128)}, u32[]{:S(2)}) copy-start(s32[64,27]{0,1:T(8,128)} %param.18) | copy-start | bytes 20740
  29.6 10.8 %copy-start.3 = (s32[64,24]{0,1:T(8,128)S(1)}, s32[64,24]{0,1:T(8,128)}, u32[]{:S(2)}) copy-start(s32[64,24]{0,1:T(8,128)} %param.19) | copy-start | bytes 18436
  29.6 11.8 %copy-start.1 = (f32[8,3,128]{2,0,1:T(8,128)S(1)}, f32[8,3,128]{2,0,1:T(8,128)}, u32[]{:S(2)}) copy-start(f32[8,3,128]{2,0,1:T(8,128)} %param.23) | copy-start | bytes 36868
  29.6 12.4 %copy-start.2 = (f32[4,3,256]{2,0,1:T(4,128)S(1)}, f32[4,3,256]{2,0,1:T(4,128)}, u32[]{:S(2)}) copy-start(f32[4,3,256]{2,0,1:T(4,128)} %param.25) | copy-start | bytes 36868
  31.1 11.5 %copy-start.4 = (s32[8,4]{0,1:T(4,128)S(1)}, s32[8,4]{0,1:T(4,128)}, u32[]{:S(2)}) copy-start(s32[8,4]{0,1:T(4,128)} %param.20) | copy-start | bytes 388
  32.7 15.9 %collective-permute-start = (f32[32,56,128]{2,1,0:T(8,128)S(1)}, f32[32,56,128]{2,1,0:T(8,128)S(1)}, u32[]{:S(2)}, u32[]{:S(2)}) collective-permute-start(f32[32,56,128]{2,1,0:T(8,128)S(1)} %get-tuple-element.18), channel_id=1, source_target_pairs={{0,1},{1,2},{2,3},{3,4},{4,5},{5,6},{6,7},{7,8},{8,9},{9,10},{10,1... | collective-permute-start | bytes 2752520 | tf_op jit(solution)/shard_map/ppermute | solution.py:413
  37.3 26.4 %collective-permute-start.1 = (f32[32,56,128]{2,1,0:T(8,128)S(1)}, f32[32,56,128]{2,1,0:T(8,128)}, u32[]{:S(2)}, u32[]{:S(2)}) collective-permute-start(f32[32,56,128]{2,1,0:T(8,128)S(1)} %get-tuple-element.17), channel_id=1, source_target_pairs={{1,0},{2,1},{3,2},{4,3},{5,4},{6,5},{7,6},{8,7},{9,8},{10,9},{11,1... | collective-permute-start | bytes 2752520 | tf_op jit(solution)/shard_map/ppermute | solution.py:414
  48.6 15.1 %copy-start.5 = (f32[32,56,128]{2,1,0:T(8,128)}, f32[32,56,128]{2,1,0:T(8,128)S(1)}, u32[]{:S(2)}) copy-start(f32[32,56,128]{2,1,0:T(8,128)S(1)} %collective-permute-done.left) | copy-start | bytes 2752516
Sparse Core Ops, SparseCore 0:
  31.3 60.5 all-gather.2
where the time goes:
time: 209 us
  Pallas kernels  159 us (76%)
  waiting for transfers between devices  18.4 us (9%)
  between operations  13.5 us (6%)
  local copies, waits for them, and re-layouts  7.67 us (4%)
  starting transfers between devices  6.7 us (3%)
  other arithmetic  3.64 us (2%)
    pallas_call x1, Pallas kernels, body(): pl.pallas_call(functools.partial(couple_kernel, near_width=near_width, fa...  94.9 us
    pallas_call x1, Pallas kernels, body(): pl.pallas_call(functools.partial(finish_kernel, subs=subs, groups=groups,...  43.6 us
    pallas_call x1, Pallas kernels, body(): pl.pallas_call(arrange_kernel, out_shape=(jax.ShapeDtypeStruct((leaves, 5...  20.7 us
    ppermute x1, waiting for transfers between devices, body(): right = lax.ppermute(geo[:HALO], both, [(i + 1, i) for i in range(ends)])  15.1 us
    ppermute x1, starting transfers between devices, body(): lax.ppermute(geo[leaves - HALO:], both, [(i, i + 1) for i in range(ends)])  4.6 us
  transfers between devices with their start and end apart: 3, of which 2 were waited for; matrix products, arithmetic and copies ran while one was open for 4% of the time, Pallas kernels for 45%

commit v1 on v0

v1 whole, which is shorter than its diff:
```python
import functools
import math

import jax
import jax.numpy as jnp
from jax import lax
from jax.experimental import pallas as pl
from jax.experimental.pallas import tpu as pltpu
from jax.sharding import PartitionSpec as P

P_SIZE = 128
CH = 8
HALO = 32
SPLIT = 64
COUNT = 63
GROUPS = 62
NEAR_GROUP = 2
NEAR_BATCH = 8
FAR_GROUP = 2
FAR_BATCH = 12

highest = lax.Precision.HIGHEST
scale = math.sqrt(3.0) / 12.0
soft = 0.0001 * scale * scale
log2e = math.log2(math.e)
f32 = jnp.float32
bf16 = jnp.bfloat16
NT = (((1,), (1,)), ((), ()))


def hdot(a, b):
    return jnp.dot(a, b, precision=highest, preferred_element_type=f32)


def hdot_nt(a, b):
    return lax.dot_general(a, b, NT, precision=highest, preferred_element_type=f32)


def profile(squared):
    squared = jnp.maximum(squared, soft)
    u = squared * lax.rsqrt(squared)
    return (1.0 + u) * jnp.exp2(u * -log2e)


def split3(v):
    high = v.astype(bf16).astype(f32)
    rest = v - high
    mid = rest.astype(bf16).astype(f32)
    return high, mid, rest - mid


def augmented(x):
    row = lax.broadcasted_iota(jnp.int32, x.shape, 0)
    norm = jnp.sum(x * x, axis=0, keepdims=True)
    source = jnp.where(row < 3, -2.0 * x, jnp.where(row == 3, 1.0, jnp.where(row == 4, norm + soft, 0.0)))
    target = jnp.where(row < 3, x, jnp.where(row == 3, norm, jnp.where(row == 4, 1.0, 0.0)))
    return source, target


def source_rows(v):
    h, m, lo = split3(v)
    return jnp.concatenate([h, m, h, m, lo, h, lo, m], axis=0)


def target_rows(v):
    h, m, lo = split3(v)
    return jnp.concatenate([h, h, m, m, h, lo, m, lo], axis=0)


def coords(block, centre):
    row = lax.broadcasted_iota(jnp.int32, block.shape, 0)
    return jnp.where(row < 3, (block - centre) * scale, 0.0)


def sort_list(ids_ref, out, base, group):
    leaves, width = ids_ref.shape
    ids = ids_ref[...]
    place = ids - base
    valid = ids >= 0
    own = valid & (place >= 0) & (place < leaves)
    other = valid & jnp.logical_not(own)
    slot = jnp.where(own, place, jnp.where(place < 0, place + HALO, place - leaves + HALO))
    ones = jnp.concatenate([own.astype(f32), other.astype(f32)], axis=0)
    before = lax.broadcasted_iota(jnp.int32, (width, width), 0) < lax.broadcasted_iota(
        jnp.int32, (width, width), 1
    )
    rank = jnp.dot(ones.astype(bf16), before.astype(bf16), preferred_element_type=f32)
    rank = rank.astype(jnp.int32)
    key = jnp.where(own, rank[0:leaves], jnp.where(other, SPLIT + rank[leaves:], -1))
    lane = lax.broadcasted_iota(jnp.int32, (leaves, P_SIZE), 1)
    table = jnp.full((leaves, P_SIZE), 2 * HALO, jnp.int32)
    for j in range(width):
        table = jnp.where(lane == key[:, j : j + 1], slot[:, j : j + 1], table)
    row = lax.broadcasted_iota(jnp.int32, (8, P_SIZE), 1)
    last = jnp.full((8, P_SIZE), 2 * HALO, jnp.int32)
    for part, lane0 in ((ones[0:leaves], 0), (ones[leaves:], SPLIT)):
        many = jnp.sum(part, axis=1, keepdims=True).astype(jnp.int32)
        table = jnp.where(lane == lane0 + COUNT, many, table)
        groups = jnp.maximum((many + group - 1) // group, 1)
        groups = jnp.sum(groups.astype(f32), axis=0, keepdims=True).astype(jnp.int32)
        last = jnp.where(row == lane0 + GROUPS, groups, jnp.where(row == lane0 + COUNT, 0, last))
    out[0:leaves, :] = table
    out[leaves : leaves + 8, :] = last


def arrange_kernel(
    morton, near_list, leaf_far, points, probes, skel, basis, leaf_tr, box_tr, sub_tr,
    geo, near_ids, far_ids, q1_out, q2_out, q3_out, rows, pad, got,
):
    leaves = geo.shape[0]
    boxes = q1_out.shape[0]
    device = lax.axis_index("group") * lax.axis_size("sub") + lax.axis_index("sub")
    sort_list(near_list, near_ids, device * leaves, NEAR_GROUP)
    sort_list(leaf_far, far_ids, device * leaves, FAR_GROUP)
    pad[...] = jnp.zeros_like(pad)

    def flip(g, c):
        for j in range(4):
            at = pl.ds(pl.multiple_of((4 * g + j) * P_SIZE, P_SIZE), P_SIZE)
            pad[j, 0:32, :] = probes[:, at]
            pad[j, 32:35, :] = points[:, at]
        for j in range(4):
            at = pl.ds(pl.multiple_of((4 * g + j) * P_SIZE, P_SIZE), P_SIZE)
            rows[at, :] = pad[j].T
        return c

    lax.fori_loop(0, leaves // 4, flip, 0)

    def one_box(b, q2):
        for j in range(CH):
            base = (b * CH + j) * P_SIZE
            for k in range(P_SIZE):
                got[j, k : k + 1, :] = rows[pl.ds(morton[base + k], 1), :]
        turned = [got[j].T for j in range(CH)]
        parts = []
        for j in range(CH):
            i = b * CH + j
            geo[i, 0:40, :] = turned[j][0:40]
            geo[i, 35:38, 0:64] = skel[i]
            q0 = hdot_nt(turned[j][0:32], basis[i])
            geo[i, 40:56, 0:64] = q0[0:16]
            geo[i, 40:56, 64:128] = q0[16:32]
            parts.append(q0)
        q1 = jnp.zeros(q1_out.shape[1:], f32)
        for j in range(0, CH, 2):
            two = jnp.concatenate([leaf_tr[b * CH + j], leaf_tr[b * CH + j + 1]], axis=0)
            q1 = q1 + hdot(jnp.concatenate(parts[j : j + 2], axis=1), two)
        q1_out[b] = q1
        return q2 + hdot(q1, box_tr[b])

    q2 = lax.fori_loop(0, boxes, one_box, jnp.zeros(q2_out.shape, f32))
    q2_out[...] = q2
    q3_out[...] = hdot(q2, sub_tr[0])


def prepare_source(block, at, centre_pt, centre_sk, src, xw, src_lo, src_hi, qw):
    geo8 = block[32:40]
    s8, t8 = augmented(coords(geo8, centre_pt))
    src[at] = source_rows(s8).T.astype(bf16)
    turned = jnp.concatenate([geo8[3:8], geo8[0:3]], axis=0)
    ks8, kt8 = augmented(coords(turned, centre_sk))
    low = lax.broadcasted_iota(jnp.int32, (8, P_SIZE), 1) < 64
    ks8 = jnp.where(low, ks8, 0.0)
    src_lo[at] = source_rows(ks8).astype(bf16)
    src_hi[at] = source_rows(pltpu.roll(ks8, 64, 1)).astype(bf16)
    x = block[0:32]
    hi = x.astype(bf16)
    lo = (x - hi.astype(f32)).astype(bf16)
    xw[at] = jnp.concatenate([hi, lo], axis=0)
    q = block[40:56]
    q = jnp.concatenate([q, pltpu.roll(q, 64, 1)], axis=0)
    qhi = q.astype(bf16).astype(f32)
    four = jnp.concatenate([qhi, q - qhi, jnp.zeros((64, P_SIZE), f32)], axis=0)
    qw[at] = four.T[0:64].astype(bf16)
    return t8, kt8


def prepare_target(t8, kt8, at, tgt, tgt_far):
    tgt[at] = target_rows(t8).astype(bf16)
    far = target_rows(kt8)
    tgt_far[at] = jnp.concatenate([far, far], axis=0).T[0:64].astype(bf16)


def clear(refs, at):
    for ref in refs:
        ref[at] = jnp.zeros(ref.shape[1:], ref.dtype)


def batches(ids, lane0, leaves, group, batch, first, step):
    def follow(at):
        leaf, off = at
        more = off + group < ids[leaf, lane0 + COUNT]
        return (
            jnp.where(more, leaf, jnp.minimum(leaf + 1, leaves)),
            jnp.where(more, off + group, 0),
        )

    def take(at):
        got = []
        for _ in range(batch):
            got.append(at)
            at = follow(at)
        return got, at

    now, at = take((jnp.int32(0), jnp.int32(0)))
    first(now)
    later, at = take(at)

    def one(i, c):
        now, later, at = c
        step(now, later)
        after, at = take(at)
        return later, after, at

    total = ids[leaves, lane0 + GROUPS]
    lax.fori_loop(0, (total + batch - 1) // batch, one, (now, later, at))


def halves(k):
    hi = k.astype(bf16)
    return hi, (k - hi.astype(f32)).astype(bf16)


def near_pass(ids, lane0, src, tgt, xw, out, dist):
    leaves = tgt.shape[0] - 1

    def squared(at, u):
        leaf, off = at
        return jnp.dot(
            src[ids[leaf, lane0 + off + u]], tgt[leaf], preferred_element_type=f32
        )

    def first(now):
        for j in range(NEAR_BATCH):
            for u in range(NEAR_GROUP):
                dist[j * NEAR_GROUP + u] = squared(now[j], u)

    def step(now, later):
        for j in range(NEAR_BATCH):
            leaf, off = now[j]
            tiles, values = [], []
            for u in range(NEAR_GROUP):
                n = j * NEAR_GROUP + u
                tiles.append(jnp.concatenate(halves(profile(dist[n])), axis=1))
                values.append(xw[ids[leaf, lane0 + off + u]])
                dist[n] = squared(later[j], u)
            acc = jnp.dot(
                jnp.concatenate(values, axis=1),
                jnp.concatenate(tiles, axis=0),
                preferred_element_type=f32,
            )
            out[leaf] = out[leaf] + (acc[0:32, 0:128] + acc[0:32, 128:256] + acc[32:64, 0:128])

    batches(ids, lane0, leaves, NEAR_GROUP, NEAR_BATCH, first, step)


def far_pass(ids, lane0, src_lo, src_hi, tgt, qw, out, dist):
    leaves = tgt.shape[0] - 1

    def squared(at):
        leaf, off = at
        source = jnp.concatenate(
            [src_lo[ids[leaf, lane0 + off]], src_hi[ids[leaf, lane0 + off + 1]]], axis=0
        )
        return jnp.dot(tgt[leaf], source, preferred_element_type=f32)

    def first(now):
        for j in range(FAR_BATCH):
            dist[j] = squared(now[j])

    def step(now, later):
        for j in range(FAR_BATCH):
            leaf, off = now[j]
            tile = jnp.concatenate(halves(profile(dist[j])), axis=1)
            a, b = qw[ids[leaf, lane0 + off]], qw[ids[leaf, lane0 + off + 1]]
            dist[j] = squared(later[j])
            acc = jnp.dot(
                tile, jnp.concatenate([a, b, a, b], axis=0), preferred_element_type=f32
            )
            out[leaf] = out[leaf] + acc

    batches(ids, lane0, leaves, FAR_GROUP, FAR_BATCH, first, step)


def inner_kernel(
    near_ids, far_ids, geo,
    near_out, far_out, tgt, tgt_far,
    src, xw, src_lo, src_hi, qw, near_dist, far_dist,
):
    leaves = geo.shape[0]
    first = geo[0, 32:40, 0:1]
    centre_sk = jnp.concatenate([first[3:8], first[0:3]], axis=0)
    sources = (src, xw, src_lo, src_hi, qw)

    def load(g, c):
        for j in range(8):
            i = g * 8 + j
            t8, kt8 = prepare_source(geo[i], i, first, centre_sk, *sources)
            prepare_target(t8, kt8, i, tgt, tgt_far)
        for j in range(8):
            clear((near_out, far_out), g * 8 + j)
        return c

    lax.fori_loop(0, leaves // 8, load, 0)
    clear(sources, 2 * HALO)
    clear((near_out, far_out, tgt, tgt_far), leaves)
    near_pass(near_ids, 0, src, tgt, xw, near_out, near_dist)
    far_pass(far_ids, 0, src_lo, src_hi, tgt_far, qw, far_out, far_dist)


def outer_kernel(
    near_ids, far_ids, origin, left, right, tgt, tgt_far, near_in, far_in,
    near_out, far_out,
    src, xw, src_lo, src_hi, qw, near_dist, far_dist,
):
    leaves = near_in.shape[0] - 1
    first = origin[0, 32:40, 0:1]
    centre_sk = jnp.concatenate([first[3:8], first[0:3]], axis=0)
    sources = (src, xw, src_lo, src_hi, qw)

    def load(g, c):
        for j in range(4):
            i = g * 4 + j
            prepare_source(left[i], i, first, centre_sk, *sources)
            prepare_source(right[i], i + HALO, first, centre_sk, *sources)
            for k in (i, i + HALO):
                near_out[k] = near_in[k]
                far_out[k] = far_in[k]
        return c

    lax.fori_loop(0, HALO // 4, load, 0)
    clear(sources, 2 * HALO)
    clear((near_out, far_out), leaves)
    near_pass(near_ids, SPLIT, src, tgt, xw, near_out, near_dist)
    far_pass(far_ids, SPLIT, src_lo, src_hi, tgt_far, qw, far_out, far_dist)


def centred(block, centre):
    return augmented(coords(block, centre))


def finish_kernel(
    morton, box_far, sub_far, place,
    near, far, q1, gathered, box_skel, group_skel,
    basis, leaf_tr, box_tr, sub_tr,
    out, rows, pad, l1s,
    *, subs, groups, box_width, sub_width, near_factor, f0, f1, f2, f3,
):
    boxes = q1.shape[0]
    leaves = near.shape[0] - 1
    device, group = place[0], place[1]

    def tile(source8, target8):
        return profile(
            jnp.dot(
                source_rows(source8).T.astype(bf16),
                target_rows(target8).astype(bf16),
                preferred_element_type=f32,
            )
        )

    own = gathered[device, 64:72, :]
    centre = own[:, 0:1]
    target = centred(own, centre)[1]

    def sub_term(j, acc):
        entry = sub_far[j]
        m = jnp.maximum(entry, 0)
        source = centred(gathered[m, 64:72, :], centre)[0]
        term = hdot(gathered[m, 0:32, :], tile(source, target))
        return acc + jnp.where(entry >= 0, term, 0.0)

    many = 4 if sub_width % 4 == 0 else 1

    def sub_terms(g, acc):
        for j in range(many):
            acc = sub_term(g * many + j, acc)
        return acc

    z2 = lax.fori_loop(0, sub_width // many, sub_terms, jnp.zeros(gathered[0, 0:32, :].shape, f32))
    g_own = group_skel[group]
    g_centre = g_own[:, 0:1]
    g_target = centred(g_own, g_centre)[1]

    def group_term(h, acc):
        q3 = lax.fori_loop(
            0, subs, lambda s, t: t + gathered[h * subs + s, 32:64, :], jnp.zeros(z2.shape, f32)
        )
        source = centred(group_skel[h], g_centre)[0]
        return acc + jnp.where(h != group, hdot(q3, tile(source, g_target)), 0.0)

    z3 = jnp.zeros(z2.shape, f32)
    for h in range(groups):
        z3 = group_term(h, z3)
    l2 = z2 * f2 + hdot_nt(z3 * f3, sub_tr[0])

    def box_level(b, c):
        mine = box_skel[b]
        b_centre = mine[:, 0:1]
        b_target = centred(mine, b_centre)[1]

        def box_term(j, acc):
            entry = box_far[b * box_width + j]
            m = jnp.maximum(entry - device * boxes, 0)
            source = centred(box_skel[m], b_centre)[0]
            return acc + jnp.where(entry >= 0, hdot(q1[m], tile(source, b_target)), 0.0)

        z1 = jnp.zeros((32, P_SIZE), f32)
        for j in range(box_width):
            z1 = box_term(j, z1)
        l1s[b] = z1 * f1 + hdot_nt(l2, box_tr[b])
        return c

    def box_pair(g, c):
        for j in range(2):
            box_level(2 * g + j, c)
        return c

    lax.fori_loop(0, boxes // 2, box_pair, 0)

    pad[...] = jnp.zeros_like(pad)

    def down(b, c):
        l1 = l1s[b]
        for j in range(CH):
            i = b * CH + j
            turned = far[i].T
            l0 = (turned[0:32] + turned[32:64]) * f0 + hdot_nt(l1, leaf_tr[i])
            pad[j, 0:32, :] = near[i] * near_factor + hdot(l0, basis[i])
        for j in range(CH):
            pad[CH + j] = pad[j].T
        for j in range(CH):
            base = (b * CH + j) * P_SIZE
            for k in range(P_SIZE):
                rows[pl.ds(morton[base + k], 1), :] = pad[CH + j, k : k + 1, :]
        return c

    lax.fori_loop(0, boxes, down, 0)

    def flip(g, c):
        for j in range(4):
            at = pl.ds(pl.multiple_of((4 * g + j) * P_SIZE, P_SIZE), P_SIZE)
            out[:, at] = rows[at, :].T[0:32]
        return c

    lax.fori_loop(0, leaves // 4, flip, 0)


VMEM = pl.BlockSpec(memory_space=pltpu.VMEM)
SMEM = pl.BlockSpec(memory_space=pltpu.SMEM)
params = pltpu.CompilerParams(vmem_limit_bytes=56 * 2**20)


def body(
    points, probes, morton, near_list, leaf_far, box_far, subtree_far,
    leaf_skeleton, box_skeleton, subtree_skeleton, group_skeleton,
    leaf_basis, leaf_transfer, box_transfer, subtree_transfer,
):
    leaves = near_list.shape[0]
    count = points.shape[1]
    nv = probes.shape[0]
    boxes = box_far.shape[0]
    r0, r1 = leaf_basis.shape[1], box_transfer.shape[1]
    r2, r3 = subtree_transfer.shape[1:]
    device = lax.axis_index(("group", "sub"))
    group = lax.axis_index("group")
    subs, groups = lax.axis_size("sub"), lax.axis_size("group")

    i32 = jnp.int32
    geo, near_ids, far_ids, q1, q2, q3 = pl.pallas_call(
        arrange_kernel,
        out_shape=(
            jax.ShapeDtypeStruct((leaves, 56, P_SIZE), f32),
            jax.ShapeDtypeStruct((leaves + 8, P_SIZE), i32),
            jax.ShapeDtypeStruct((leaves + 8, P_SIZE), i32),
            jax.ShapeDtypeStruct((boxes, nv, r1), f32),
            jax.ShapeDtypeStruct((nv, r2), f32),
            jax.ShapeDtypeStruct((nv, r3), f32),
        ),
        in_specs=[SMEM] + [VMEM] * 9,
        out_specs=(VMEM,) * 6,
        scratch_shapes=[
            pltpu.VMEM((count, P_SIZE), f32),
            pltpu.VMEM((4, P_SIZE, P_SIZE), f32),
            pltpu.VMEM((CH, P_SIZE, P_SIZE), f32),
        ],
        compiler_params=params,
        name="arrange",
    )(morton, near_list, leaf_far, points, probes, leaf_skeleton, leaf_basis, leaf_transfer, box_transfer, subtree_transfer)

    both = ("group", "sub")
    ends = subs * groups - 1
    left = lax.ppermute(geo[leaves - HALO :], both, [(i, i + 1) for i in range(ends)])
    right = lax.ppermute(geo[:HALO], both, [(i + 1, i) for i in range(ends)])
    packed = jnp.concatenate(
        [q2, q3, subtree_skeleton[0], jnp.zeros((5, r2), f32)], axis=0
    )
    gathered = lax.all_gather(packed, both, axis=0)

    acc_shapes = (
        jax.ShapeDtypeStruct((leaves + 1, nv, P_SIZE), f32),
        jax.ShapeDtypeStruct((leaves + 1, r0, P_SIZE), f32),
    )
    tables = [
        pltpu.VMEM((2 * HALO + 1, P_SIZE, 64), bf16),
        pltpu.VMEM((2 * HALO + 1, 2 * nv, P_SIZE), bf16),
        pltpu.VMEM((2 * HALO + 1, 64, P_SIZE), bf16),
        pltpu.VMEM((2 * HALO + 1, 64, P_SIZE), bf16),
        pltpu.VMEM((2 * HALO + 1, 64, P_SIZE), bf16),
        pltpu.VMEM((NEAR_BATCH * NEAR_GROUP, P_SIZE, P_SIZE), f32),
        pltpu.VMEM((FAR_BATCH, 64, P_SIZE), f32),
    ]
    near, far, tgt, tgt_far = pl.pallas_call(
        inner_kernel,
        out_shape=acc_shapes
        + (
            jax.ShapeDtypeStruct((leaves + 1, 64, P_SIZE), bf16),
            jax.ShapeDtypeStruct((leaves + 1, 64, P_SIZE), bf16),
        ),
        in_specs=[SMEM] * 2 + [VMEM],
        out_specs=(VMEM,) * 4,
        scratch_shapes=tables,
        compiler_params=params,
        cost_estimate=pl.CostEstimate(flops=2 * 10**10, bytes_accessed=10**7, transcendentals=5 * 10**7),
        name="inner",
    )(near_ids, far_ids, geo)
    near, far = pl.pallas_call(
        outer_kernel,
        out_shape=acc_shapes,
        in_specs=[SMEM] * 2 + [VMEM] * 7,
        out_specs=(VMEM,) * 2,
        scratch_shapes=tables,
        compiler_params=params,
        name="outer",
    )(near_ids, far_ids, geo[:1], left, right, tgt, tgt_far, near, far)

    pad8 = lambda a: jnp.pad(a, ((0, 0), (0, 5), (0, 0)))
    return pl.pallas_call(
        functools.partial(
            finish_kernel,
            subs=subs,
            groups=groups,
            box_width=box_far.shape[1],
            sub_width=subtree_far.shape[1],
            near_factor=(P_SIZE * near_list.shape[1]) ** -0.5,
            f0=(r0 * leaf_far.shape[1]) ** -0.5,
            f1=(r1 * box_far.shape[1]) ** -0.5,
            f2=(r2 * subtree_far.shape[1]) ** -0.5,
            f3=r3**-0.5,
        ),
        out_shape=jax.ShapeDtypeStruct((nv, count), f32),
        in_specs=[SMEM] * 4 + [VMEM] * 10,
        out_specs=VMEM,
        scratch_shapes=[
            pltpu.VMEM((count, P_SIZE), f32),
            pltpu.VMEM((2 * CH, P_SIZE, P_SIZE), f32),
            pltpu.VMEM((boxes, nv, P_SIZE), f32),
        ],
        compiler_params=params,
        name="finish",
    )(
        morton, box_far.reshape(-1), subtree_far.reshape(-1),
        jnp.stack([device, group]).astype(jnp.int32),
        near, far, q1, gathered, pad8(box_skeleton), pad8(group_skeleton),
        leaf_basis, leaf_transfer, box_transfer, subtree_transfer,
    )


def solution(mesh):
    two = ("group", "sub")
    placed = (
        (P(None, two),) * 2
        + (P(two),)
        + (P(two, None),) * 4
        + (P(two, None, None),) * 3
        + (P(),)
        + (P(two, None, None),) * 4
    )
    return jax.shard_map(
        body, mesh=mesh, in_specs=placed, out_specs=P(None, two), check_vma=False
    )
```

time: 209 us -> 181 us (0.87)
  the two profiles are of different devices: /device:TPU:1 before, /device:TPU:4 now
where the time goes in v1:
time: 181 us; the launch traced here: 178 us
  Pallas kernels  141 us (78%)
  between operations  13.5 us (7%)
  local copies, waits for them, and re-layouts  12.1 us (7%)
  starting transfers between devices  9.15 us (5%)
  other arithmetic  2.07 us (1%)
    pallas_call x1, Pallas kernels, body(): pl.pallas_call(inner_kernel, out_shape=acc_shapes + (jax.ShapeDtypeStruct...  53.5 us
    pallas_call x1, Pallas kernels, body(): pl.pallas_call(functools.partial(finish_kernel, subs=subs, groups=groups,...  40.2 us
    pallas_call x1, Pallas kernels, body(): pl.pallas_call(outer_kernel, out_shape=acc_shapes, in_specs=[SMEM] * 2 +...  25.1 us
    pallas_call x1, Pallas kernels, body(): pl.pallas_call(arrange_kernel, out_shape=(jax.ShapeDtypeStruct((leaves, 5...  22 us
    ppermute x1, starting transfers between devices, body(): right = lax.ppermute(geo[:HALO], both, [(i + 1, i) for i in range(ends)])  7.24 us
    unnamed x17, local copies, waits for them, and re-layouts  6.41 us
  transfers between devices with their start and end apart: 3, of which 0 were waited for; matrix products, arithmetic and copies ran while one was open for 4% of the time, Pallas kernels for 44%

profile of v1, /device:TPU:4, one launch (start us, length us, event | category | flops | bytes accessed | tf_op | source)
XLA Modules:
  0.0 177.7 jit_solution(8888547844385727899)
XLA Ops:
  6.5 0.0 all-gather.3.cloned.1.call-start
  6.5 1.6 copy.25.skel
  8.2 1.4 copy.23.near_list
  9.6 1.4 copy.24.leaf_far
  10.9 0.7 copy.30
  11.6 0.1 pad.13.clone
  11.7 22.0 %arrange.1 = (f32[64,56,128]{2,1,0:T(8,128)}, s32[72,128]{1,0:T(8,128)}, s32[72,128]{1,0:T(8,128)}, f32[8,32,128]{2,1,0:T(8,128)}, f32[32,256]{1,0:T(8,128)}, /*index=5*/f32[32,256]{1,0:T(8,128)}) custom-call(s32[8192]{0:T(1024)} %morton.3, s32[64,27]{1,0:T(8,128)} %copy.23.near_list, s32[64,24]{1,0:T(8,128)} %copy.24.leaf_far, f32[3,8192]{1,0:T(4,128)} %points.1, ...), custom_call_target="tpu_custom_call" | custom-call | tf_op jit(solution)/shard_map/arrange/pallas_call | solution.py:470
  33.7 1.5 maximum_maximum_fusion
  35.1 0.0 all-gather.3.cloned.1.call-update
  35.2 2.5 %fusion = (f32[32,56,128]{2,1,0:T(8,128)S(1)}, f32[32,56,128]{2,1,0:T(8,128)}) fusion(f32[64,56,128]{2,1,0:T(8,128)} %get-tuple-element.19.geo), kind=kLoop, calls=%fused_computation.3 | loop fusion | bytes 3670016 | tf_op jit(solution)/shard_map/slice | solution.py:494
  37.7 1.9 %collective-permute-start = (f32[32,56,128]{2,1,0:T(8,128)}, f32[32,56,128]{2,1,0:T(8,128)S(1)}, u32[]{:S(2)}, u32[]{:S(2)}) collective-permute-start(f32[32,56,128]{2,1,0:T(8,128)} %get-tuple-element.30), channel_id=1, source_target_pairs={{0,1},{1,2},{2,3},{3,4},{4,5},{5,6},{6,7},{7,8},{8,9},{9,10},{10,1... | collective-permute-start | bytes 2752520 | tf_op jit(solution)/shard_map/ppermute | solution.py:493
  39.6 7.2 %collective-permute-start.1 = (f32[32,56,128]{2,1,0:T(8,128)S(1)}, f32[32,56,128]{2,1,0:T(8,128)S(1)}, u32[]{:S(2)}, u32[]{:S(2)}) collective-permute-start(f32[32,56,128]{2,1,0:T(8,128)S(1)} %get-tuple-element.29), channel_id=1, source_target_pairs={{1,0},{2,1},{3,2},{4,3},{5,4},{6,5},{7,6},{8,7},{9,8},{10,9},{11,1... | collective-permute-start | bytes 2752520 | tf_op jit(solution)/shard_map/ppermute | solution.py:494
  46.8 0.0 copy-start.2
  46.8 0.0 copy-start.3
  46.9 0.0 copy-start.4
  46.9 53.5 %inner.1 = (f32[65,32,128]{2,1,0:T(8,128)}, f32[65,64,128]{2,1,0:T(8,128)}, bf16[65,64,128]{2,1,0:T(8,128)(2,1)}, bf16[65,64,128]{2,1,0:T(8,128)(2,1)}) custom-call(s32[72,128]{1,0:T(8,128)} %get-tuple-element.17.near_ids, s32[72,128]{1,0:T(8,128)} %get-tuple-element.18.far_ids, f32[64,56,128]{2,1,0:T(8,128)} %get-tuple-element.19.geo), custom_call_target="tpu_custom_call" | custom-call | flops 20000000000 | bytes 10000000 | tf_op jit(solution)/shard_map/inner/pallas_call | solution.py:513
  100.4 1.3 slice.9.origin
  101.8 0.0 copy-done.2
  101.8 0.6 pad.8.box_skel
  102.4 0.0 copy-done.3
  102.4 0.6 pad.9.group_skel
  103.0 0.0 copy-done.4
  103.0 0.1 copy.22
  103.1 0.6 reshape.6.box_far
  103.7 0.6 pad_add_fusion.place
  104.3 0.0 collective-permute-done.left
  104.3 0.0 copy-start
  104.3 0.0 collective-permute-done.1.right
  104.3 0.0 copy-start.1
  104.3 0.9 copy-done
  105.2 0.3 copy-done.1
  105.5 25.1 %outer.1 = (f32[65,32,128]{2,1,0:T(8,128)}, f32[65,64,128]{2,1,0:T(8,128)}) custom-call(s32[72,128]{1,0:T(8,128)} %get-tuple-element.17.near_ids, s32[72,128]{1,0:T(8,128)} %get-tuple-element.18.far_ids, f32[1,56,128]{2,1,0:T(8,128)} %slice.9.origin, f32[32,56,128]{2,1,0:T(8,128)} %copy-done, f32[32,56,128]{2,1,0:T(8,128)} %copy-done.1, ...), custom_call_target="tpu_custom_call" | custom-call | tf_op jit(solution)/shard_map/outer/pallas_call | solution.py:527
  130.6 0.0 all-gather.3.cloned.1.call-done
  130.6 40.2 %finish.1 = f32[32,8192]{1,0:T(8,128)} custom-call(s32[8192]{0:T(1024)} %morton.3, s32[32]{0:T(128)} %reshape.6.box_far, s32[4]{0:T(128)} %bitcast.9, s32[2]{0:T(128)} %pad_add_fusion.place, f32[65,32,128]{2,1,0:T(8,128)} %get-tuple-element.24.near, f32[65,64,128]{2,1,0:T(8,128)} %get-tuple-element.25.far, f32[8,32,128]{2,1,0:T(8,128)} %get-tuple-element.26.q1, ...), custom_call_target="tpu_custom_call" | custom-call | tf_op jit(solution)/shard_map/finish/pallas_call | solution.py:538
  (3 shorter events, 0.0 us)
Async XLA Ops:
  6.5 124.1 %all-gather.3.cloned.1.call-start = ((), (), s32[]{:S(2)}) async-start(), calls=%async_computation | async-start | bytes 2433024 | tf_op jit(solution)/shard_map/all_gather | solution.py:498
  37.7 66.6 %collective-permute-start = (f32[32,56,128]{2,1,0:T(8,128)}, f32[32,56,128]{2,1,0:T(8,128)S(1)}, u32[]{:S(2)}, u32[]{:S(2)}) collective-permute-start(f32[32,56,128]{2,1,0:T(8,128)} %get-tuple-element.30), channel_id=1, source_target_pairs={{0,1},{1,2},{2,3},{3,4},{4,5},{5,6},{6,7},{7,8},{8,9},{9,10},{10,1... | collective-permute-start | bytes 2752520 | tf_op jit(solution)/shard_map/ppermute | solution.py:493
  39.6 64.7 %collective-permute-start.1 = (f32[32,56,128]{2,1,0:T(8,128)S(1)}, f32[32,56,128]{2,1,0:T(8,128)S(1)}, u32[]{:S(2)}, u32[]{:S(2)}) collective-permute-start(f32[32,56,128]{2,1,0:T(8,128)S(1)} %get-tuple-element.29), channel_id=1, source_target_pairs={{1,0},{2,1},{3,2},{4,3},{5,4},{6,5},{7,6},{8,7},{9,8},{10,9},{11,1... | collective-permute-start | bytes 2752520 | tf_op jit(solution)/shard_map/ppermute | solution.py:494
  46.8 54.9 %copy-start.2 = (f32[8,3,128]{2,0,1:T(8,128)S(1)}, f32[8,3,128]{2,0,1:T(8,128)}, u32[]{:S(2)}) copy-start(f32[8,3,128]{2,0,1:T(8,128)} %param.23) | copy-start | bytes 36868
  46.8 55.5 %copy-start.3 = (f32[4,3,256]{2,0,1:T(4,128)S(1)}, f32[4,3,256]{2,0,1:T(4,128)}, u32[]{:S(2)}) copy-start(f32[4,3,256]{2,0,1:T(4,128)} %param.25) | copy-start | bytes 36868
  46.9 56.2 %copy-start.4 = (s32[8,4]{0,1:T(4,128)S(1)}, s32[8,4]{0,1:T(4,128)}, u32[]{:S(2)}) copy-start(s32[8,4]{0,1:T(4,128)} %param.20) | copy-start | bytes 388
  104.3 0.9 copy-start
  104.3 1.2 copy-start.1
Sparse Core Ops, SparseCore 0:
  35.3 59.7 all-gather.2

commit v2 on v1

v2 whole, which is shorter than its diff:
```python
import functools
import math

import jax
import jax.numpy as jnp
from jax import lax
from jax.experimental import pallas as pl
from jax.experimental.pallas import tpu as pltpu
from jax.sharding import PartitionSpec as P

P_SIZE = 128
CH = 8
HALO = 32
SPLIT = 16
COUNT = 15
TOTAL = 14
NONE = 2 * HALO
RADIX = 128
NEAR_BATCH = 8
FAR_BATCH = 12

highest = lax.Precision.HIGHEST
scale = math.sqrt(3.0) / 12.0
soft = 0.0001 * scale * scale
log2e = math.log2(math.e)
f32 = jnp.float32
bf16 = jnp.bfloat16
NT = (((1,), (1,)), ((), ()))


def hdot(a, b):
    return jnp.dot(a, b, precision=highest, preferred_element_type=f32)


def hdot_nt(a, b):
    return lax.dot_general(a, b, NT, precision=highest, preferred_element_type=f32)


def profile(squared):
    squared = jnp.maximum(squared, soft)
    u = squared * lax.rsqrt(squared)
    return (1.0 + u) * jnp.exp2(u * -log2e)


def split3(v):
    high = v.astype(bf16).astype(f32)
    rest = v - high
    mid = rest.astype(bf16).astype(f32)
    return high, mid, rest - mid


def augmented(x):
    row = lax.broadcasted_iota(jnp.int32, x.shape, 0)
    norm = jnp.sum(x * x, axis=0, keepdims=True)
    source = jnp.where(row < 3, -2.0 * x, jnp.where(row == 3, 1.0, jnp.where(row == 4, norm + soft, 0.0)))
    target = jnp.where(row < 3, x, jnp.where(row == 3, norm, jnp.where(row == 4, 1.0, 0.0)))
    return source, target


def source_rows(v):
    h, m, lo = split3(v)
    return jnp.concatenate([h, m, h, m, lo, h, lo, m], axis=0)


def target_rows(v):
    h, m, lo = split3(v)
    return jnp.concatenate([h, h, m, m, h, lo, m, lo], axis=0)


def coords(block, centre):
    row = lax.broadcasted_iota(jnp.int32, block.shape, 0)
    return jnp.where(row < 3, (block - centre) * scale, 0.0)


def sort_list(ids_ref, out, wide, base):
    width, leaves = ids_ref.shape
    wide[...] = jnp.full(wide.shape, -1, jnp.int32)
    wide[0:width, 0:leaves] = ids_ref[...]
    ids = wide[...]
    shape = ids.shape
    place = ids - base
    valid = ids >= 0
    own = valid & (place >= 0) & (place < leaves)
    other = valid & jnp.logical_not(own)
    slot = jnp.where(own, place, jnp.where(place < 0, place + HALO, place - leaves + HALO))
    ones = jnp.concatenate([own.astype(f32), other.astype(f32)], axis=1)
    row = lax.broadcasted_iota(jnp.int32, shape, 0)
    lane = lax.broadcasted_iota(jnp.int32, shape, 1)
    square = (shape[0], shape[0])
    before = lax.broadcasted_iota(jnp.int32, square, 1) < lax.broadcasted_iota(jnp.int32, square, 0)
    rank = jnp.dot(
        before.astype(f32).astype(bf16), ones.astype(bf16), preferred_element_type=f32
    ).astype(jnp.int32)
    rank = jnp.where(own, rank[:, 0:P_SIZE], rank[:, P_SIZE:])
    goes = jnp.where(own, rank // 2, jnp.where(other, SPLIT + rank // 2, -1))
    value = jnp.where(rank % 2 == 1, slot * RADIX, slot).astype(f32)
    many = jnp.sum(ones, axis=0, keepdims=True).astype(jnp.int32)
    many = jnp.where(row < SPLIT, many[:, 0:P_SIZE], many[:, P_SIZE:])
    at = 2 * (row % SPLIT)
    table = jnp.where(many <= at, 1.0 * NONE, 0.0) + jnp.where(many <= at + 1, 1.0 * NONE * RADIX, 0.0)
    for j in range(width):
        table = table + jnp.where(row == goes[j : j + 1], value[j : j + 1], 0.0)
    groups = jnp.where(lane < leaves, jnp.maximum((many + 1) // 2, 1), 0).astype(f32)
    table = jnp.where(row % SPLIT == COUNT, groups, table)
    total = jnp.sum(groups, axis=1, keepdims=True)
    table = jnp.where((row % SPLIT == TOTAL) & (lane == leaves), total, table)
    square = jnp.concatenate([table, jnp.zeros((P_SIZE - shape[0], P_SIZE), f32)], axis=0).T
    out[...] = square[0 : out.shape[0]].astype(jnp.int32)


def row_of(morton, b, offset):
    return morton.at[pl.ds(offset, morton.shape[0] - CH * P_SIZE + 1)][b * (CH * P_SIZE)]


def fetch(pairs, sems):
    copies = [pltpu.make_async_copy(a, b, sems.at[i]) for i, (a, b) in enumerate(pairs)]
    for copy in copies:
        copy.start()
    return copies


def arrange_kernel(
    morton, near_list, leaf_far, points, probes, skel, sub_skel, basis_hbm, leaf_hbm, box_hbm, sub_hbm,
    geo_lo, geo_hi, near_ids, far_ids, q1_out, packed,
    rows, got, got_too, wide, basis, leaf_tr, box_tr, sub_tr, sems,
):
    copies = fetch(
        ((basis_hbm, basis), (leaf_hbm, leaf_tr), (box_hbm, box_tr), (sub_hbm, sub_tr)), sems
    )
    half = geo_lo.shape[0]
    leaves = 2 * half
    middle = q1_out.shape[0] // 2
    device = lax.axis_index("group") * lax.axis_size("sub") + lax.axis_index("sub")
    sort_list(near_list, near_ids, wide, device * leaves)
    sort_list(leaf_far, far_ids, wide, device * leaves)

    def flip(g, c):
        for j in range(8):
            at = pl.ds(pl.multiple_of((8 * g + j) * P_SIZE, P_SIZE), P_SIZE)
            both = jnp.concatenate(
                [probes[:, at], points[:, at], jnp.zeros((5, P_SIZE), f32)], axis=0
            )
            rows[at, 0:40] = both.T
        return c

    lax.fori_loop(0, leaves // 8, flip, 0)
    for copy in copies:
        copy.wait()

    def gather(b, into):
        for j in range(CH):
            for k in range(P_SIZE):
                into[j, k : k + 1, :] = rows[pl.ds(row_of(morton, b, j * P_SIZE + k), 1), :]

    def combine(b, start, held, geo):
        turned = [held[j].T for j in range(CH)]
        parts = []
        for j in range(CH):
            i = b * CH + j
            at = i - start
            geo[at, 0:40, :] = turned[j][0:40]
            for c in range(3):
                geo[at, 35 + c : 36 + c, 0:64] = skel[c, pl.ds(i, 1), :]
            q0 = hdot_nt(turned[j][0:32], basis[i])
            geo[at, 40:56, 0:64] = q0[0:16]
            geo[at, 40:56, 64:128] = q0[16:32]
            parts.append(q0)
        q1 = jnp.zeros(q1_out.shape[1:], f32)
        for j in range(0, CH, 2):
            two = jnp.concatenate([leaf_tr[b * CH + j], leaf_tr[b * CH + j + 1]], axis=0)
            q1 = q1 + hdot(jnp.concatenate(parts[j : j + 2], axis=1), two)
        q1_out[b] = q1
        return hdot(q1, box_tr[b])

    def two_boxes(g, q2):
        gather(g, got)
        late = combine(middle + jnp.maximum(g - 1, 0), half, got_too, geo_hi)
        gather(middle + g, got_too)
        return q2 + jnp.where(g > 0, late, 0.0) + combine(g, 0, got, geo_lo)

    q2 = lax.fori_loop(0, middle, two_boxes, jnp.zeros((32, packed.shape[1]), f32))
    q2 = q2 + combine(2 * middle - 1, half, got_too, geo_hi)
    packed[0:32, :] = q2
    packed[32:64, :] = hdot(q2, sub_tr[0])
    packed[64:72, :] = jnp.zeros((8, packed.shape[1]), f32)
    for c in range(3):
        packed[64 + c : 65 + c, :] = sub_skel[c]


def prepare_source(block, at, centre_pt, centre_sk, src, xw, src_lo, src_hi, qw):
    geo8 = block[32:40]
    s8, t8 = augmented(coords(geo8, centre_pt))
    src[at] = source_rows(s8).T.astype(bf16)
    turned = jnp.concatenate([geo8[3:8], geo8[0:3]], axis=0)
    ks8, kt8 = augmented(coords(turned, centre_sk))
    low = lax.broadcasted_iota(jnp.int32, (8, P_SIZE), 1) < 64
    ks8 = jnp.where(low, ks8, 0.0)
    src_lo[at] = source_rows(ks8).astype(bf16)
    src_hi[at] = source_rows(pltpu.roll(ks8, 64, 1)).astype(bf16)
    x = block[0:32]
    hi = x.astype(bf16)
    lo = (x - hi.astype(f32)).astype(bf16)
    xw[at] = jnp.concatenate([hi, lo], axis=0)
    q = block[40:56]
    q = jnp.concatenate([q, pltpu.roll(q, 64, 1)], axis=0)
    qhi = q.astype(bf16).astype(f32)
    four = jnp.concatenate([qhi, q - qhi, jnp.zeros((64, P_SIZE), f32)], axis=0)
    qw[at] = four.T[0:64].astype(bf16)
    return t8, kt8


def prepare_target(t8, kt8, at, tgt, tgt_far):
    tgt[at] = target_rows(t8).astype(bf16)
    far = target_rows(kt8)
    tgt_far[at] = jnp.concatenate([far, far], axis=0).T[0:64].astype(bf16)


def clear(refs, at):
    for ref in refs:
        ref[at] = jnp.zeros(ref.shape[1:], ref.dtype)


def batches(ids, lane0, leaves, batch, out, first, part):
    def follow(at):
        leaf, off = at
        more = off + 1 < ids[leaf, lane0 + COUNT]
        return (
            jnp.where(more, leaf, jnp.minimum(leaf + 1, leaves)),
            jnp.where(more, off + 1, 0),
        )

    def take(at):
        got = []
        for _ in range(batch):
            got.append(at)
            at = follow(at)
        return got, at

    def pair(at):
        word = ids[at[0], lane0 + at[1]]
        return at[0], word & (RADIX - 1), word >> 7

    now, at = take((jnp.int32(0), jnp.int32(0)))
    for j in range(batch):
        first(j, pair(now[j]))
    later, at = take(at)

    def one(i, c):
        now, later, at, leaf, acc = c
        for j in range(batch):
            more = part(j, pair(now[j]), pair(later[j]))
            acc = jnp.where(now[j][0] == leaf, acc, 0.0) + more
            leaf = now[j][0]
            out[leaf] = acc
        after, at = take(at)
        return later, after, at, leaf, acc

    total = ids[leaves, lane0 + TOTAL]
    lax.fori_loop(
        0, (total + batch - 1) // batch, one,
        (now, later, at, jnp.int32(0), jnp.zeros(out.shape[1:], f32)),
    )


def halves(k):
    hi = k.astype(bf16)
    return hi, (k - hi.astype(f32)).astype(bf16)


def near_pass(ids, lane0, src, tgt, xw, out, dist):
    def first(j, at):
        leaf, a, b = at
        target = tgt[leaf]
        dist[2 * j] = jnp.dot(src[a], target, preferred_element_type=f32)
        dist[2 * j + 1] = jnp.dot(src[b], target, preferred_element_type=f32)

    def part(j, at, ahead):
        tiles = [jnp.concatenate(halves(profile(dist[2 * j + u])), axis=1) for u in range(2)]
        first(j, ahead)
        acc = jnp.dot(
            jnp.concatenate([xw[at[1]], xw[at[2]]], axis=1),
            jnp.concatenate(tiles, axis=0),
            preferred_element_type=f32,
        )
        return acc[0:32, 0:128] + acc[0:32, 128:256] + acc[32:64, 0:128]

    batches(ids, lane0, tgt.shape[0] - 1, NEAR_BATCH, out, first, part)


def far_pass(ids, lane0, src_lo, src_hi, tgt, qw, out, dist):
    def first(j, at):
        leaf, a, b = at
        source = jnp.concatenate([src_lo[a], src_hi[b]], axis=0)
        dist[j] = jnp.dot(tgt[leaf], source, preferred_element_type=f32)

    def part(j, at, ahead):
        tile = jnp.concatenate(halves(profile(dist[j])), axis=1)
        first(j, ahead)
        a, b = qw[at[1]], qw[at[2]]
        return jnp.dot(
            tile, jnp.concatenate([a, b, a, b], axis=0), preferred_element_type=f32
        )

    batches(ids, lane0, tgt.shape[0] - 1, FAR_BATCH, out, first, part)


def inner_kernel(
    near_ids, far_ids, geo_lo, geo_hi,
    near_out, far_out, tgt, tgt_far, origin,
    src, xw, src_lo, src_hi, qw, near_dist, far_dist,
):
    half = geo_lo.shape[0]
    leaves = 2 * half
    first = geo_lo[0, 32:40, 0:1]
    origin[...] = geo_lo[0, 32:40, :]
    centre_sk = jnp.concatenate([first[3:8], first[0:3]], axis=0)
    sources = (src, xw, src_lo, src_hi, qw)

    def load(g, c):
        for geo, start in ((geo_lo, 0), (geo_hi, half)):
            for j in range(4):
                i = g * 4 + j
                t8, kt8 = prepare_source(geo[i], i + start, first, centre_sk, *sources)
                prepare_target(t8, kt8, i + start, tgt, tgt_far)
        return c

    lax.fori_loop(0, half // 4, load, 0)
    clear(sources, NONE)
    clear((tgt, tgt_far), leaves)
    near_pass(near_ids, 0, src, tgt, xw, near_out, near_dist)
    far_pass(far_ids, 0, src_lo, src_hi, tgt_far, qw, far_out, far_dist)


def centred(block, centre):
    return augmented(coords(block, centre))


def finish_kernel(
    morton, near_ids, far_ids, box_far, sub_far,
    origin, left, right, tgt, tgt_far, near_own, far_own,
    q1, gathered, box_skel3, group_skel3, basis_hbm, leaf_hbm, box_hbm, sub_hbm,
    out,
    near, far, src, xw, src_lo, src_hi, qw, near_dist, far_dist,
    box_skel, group_skel, rows, pad, tall, tall_too, l1s, basis, leaf_tr, box_tr, sub_tr, sems,
    *, subs, groups, box_width, sub_width, near_factor, f0, f1, f2, f3,
):
    copies = fetch(
        ((basis_hbm, basis), (leaf_hbm, leaf_tr), (box_hbm, box_tr), (sub_hbm, sub_tr)), sems
    )
    boxes = q1.shape[0]
    leaves = near.shape[0] - 1
    group = lax.axis_index("group")
    device = group * subs + lax.axis_index("sub")
    first = origin[:, 0:1]
    centre_sk = jnp.concatenate([first[3:8], first[0:3]], axis=0)
    sources = (src, xw, src_lo, src_hi, qw)

    def load(g, c):
        for block, start in ((left, 0), (right, HALO)):
            for j in range(4):
                i = g * 4 + j
                prepare_source(block[i], i + start, first, centre_sk, *sources)
        return c

    lax.fori_loop(0, HALO // 4, load, 0)
    clear(sources, NONE)
    near_pass(near_ids, SPLIT, src, tgt, xw, near, near_dist)
    far_pass(far_ids, SPLIT, src_lo, src_hi, tgt_far, qw, far, far_dist)
    for ref, ref3 in ((box_skel, box_skel3), (group_skel, group_skel3)):
        ref[...] = jnp.zeros_like(ref)
        for b in range(ref.shape[0]):
            for c in range(3):
                ref[b, c : c + 1, :] = ref3[c, b : b + 1, :]
    for copy in copies:
        copy.wait()

    def tile(source8, target8):
        return profile(
            jnp.dot(
                source_rows(source8).T.astype(bf16),
                target_rows(target8).astype(bf16),
                preferred_element_type=f32,
            )
        )

    own = gathered[device, 64:72, :]
    centre = own[:, 0:1]
    target = centred(own, centre)[1]

    def sub_term(j, acc):
        entry = sub_far[j]
        m = jnp.maximum(entry, 0)
        source = centred(gathered[m, 64:72, :], centre)[0]
        term = hdot(gathered[m, 0:32, :], tile(source, target))
        return acc + jnp.where(entry >= 0, term, 0.0)

    many = 4 if sub_width % 4 == 0 else 1

    def sub_terms(g, acc):
        for j in range(many):
            acc = sub_term(g * many + j, acc)
        return acc

    z2 = lax.fori_loop(0, sub_width // many, sub_terms, jnp.zeros(gathered[0, 0:32, :].shape, f32))
    g_own = group_skel[group]
    g_centre = g_own[:, 0:1]
    g_target = centred(g_own, g_centre)[1]

    def group_term(h, acc):
        q3 = lax.fori_loop(
            0, subs, lambda s, t: t + gathered[h * subs + s, 32:64, :], jnp.zeros(z2.shape, f32)
        )
        source = centred(group_skel[h], g_centre)[0]
        return acc + jnp.where(h != group, hdot(q3, tile(source, g_target)), 0.0)

    z3 = jnp.zeros(z2.shape, f32)
    for h in range(groups):
        z3 = group_term(h, z3)
    l2 = z2 * f2 + hdot_nt(z3 * f3, sub_tr[0])

    def box_level(b, c):
        mine = box_skel[b]
        b_centre = mine[:, 0:1]
        b_target = centred(mine, b_centre)[1]

        def box_term(j, acc):
            entry = box_far[j, b]
            m = jnp.maximum(entry - device * boxes, 0)
            source = centred(box_skel[m], b_centre)[0]
            return acc + jnp.where(entry >= 0, hdot(q1[m], tile(source, b_target)), 0.0)

        z1 = jnp.zeros((32, P_SIZE), f32)
        for j in range(box_width):
            z1 = box_term(j, z1)
        l1s[b] = z1 * f1 + hdot_nt(l2, box_tr[b])
        return c

    def box_pair(g, c):
        for j in range(2):
            box_level(2 * g + j, c)
        return c

    lax.fori_loop(0, boxes // 2, box_pair, 0)

    def down(b, into):
        l1 = l1s[b]
        for j in range(CH):
            i = b * CH + j
            turned = (far_own[i] + far[i]).T
            l0 = (turned[0:32] + turned[32:64]) * f0 + hdot_nt(l1, leaf_tr[i])
            pad[j, 0:32, :] = (near_own[i] + near[i]) * near_factor + hdot(l0, basis[i])
        for j in range(CH):
            into[j] = pad[j].T

    def scatter(b, held):
        for j in range(CH):
            for k in range(P_SIZE):
                rows[pl.ds(row_of(morton, b, j * P_SIZE + k), 1), :] = held[j, k : k + 1, :]

    pad[...] = jnp.zeros_like(pad)
    tall_too[...] = jnp.zeros_like(tall_too)

    def two_boxes(g, c):
        scatter(jnp.maximum(2 * g - 1, 1), tall_too)
        down(2 * g, tall)
        scatter(2 * g, tall)
        down(2 * g + 1, tall_too)
        return c

    lax.fori_loop(0, boxes // 2, two_boxes, 0)
    scatter(boxes - 1, tall_too)

    def flip(g, c):
        for j in range(8):
            at = pl.ds(pl.multiple_of((8 * g + j) * P_SIZE, P_SIZE), P_SIZE)
            out[:, at] = rows[at, :].T[0:32]
        return c

    lax.fori_loop(0, leaves // 8, flip, 0)


VMEM = pl.BlockSpec(memory_space=pltpu.VMEM)
SMEM = pl.BlockSpec(memory_space=pltpu.SMEM)
ANY = pl.BlockSpec(memory_space=pl.ANY)
params = pltpu.CompilerParams(vmem_limit_bytes=56 * 2**20)


def body(
    points, probes, morton, near_list, leaf_far, box_far, subtree_far,
    leaf_skeleton, box_skeleton, subtree_skeleton, group_skeleton,
    leaf_basis, leaf_transfer, box_transfer, subtree_transfer,
):
    leaves = near_list.shape[0]
    count = points.shape[1]
    nv = probes.shape[0]
    boxes = box_far.shape[0]
    r0, r1 = leaf_basis.shape[1], box_transfer.shape[1]
    r2, r3 = subtree_transfer.shape[1:]
    subs, groups = lax.axis_size("sub"), lax.axis_size("group")
    i32 = jnp.int32
    front = lambda a: jnp.transpose(a, (1, 0, 2))
    bases = (leaf_basis, leaf_transfer, box_transfer, subtree_transfer)
    held = [pltpu.VMEM(a.shape, f32) for a in bases]
    sems = pltpu.SemaphoreType.DMA((len(bases),))

    geo_lo, geo_hi, near_ids, far_ids, q1, packed = pl.pallas_call(
        arrange_kernel,
        out_shape=(
            jax.ShapeDtypeStruct((leaves // 2, 56, P_SIZE), f32),
            jax.ShapeDtypeStruct((leaves // 2, 56, P_SIZE), f32),
            jax.ShapeDtypeStruct((leaves + 8, P_SIZE), i32),
            jax.ShapeDtypeStruct((leaves + 8, P_SIZE), i32),
            jax.ShapeDtypeStruct((boxes, nv, r1), f32),
            jax.ShapeDtypeStruct((72, r2), f32),
        ),
        in_specs=[SMEM] + [VMEM] * 6 + [ANY] * 4,
        out_specs=(VMEM,) * 6,
        scratch_shapes=[
            pltpu.VMEM((count, P_SIZE), f32),
            pltpu.VMEM((CH, P_SIZE, P_SIZE), f32),
            pltpu.VMEM((CH, P_SIZE, P_SIZE), f32),
            pltpu.VMEM((2 * SPLIT, P_SIZE), i32),
        ]
        + held
        + [sems],
        compiler_params=params,
        name="arrange",
    )(
        morton, near_list.T, leaf_far.T, points, probes, front(leaf_skeleton),
        front(subtree_skeleton), *bases,
    )

    both = ("group", "sub")
    ends = subs * groups - 1
    left = lax.ppermute(geo_hi, both, [(i, i + 1) for i in range(ends)])
    right = lax.ppermute(geo_lo, both, [(i + 1, i) for i in range(ends)])
    gathered = lax.all_gather(packed, both, axis=0)

    acc_shapes = ((leaves + 1, nv, P_SIZE), (leaves + 1, r0, P_SIZE))
    tables = [
        pltpu.VMEM((NONE + 1, P_SIZE, 64), bf16),
        pltpu.VMEM((NONE + 1, 2 * nv, P_SIZE), bf16),
        pltpu.VMEM((NONE + 1, 64, P_SIZE), bf16),
        pltpu.VMEM((NONE + 1, 64, P_SIZE), bf16),
        pltpu.VMEM((NONE + 1, 64, P_SIZE), bf16),
        pltpu.VMEM((2 * NEAR_BATCH, P_SIZE, P_SIZE), f32),
        pltpu.VMEM((FAR_BATCH, 64, P_SIZE), f32),
    ]
    near, far, tgt, tgt_far, origin = pl.pallas_call(
        inner_kernel,
        out_shape=tuple(jax.ShapeDtypeStruct(a, f32) for a in acc_shapes)
        + (
            jax.ShapeDtypeStruct((leaves + 1, 64, P_SIZE), bf16),
            jax.ShapeDtypeStruct((leaves + 1, 64, P_SIZE), bf16),
            jax.ShapeDtypeStruct((8, P_SIZE), f32),
        ),
        in_specs=[SMEM] * 2 + [VMEM] * 2,
        out_specs=(VMEM,) * 5,
        scratch_shapes=tables,
        compiler_params=params,
        cost_estimate=pl.CostEstimate(flops=2 * 10**10, bytes_accessed=10**7, transcendentals=5 * 10**7),
        name="inner",
    )(near_ids, far_ids, geo_lo, geo_hi)

    return pl.pallas_call(
        functools.partial(
            finish_kernel,
            subs=subs,
            groups=groups,
            box_width=box_far.shape[1],
            sub_width=subtree_far.shape[1],
            near_factor=(P_SIZE * near_list.shape[1]) ** -0.5,
            f0=(r0 * leaf_far.shape[1]) ** -0.5,
            f1=(r1 * box_far.shape[1]) ** -0.5,
            f2=(r2 * subtree_far.shape[1]) ** -0.5,
            f3=r3**-0.5,
        ),
        out_shape=jax.ShapeDtypeStruct((nv, count), f32),
        in_specs=[SMEM] * 5 + [VMEM] * 11 + [ANY] * 4,
        out_specs=VMEM,
        scratch_shapes=[pltpu.VMEM(a, f32) for a in acc_shapes]
        + tables
        + [
            pltpu.VMEM((boxes, 8, r1), f32),
            pltpu.VMEM((groups, 8, r3), f32),
            pltpu.VMEM((count, P_SIZE), f32),
            pltpu.VMEM((CH, P_SIZE, P_SIZE), f32),
            pltpu.VMEM((CH, P_SIZE, P_SIZE), f32),
            pltpu.VMEM((CH, P_SIZE, P_SIZE), f32),
            pltpu.VMEM((boxes, nv, P_SIZE), f32),
        ]
        + held
        + [sems],
        compiler_params=params,
        name="finish",
    )(
        morton, near_ids, far_ids, box_far.T, subtree_far.reshape(-1),
        origin, left, right, tgt, tgt_far, near, far,
        q1, gathered, front(box_skeleton), front(group_skeleton), *bases,
    )


def solution(mesh):
    two = ("group", "sub")
    placed = (
        (P(None, two),) * 2
        + (P(two),)
        + (P(two, None),) * 4
        + (P(two, None, None),) * 3
        + (P(),)
        + (P(two, None, None),) * 4
    )
    return jax.shard_map(
        body, mesh=mesh, in_specs=placed, out_specs=P(None, two), check_vma=False
    )
```

time: 181 us -> 154 us (0.85)
  Pallas kernels: 141 us -> 127 us
  local copies, waits for them, and re-layouts: 12.1 us -> 0.01 us
  waiting for transfers between devices: 0.02 us -> 2.9 us
  other arithmetic: 2.07 us -> 0 us
    pallas_call x3 -> x2, Pallas kernels: 101 us -> 70.4 us  [the longest x1 52.8 us: body(): pl.pallas_call(inner_kernel, out_shape=tuple((jax.ShapeDtypeStruct(a, f32...]
    pallas_call x1, Pallas kernels: 40.2 us -> 56.4 us  [body(): pl.pallas_call(functools.partial(finish_kernel, subs=subs, groups=groups,...]
    unnamed x17 -> x4, local copies, waits for them, and re-layouts: 6.41 us -> 0.01 us
    slice x2 -> x0, local copies, waits for them, and re-layouts: 3.85 us -> none  [the longest x1 2.5 us: body(): right = lax.ppermute(geo[:HALO], both, [(i + 1, i) for i in range(ends)])]
    all_gather x1, waiting for transfers between devices: 0.01 us -> 2.88 us  [body(): gathered = lax.all_gather(packed, both, axis=0)]
  transfers between devices with their start and end apart: 3 -> 3, of which waited for: 0 -> 1; matrix products, arithmetic and copies ran while one was open for 4% -> 0% of each run, Pallas kernels for 44% -> 35%
where the time goes in v2:
time: 154 us; the launch traced here: 152 us
  Pallas kernels  127 us (82%)
  between operations  13.5 us (9%)
  starting transfers between devices  9.16 us (6%)
  waiting for transfers between devices  2.9 us (2%)
    pallas_call x1, Pallas kernels, body(): pl.pallas_call(functools.partial(finish_kernel, subs=subs, groups=groups,...  56.4 us
    pallas_call x1, Pallas kernels, body(): pl.pallas_call(inner_kernel, out_shape=tuple((jax.ShapeDtypeStruct(a, f32...  52.8 us
    pallas_call x1, Pallas kernels, body(): pl.pallas_call(arrange_kernel, out_shape=(jax.ShapeDtypeStruct((leaves //...  17.6 us
    ppermute x1, starting transfers between devices, body(): right = lax.ppermute(geo_lo, both, [(i + 1, i) for i in range(ends)])  7.24 us
  transfers between devices with their start and end apart: 3, of which 1 were waited for; matrix products, arithmetic and copies ran while one was open for 0% of the time, Pallas kernels for 35%

profile of v2, /device:TPU:4, one launch (start us, length us, event | category | flops | bytes accessed | tf_op | source)
XLA Modules:
  0.0 152.4 jit_solution(292346106336511230)
XLA Ops:
  6.5 0.0 all-gather.3.cloned.1.call-start
  6.5 17.6 %arrange.1 = (f32[32,56,128]{2,1,0:T(8,128)}, f32[32,56,128]{2,1,0:T(8,128)}, s32[72,128]{1,0:T(8,128)}, s32[72,128]{1,0:T(8,128)}, f32[8,32,128]{2,1,0:T(8,128)}, /*index=5*/f32[72,256]{1,0:T(8,128)}) custom-call(s32[8192]{0:T(1024)} %morton.3, s32[27,64]{1,0:T(8,128)} %bitcast.11, s32[24,64]{1,0:T(8,128)} %bitcast.12, f32[3,8192]{1,0:T(4,128)} %points.1, ...), custom_call_target="tpu_custom_call" | custom-call | tf_op jit(solution)/shard_map/arrange/pallas_call | solution.py:506
  24.2 0.0 all-gather.3.cloned.1.call-update
  24.2 1.9 %collective-permute-start = (f32[32,56,128]{2,1,0:T(8,128)}, f32[32,56,128]{2,1,0:T(8,128)S(1)}, u32[]{:S(2)}, u32[]{:S(2)}) collective-permute-start(f32[32,56,128]{2,1,0:T(8,128)} %get-tuple-element.19.geo_hi), channel_id=1, source_target_pairs={{0,1},{1,2},{2,3},{3,4},{4,5},{5,6},{6,7},{7,8},{8,9},{9,10},{10,1... | collective-permute-start | bytes 2752520 | tf_op jit(solution)/shard_map/ppermute | solution.py:535
  26.1 7.2 %collective-permute-start.1 = (f32[32,56,128]{2,1,0:T(8,128)}, f32[32,56,128]{2,1,0:T(8,128)S(1)}, u32[]{:S(2)}, u32[]{:S(2)}) collective-permute-start(f32[32,56,128]{2,1,0:T(8,128)} %get-tuple-element.18.geo_lo), channel_id=1, source_target_pairs={{1,0},{2,1},{3,2},{4,3},{5,4},{6,5},{7,6},{8,7},{9,8},{10,9},{11,1... | collective-permute-start | bytes 2752520 | tf_op jit(solution)/shard_map/ppermute | solution.py:536
  33.4 52.8 %inner.1 = (f32[65,32,128]{2,1,0:T(8,128)}, f32[65,64,128]{2,1,0:T(8,128)}, bf16[65,64,128]{2,1,0:T(8,128)(2,1)}, bf16[65,64,128]{2,1,0:T(8,128)(2,1)}, f32[8,128]{1,0:T(8,128)}) custom-call(s32[72,128]{1,0:T(8,128)} %get-tuple-element.16.near_ids, s32[72,128]{1,0:T(8,128)} %get-tuple-element.17.far_ids, f32[32,56,128]{2,1,0:T(8,128)} %get-tuple-element.18.geo_lo, ...), custom_call_target="tpu_custom_call" | custom-call | flops 20000000000 | bytes 10000000 | tf_op jit(solution)/shard_map/inner/pallas_call | solution.py:549
  86.2 0.0 collective-permute-done.left
  86.2 0.0 copy-start
  86.2 0.0 collective-permute-done.1.right
  86.2 0.0 copy-start.1
  86.2 2.9 %all-gather.3.cloned.1.call-done = f32[2304,256]{1,0:T(8,128)} async-done(((f32[72,256]{1,0:T(8,128)}), f32[2304,256]{1,0:T(8,128)}) %all-gather.3.cloned.1.call-update) | async-done | bytes 2359312 | tf_op jit(solution)/shard_map/all_gather | solution.py:537
  89.1 0.0 copy-done
  89.1 0.0 copy-done.1
  89.1 56.4 %finish.1 = f32[32,8192]{1,0:T(8,128)} custom-call(s32[8192]{0:T(1024)} %morton.3, s32[72,128]{1,0:T(8,128)} %get-tuple-element.16.near_ids, s32[72,128]{1,0:T(8,128)} %get-tuple-element.17.far_ids, s32[4,8]{1,0:T(4,128)} %bitcast.16, s32[4]{0:T(128)} %bitcast.17, f32[8,128]{1,0:T(8,128)} %get-tuple-element.20.origin, f32[32,56,128]{2,1,0:T(8,128)} %copy-done, ...), custom_call_target="tpu_custom_call" | custom-call | tf_op jit(solution)/shard_map/finish/pallas_call | solution.py:565
Async XLA Ops:
  6.5 82.5 %all-gather.3.cloned.1.call-start = ((), (), s32[]{:S(2)}) async-start(), calls=%async_computation | async-start | bytes 2433024 | tf_op jit(solution)/shard_map/all_gather | solution.py:537
  24.2 61.9 %collective-permute-start = (f32[32,56,128]{2,1,0:T(8,128)}, f32[32,56,128]{2,1,0:T(8,128)S(1)}, u32[]{:S(2)}, u32[]{:S(2)}) collective-permute-start(f32[32,56,128]{2,1,0:T(8,128)} %get-tuple-element.19.geo_hi), channel_id=1, source_target_pairs={{0,1},{1,2},{2,3},{3,4},{4,5},{5,6},{6,7},{7,8},{8,9},{9,10},{10,1... | collective-permute-start | bytes 2752520 | tf_op jit(solution)/shard_map/ppermute | solution.py:535
  26.1 60.0 %collective-permute-start.1 = (f32[32,56,128]{2,1,0:T(8,128)}, f32[32,56,128]{2,1,0:T(8,128)S(1)}, u32[]{:S(2)}, u32[]{:S(2)}) collective-permute-start(f32[32,56,128]{2,1,0:T(8,128)} %get-tuple-element.18.geo_lo), channel_id=1, source_target_pairs={{1,0},{2,1},{3,2},{4,3},{5,4},{6,5},{7,6},{8,7},{9,8},{10,9},{11,1... | collective-permute-start | bytes 2752520 | tf_op jit(solution)/shard_map/ppermute | solution.py:536
  86.2 2.9 %copy-start = (f32[32,56,128]{2,1,0:T(8,128)}, f32[32,56,128]{2,1,0:T(8,128)S(1)}, u32[]{:S(2)}) copy-start(f32[32,56,128]{2,1,0:T(8,128)S(1)} %collective-permute-done.left) | copy-start | bytes 2752516
  86.2 2.9 %copy-start.1 = (f32[32,56,128]{2,1,0:T(8,128)}, f32[32,56,128]{2,1,0:T(8,128)S(1)}, u32[]{:S(2)}) copy-start(f32[32,56,128]{2,1,0:T(8,128)S(1)} %collective-permute-done.1.right) | copy-start | bytes 2752516
Sparse Core Ops, SparseCore 0:
  24.3 64.6 all-gather.2

commit v3 on v2

--- a/solution.py
+++ b/solution.py
@@ -11,13 +11,13 @@
 P_SIZE = 128
 CH = 8
 HALO = 32
-SPLIT = 16
-COUNT = 15
-TOTAL = 14
+SLOTS = 16
 NONE = 2 * HALO
 RADIX = 128
-NEAR_BATCH = 8
-FAR_BATCH = 12
+FLAT = 8 * P_SIZE
+REACH = FLAT - 48
+NEAR_BATCH = 16
+FAR_BATCH = 14
 
 highest = lax.Precision.HIGHEST
 scale = math.sqrt(3.0) / 12.0
@@ -72,7 +72,7 @@
     return jnp.where(row < 3, (block - centre) * scale, 0.0)
 
 
-def sort_list(ids_ref, out, wide, base):
+def sort_list(ids_ref, outs, wide, base):
     width, leaves = ids_ref.shape
     wide[...] = jnp.full(wide.shape, -1, jnp.int32)
     wide[0:width, 0:leaves] = ids_ref[...]
@@ -91,21 +91,50 @@
     rank = jnp.dot(
         before.astype(f32).astype(bf16), ones.astype(bf16), preferred_element_type=f32
     ).astype(jnp.int32)
-    rank = jnp.where(own, rank[:, 0:P_SIZE], rank[:, P_SIZE:])
-    goes = jnp.where(own, rank // 2, jnp.where(other, SPLIT + rank // 2, -1))
-    value = jnp.where(rank % 2 == 1, slot * RADIX, slot).astype(f32)
-    many = jnp.sum(ones, axis=0, keepdims=True).astype(jnp.int32)
-    many = jnp.where(row < SPLIT, many[:, 0:P_SIZE], many[:, P_SIZE:])
-    at = 2 * (row % SPLIT)
-    table = jnp.where(many <= at, 1.0 * NONE, 0.0) + jnp.where(many <= at + 1, 1.0 * NONE * RADIX, 0.0)
-    for j in range(width):
-        table = table + jnp.where(row == goes[j : j + 1], value[j : j + 1], 0.0)
-    groups = jnp.where(lane < leaves, jnp.maximum((many + 1) // 2, 1), 0).astype(f32)
-    table = jnp.where(row % SPLIT == COUNT, groups, table)
-    total = jnp.sum(groups, axis=1, keepdims=True)
-    table = jnp.where((row % SPLIT == TOTAL) & (lane == leaves), total, table)
-    square = jnp.concatenate([table, jnp.zeros((P_SIZE - shape[0], P_SIZE), f32)], axis=0).T
-    out[...] = square[0 : out.shape[0]].astype(jnp.int32)
+    total = jnp.sum(ones, axis=0, keepdims=True).astype(jnp.int32)
+    value = slot.astype(f32)
+    square = (P_SIZE, P_SIZE)
+    ahead = lax.broadcasted_iota(jnp.int32, square, 0) < lax.broadcasted_iota(jnp.int32, square, 1)
+    ahead = ahead.astype(f32).astype(bf16)
+    lane8 = lane[0:8]
+    row8 = row[0:8]
+    for part, out in enumerate(outs):
+        mask = (own, other)[part]
+        order = jnp.where(mask, rank[:, part * P_SIZE : (part + 1) * P_SIZE], -1)
+        goes = jnp.where(order % 2 == 1, SLOTS + order // 2, order // 2)
+        goes = jnp.where(mask, goes, -1)
+        many = total[:, part * P_SIZE : (part + 1) * P_SIZE]
+        at = jnp.where(row < SLOTS, 2 * row, 2 * (row - SLOTS) + 1)
+        table = jnp.where(many <= at, 1.0 * NONE, 0.0)
+        for j in range(width):
+            table = table + jnp.where(row == goes[j : j + 1], value[j : j + 1], 0.0)
+        groups = jnp.where(lane8 < leaves, jnp.maximum((many + 1) // 2, 1), 0)
+        start = jnp.dot(
+            groups.astype(f32).astype(bf16), ahead, preferred_element_type=f32
+        ).astype(jnp.int32)
+        stop = jnp.where(lane8 == leaves, FLAT, start + groups)
+        extra = jnp.where(
+            row8 == 0, start // 32, jnp.where(row8 == 1, start % 32, jnp.where(row8 == 2, lane8, 0))
+        )
+        look = jnp.concatenate([table, extra.astype(f32)], axis=0).astype(bf16)
+        ends = jnp.concatenate(
+            [jnp.where(row8 == 0, start, stop).astype(f32), jnp.zeros((P_SIZE - 8, P_SIZE), f32)],
+            axis=0,
+        ).T
+        begin, end = ends[:, 0:1], ends[:, 1:2]
+        spot = lax.broadcasted_iota(jnp.int32, square, 1).astype(f32)
+        for t in range(FLAT // P_SIZE):
+            here = spot + 1.0 * t * P_SIZE
+            hot = ((begin <= here) & (here < end)).astype(f32).astype(bf16)
+            found = jnp.dot(look, hot, preferred_element_type=f32)
+            k = here[0:1] - (found[32:33] * 32.0 + found[33:34])
+            pick = row[0:SLOTS].astype(f32) == k
+            a = jnp.sum(jnp.where(pick, found[0:SLOTS], 0.0), axis=0, keepdims=True)
+            b = jnp.sum(jnp.where(pick, found[SLOTS : 2 * SLOTS], 0.0), axis=0, keepdims=True)
+            word = a + b * RADIX + found[34:35] * (RADIX * RADIX)
+            out[t : t + 1, :] = word.astype(jnp.int32)
+        count = start[0:1, leaves : leaves + 1]
+        out[7:8, P_SIZE - 1 : P_SIZE] = count
 
 
 def row_of(morton, b, offset):
@@ -121,7 +150,7 @@
 
 def arrange_kernel(
     morton, near_list, leaf_far, points, probes, skel, sub_skel, basis_hbm, leaf_hbm, box_hbm, sub_hbm,
-    geo_lo, geo_hi, near_ids, far_ids, q1_out, packed,
+    geo_lo, geo_hi, near_ids, near_ids_out, far_ids, far_ids_out, q1_out, packed,
     rows, got, got_too, wide, basis, leaf_tr, box_tr, sub_tr, sems,
 ):
     copies = fetch(
@@ -131,8 +160,8 @@
     leaves = 2 * half
     middle = q1_out.shape[0] // 2
     device = lax.axis_index("group") * lax.axis_size("sub") + lax.axis_index("sub")
-    sort_list(near_list, near_ids, wide, device * leaves)
-    sort_list(leaf_far, far_ids, wide, device * leaves)
+    sort_list(near_list, (near_ids, near_ids_out), wide, device * leaves)
+    sort_list(leaf_far, (far_ids, far_ids_out), wide, device * leaves)
 
     def flip(g, c):
         for j in range(8):
@@ -220,46 +249,41 @@
         ref[at] = jnp.zeros(ref.shape[1:], ref.dtype)
 
 
-def batches(ids, lane0, leaves, batch, out, first, part):
-    def follow(at):
-        leaf, off = at
-        more = off + 1 < ids[leaf, lane0 + COUNT]
-        return (
-            jnp.where(more, leaf, jnp.minimum(leaf + 1, leaves)),
-            jnp.where(more, off + 1, 0),
-        )
-
-    def take(at):
-        got = []
-        for _ in range(batch):
-            got.append(at)
-            at = follow(at)
-        return got, at
-
-    def pair(at):
-        word = ids[at[0], lane0 + at[1]]
-        return at[0], word & (RADIX - 1), word >> 7
-
-    now, at = take((jnp.int32(0), jnp.int32(0)))
-    for j in range(batch):
-        first(j, pair(now[j]))
-    later, at = take(at)
-
+def stream(ids, leaves, batch, out, first, part):
+    def entry(i, j):
+        word = ids.at[pl.ds(j, REACH)][i * batch]
+        return word >> 14, word & (RADIX - 1), (word >> 7) & (RADIX - 1)
+
+    def start():
+        for j in range(batch):
+            first(j, entry(0, j))
+        return jnp.int32(0), jnp.zeros(out.shape[1:], f32)
+
+    def steps(i, c):
+        leaf, acc = c
+        for j in range(batch):
+            now = entry(i, j)
+            more = part(j, now, entry(i, j + batch))
+            acc = jnp.where(now[0] == leaf, acc, 0.0) + more
+            leaf = now[0]
+            out[leaf] = acc
+            yield None
+        yield leaf, acc
+
+    trips = (ids[FLAT - 1] + batch - 1) // batch
+    return start, steps, trips
+
+
+def run(*streams):
     def one(i, c):
-        now, later, at, leaf, acc = c
-        for j in range(batch):
-            more = part(j, pair(now[j]), pair(later[j]))
-            acc = jnp.where(now[j][0] == leaf, acc, 0.0) + more
-            leaf = now[j][0]
-            out[leaf] = acc
-        after, at = take(at)
-        return later, after, at, leaf, acc
-
-    total = ids[leaves, lane0 + TOTAL]
-    lax.fori_loop(
-        0, (total + batch - 1) // batch, one,
-        (now, later, at, jnp.int32(0), jnp.zeros(out.shape[1:], f32)),
-    )
+        work = [steps(i, held) for (_, steps, _), held in zip(streams, c)]
+        done = [None] * len(work)
+        while any(d is None for d in done):
+            done = [next(w) if d is None else d for w, d in zip(work, done)]
+        return tuple(done)
+
+    trips = functools.reduce(jnp.maximum, [t for _, _, t in streams])
+    lax.fori_loop(0, trips, one, tuple(start() for start, _, _ in streams))
 
 
 def halves(k):
@@ -267,7 +291,7 @@
     return hi, (k - hi.astype(f32)).astype(bf16)
 
 
-def near_pass(ids, lane0, src, tgt, xw, out, dist):
+def near_pass(ids, src, tgt, xw, out, dist):
     def first(j, at):
         leaf, a, b = at
         target = tgt[leaf]
@@ -284,10 +308,10 @@
         )
         return acc[0:32, 0:128] + acc[0:32, 128:256] + acc[32:64, 0:128]
 
-    batches(ids, lane0, tgt.shape[0] - 1, NEAR_BATCH, out, first, part)
-
-
-def far_pass(ids, lane0, src_lo, src_hi, tgt, qw, out, dist):
+    return stream(ids, tgt.shape[0] - 1, NEAR_BATCH, out, first, part)
+
+
+def far_pass(ids, src_lo, src_hi, tgt, qw, out, dist):
     def first(j, at):
         leaf, a, b = at
         source = jnp.concatenate([src_lo[a], src_hi[b]], axis=0)
@@ -301,7 +325,7 @@
             tile, jnp.concatenate([a, b, a, b], axis=0), preferred_element_type=f32
         )
 
-    batches(ids, lane0, tgt.shape[0] - 1, FAR_BATCH, out, first, part)
+    return stream(ids, tgt.shape[0] - 1, FAR_BATCH, out, first, part)
 
 
 def inner_kernel(
@@ -327,30 +351,17 @@
     lax.fori_loop(0, half // 4, load, 0)
     clear(sources, NONE)
     clear((tgt, tgt_far), leaves)
-    near_pass(near_ids, 0, src, tgt, xw, near_out, near_dist)
-    far_pass(far_ids, 0, src_lo, src_hi, tgt_far, qw, far_out, far_dist)
-
-
-def centred(block, centre):
-    return augmented(coords(block, centre))
-
-
-def finish_kernel(
-    morton, near_ids, far_ids, box_far, sub_far,
-    origin, left, right, tgt, tgt_far, near_own, far_own,
-    q1, gathered, box_skel3, group_skel3, basis_hbm, leaf_hbm, box_hbm, sub_hbm,
-    out,
-    near, far, src, xw, src_lo, src_hi, qw, near_dist, far_dist,
-    box_skel, group_skel, rows, pad, tall, tall_too, l1s, basis, leaf_tr, box_tr, sub_tr, sems,
-    *, subs, groups, box_width, sub_width, near_factor, f0, f1, f2, f3,
+    run(
+        near_pass(near_ids, src, tgt, xw, near_out, near_dist),
+        far_pass(far_ids, src_lo, src_hi, tgt_far, qw, far_out, far_dist),
+    )
+
+
+def outer_kernel(
+    near_ids, far_ids, origin, left, right, tgt, tgt_far,
+    near_out, far_out,
+    src, xw, src_lo, src_hi, qw, near_dist, far_dist,
 ):
-    copies = fetch(
-        ((basis_hbm, basis), (leaf_hbm, leaf_tr), (box_hbm, box_tr), (sub_hbm, sub_tr)), sems
-    )
-    boxes = q1.shape[0]
-    leaves = near.shape[0] - 1
-    group = lax.axis_index("group")
-    device = group * subs + lax.axis_index("sub")
     first = origin[:, 0:1]
     centre_sk = jnp.concatenate([first[3:8], first[0:3]], axis=0)
     sources = (src, xw, src_lo, src_hi, qw)
@@ -364,8 +375,32 @@
 
     lax.fori_loop(0, HALO // 4, load, 0)
     clear(sources, NONE)
-    near_pass(near_ids, SPLIT, src, tgt, xw, near, near_dist)
-    far_pass(far_ids, SPLIT, src_lo, src_hi, tgt_far, qw, far, far_dist)
+    run(
+        near_pass(near_ids, src, tgt, xw, near_out, near_dist),
+        far_pass(far_ids, src_lo, src_hi, tgt_far, qw, far_out, far_dist),
+    )
+
+
+def centred(block, centre):
+    return augmented(coords(block, centre))
+
+
+def finish_kernel(
+    morton, box_far, sub_far, near_own, far_own, near, far,
+    q1, family, tops, box_skel3, group_skel3, basis_hbm, leaf_hbm, box_hbm, sub_hbm,
+    out,
+    box_skel, group_skel, rows, pad, tall, tall_too, l1s, basis, leaf_tr, box_tr, sub_tr, sems,
+    *, groups, box_width, sub_width, near_factor, f0, f1, f2, f3,
+):
+    copies = fetch(
+        ((basis_hbm, basis), (leaf_hbm, leaf_tr), (box_hbm, box_tr), (sub_hbm, sub_tr)), sems
+    )
+    boxes = q1.shape[0]
+    leaves = near.shape[0] - 1
+    group = lax.axis_index("group")
+    sub = lax.axis_index("sub")
+    subs = lax.axis_size("sub")
+    device = group * subs + sub
     for ref, ref3 in ((box_skel, box_skel3), (group_skel, group_skel3)):
         ref[...] = jnp.zeros_like(ref)
         for b in range(ref.shape[0]):
@@ -383,15 +418,15 @@
             )
         )
 
-    own = gathered[device, 64:72, :]
+    own = family[sub, 64:72, :]
     centre = own[:, 0:1]
     target = centred(own, centre)[1]
 
     def sub_term(j, acc):
         entry = sub_far[j]
-        m = jnp.maximum(entry, 0)
-        source = centred(gathered[m, 64:72, :], centre)[0]
-        term = hdot(gathered[m, 0:32, :], tile(source, target))
+        m = jnp.maximum(entry - group * subs, 0)
+        source = centred(family[m, 64:72, :], centre)[0]
+        term = hdot(family[m, 0:32, :], tile(source, target))
         return acc + jnp.where(entry >= 0, term, 0.0)
 
     many = 4 if sub_width % 4 == 0 else 1
@@ -401,17 +436,14 @@
             acc = sub_term(g * many + j, acc)
         return acc
 
-    z2 = lax.fori_loop(0, sub_width // many, sub_terms, jnp.zeros(gathered[0, 0:32, :].shape, f32))
+    z2 = lax.fori_loop(0, sub_width // many, sub_terms, jnp.zeros((32, family.shape[2]), f32))
     g_own = group_skel[group]
     g_centre = g_own[:, 0:1]
     g_target = centred(g_own, g_centre)[1]
 
     def group_term(h, acc):
-        q3 = lax.fori_loop(
-            0, subs, lambda s, t: t + gathered[h * subs + s, 32:64, :], jnp.zeros(z2.shape, f32)
-        )
         source = centred(group_skel[h], g_centre)[0]
-        return acc + jnp.where(h != group, hdot(q3, tile(source, g_target)), 0.0)
+        return acc + jnp.where(h != group, hdot(tops[h], tile(source, g_target)), 0.0)
 
     z3 = jnp.zeros(z2.shape, f32)
     for h in range(groups):
@@ -503,23 +535,22 @@
     held = [pltpu.VMEM(a.shape, f32) for a in bases]
     sems = pltpu.SemaphoreType.DMA((len(bases),))
 
-    geo_lo, geo_hi, near_ids, far_ids, q1, packed = pl.pallas_call(
+    geo_lo, geo_hi, near_ids, near_ids_out, far_ids, far_ids_out, q1, packed = pl.pallas_call(
         arrange_kernel,
         out_shape=(
             jax.ShapeDtypeStruct((leaves // 2, 56, P_SIZE), f32),
             jax.ShapeDtypeStruct((leaves // 2, 56, P_SIZE), f32),
-            jax.ShapeDtypeStruct((leaves + 8, P_SIZE), i32),
-            jax.ShapeDtypeStruct((leaves + 8, P_SIZE), i32),
+            *[jax.ShapeDtypeStruct((FLAT // P_SIZE, P_SIZE), i32)] * 4,
             jax.ShapeDtypeStruct((boxes, nv, r1), f32),
             jax.ShapeDtypeStruct((72, r2), f32),
         ),
         in_specs=[SMEM] + [VMEM] * 6 + [ANY] * 4,
-        out_specs=(VMEM,) * 6,
+        out_specs=(VMEM,) * 8,
         scratch_shapes=[
             pltpu.VMEM((count, P_SIZE), f32),
             pltpu.VMEM((CH, P_SIZE, P_SIZE), f32),
             pltpu.VMEM((CH, P_SIZE, P_SIZE), f32),
-            pltpu.VMEM((2 * SPLIT, P_SIZE), i32),
+            pltpu.VMEM((2 * SLOTS, P_SIZE), i32),
         ]
         + held
         + [sems],
@@ -534,7 +565,7 @@
     ends = subs * groups - 1
     left = lax.ppermute(geo_hi, both, [(i, i + 1) for i in range(ends)])
     right = lax.ppermute(geo_lo, both, [(i + 1, i) for i in range(ends)])
-    gathered = lax.all_gather(packed, both, axis=0)
+    family = lax.all_gather(packed, "sub", axis=0)
 
     acc_shapes = ((leaves + 1, nv, P_SIZE), (leaves + 1, r0, P_SIZE))
     tables = [
@@ -560,12 +591,23 @@
         compiler_params=params,
         cost_estimate=pl.CostEstimate(flops=2 * 10**10, bytes_accessed=10**7, transcendentals=5 * 10**7),
         name="inner",
-    )(near_ids, far_ids, geo_lo, geo_hi)
+    )(near_ids.reshape(-1), far_ids.reshape(-1), geo_lo, geo_hi)
+
+    tops = lax.all_gather(jnp.sum(family[:, nv : 2 * nv, :], axis=0), "group", axis=0)
+    near_halo, far_halo = pl.pallas_call(
+        outer_kernel,
+        out_shape=tuple(jax.ShapeDtypeStruct(a, f32) for a in acc_shapes),
+        in_specs=[SMEM] * 2 + [VMEM] * 5,
+        out_specs=(VMEM,) * 2,
+        scratch_shapes=tables,
+        compiler_params=params,
+        cost_estimate=pl.CostEstimate(flops=10**10, bytes_accessed=10**7, transcendentals=3 * 10**7),
+        name="outer",
+    )(near_ids_out.reshape(-1), far_ids_out.reshape(-1), origin, left, right, tgt, tgt_far)
 
     return pl.pallas_call(
         functools.partial(
             finish_kernel,
-            subs=subs,
             groups=groups,
             box_width=box_far.shape[1],
             sub_width=subtree_far.shape[1],
@@ -576,11 +618,9 @@
             f3=r3**-0.5,
         ),
         out_shape=jax.ShapeDtypeStruct((nv, count), f32),
-        in_specs=[SMEM] * 5 + [VMEM] * 11 + [ANY] * 4,
+        in_specs=[SMEM] * 3 + [VMEM] * 9 + [ANY] * 4,
         out_specs=VMEM,
-        scratch_shapes=[pltpu.VMEM(a, f32) for a in acc_shapes]
-        + tables
-        + [
+        scratch_shapes=[
             pltpu.VMEM((boxes, 8, r1), f32),
             pltpu.VMEM((groups, 8, r3), f32),
             pltpu.VMEM((count, P_SIZE), f32),
@@ -594,9 +634,8 @@
         compiler_params=params,
         name="finish",
     )(
-        morton, near_ids, far_ids, box_far.T, subtree_far.reshape(-1),
-        origin, left, right, tgt, tgt_far, near, far,
-        q1, gathered, front(box_skeleton), front(group_skeleton), *bases,
+        morton, box_far.T, subtree_far.reshape(-1), near, far, near_halo, far_halo,
+        q1, family, tops, front(box_skeleton), front(group_skeleton), *bases,
     )
 
 

time: 154 us -> 157 us (1.019); the launches traced: 152 us -> 157 us
  blocking collectives: 0 us -> 24.6 us
  between operations: 13.5 us -> 0.23 us
  Pallas kernels: 127 us -> 122 us
  waiting for transfers between devices: 2.9 us -> 0.01 us
    all_gather x0 -> x2, blocking collectives: none -> 24.6 us  [the longest x1 15.2 us: body(): family = lax.all_gather(packed, 'sub', axis=0)]
    pallas_call x1, Pallas kernels: 52.8 us -> 45.2 us  [body(): pl.pallas_call(inner_kernel, out_shape=tuple((jax.ShapeDtypeStruct(a, f32...]
    all_gather x1 -> x0, waiting for transfers between devices: 2.88 us -> none  [body(): gathered = lax.all_gather(packed, both, axis=0)]
    pallas_call x1 -> x2, Pallas kernels: 56.4 us -> 58.2 us  [the longest x1 35.8 us: body(): pl.pallas_call(functools.partial(finish_kernel, groups=groups, box_width=...]
  transfers between devices with their start and end apart: 3 -> 2, of which waited for: 1 -> 0; matrix products, arithmetic and copies ran while one was open for 0% -> 0% of each run, Pallas kernels for 35% -> 29%
where the time goes in v3:
time: 157 us
  Pallas kernels  122 us (78%)
  blocking collectives  24.6 us (16%)
  starting transfers between devices  9.16 us (6%)
    pallas_call x1, Pallas kernels, body(): pl.pallas_call(inner_kernel, out_shape=tuple((jax.ShapeDtypeStruct(a, f32...  45.2 us
    pallas_call x1, Pallas kernels, body(): pl.pallas_call(functools.partial(finish_kernel, groups=groups, box_width=...  35.8 us
    pallas_call x1, Pallas kernels, body(): pl.pallas_call(outer_kernel, out_shape=tuple((jax.ShapeDtypeStruct(a, f32...  22.4 us
    pallas_call x1, Pallas kernels, body(): pl.pallas_call(arrange_kernel, out_shape=(jax.ShapeDtypeStruct((leaves //...  18.7 us
    all_gather x1, blocking collectives, body(): family = lax.all_gather(packed, 'sub', axis=0)  15.2 us
    all_gather x1, blocking collectives, body(): lax.all_gather(jnp.sum(family[:, nv:2 * nv, :], axis=0), 'group', axis=0)  9.39 us
    ppermute x1, starting transfers between devices, body(): right = lax.ppermute(geo_lo, both, [(i + 1, i) for i in range(ends)])  7.24 us
  transfers between devices with their start and end apart: 2, of which 0 were waited for; matrix products, arithmetic and copies ran while one was open for 0% of the time, Pallas kernels for 29%

profile of v3, /device:TPU:4, one launch (start us, length us, event | category | flops | bytes accessed | tf_op | source)
XLA Modules:
  0.0 157.3 jit_solution(2675914123342876044)
XLA Ops:
  0.0 18.7 %arrange.1 = (f32[32,56,128]{2,1,0:T(8,128)}, f32[32,56,128]{2,1,0:T(8,128)}, s32[8,128]{1,0:T(8,128)}, s32[8,128]{1,0:T(8,128)}, s32[8,128]{1,0:T(8,128)}, /*in...) custom-call(s32[8192]{0:T(1024)} %morton.3, s32[27,64]{1,0:T(8,128)} %bitcast.18, s32[24,64]{1,0:T(8,128)} %bitcast.19, ...), custom_call_target="tpu_custom_call" | custom-call | tf_op jit(solution)/shard_map/arrange/pallas_call | solution.py:538
  18.7 1.9 %collective-permute-start = (f32[32,56,128]{2,1,0:T(8,128)}, f32[32,56,128]{2,1,0:T(8,128)S(1)}, u32[]{:S(2)}, u32[]{:S(2)}) collective-permute-start(f32[32,56,128]{2,1,0:T(8,128)} %get-tuple-element.23.geo_hi), channel_id=1, source_target_pairs={{0,1},{1,2},{2,3},{3,4},{4,5},{5,6},{6,7},{7,8},{8,9},{9,10},{10,1... | collective-permute-start | bytes 2752520 | tf_op jit(solution)/shard_map/ppermute | solution.py:566
  20.7 7.2 %collective-permute-start.1 = (f32[32,56,128]{2,1,0:T(8,128)}, f32[32,56,128]{2,1,0:T(8,128)S(1)}, u32[]{:S(2)}, u32[]{:S(2)}) collective-permute-start(f32[32,56,128]{2,1,0:T(8,128)} %get-tuple-element.22.geo_lo), channel_id=1, source_target_pairs={{1,0},{2,1},{3,2},{4,3},{5,4},{6,5},{7,6},{8,7},{9,8},{10,9},{11,1... | collective-permute-start | bytes 2752520 | tf_op jit(solution)/shard_map/ppermute | solution.py:567
  27.9 0.0 copy-start.1
  27.9 45.2 %inner.1 = (f32[65,32,128]{2,1,0:T(8,128)}, f32[65,64,128]{2,1,0:T(8,128)}, bf16[65,64,128]{2,1,0:T(8,128)(2,1)}, bf16[65,64,128]{2,1,0:T(8,128)(2,1)}, f32[8,128]{1,0:T(8,128)}) custom-call(s32[1024]{0:T(1024)} %bitcast.27, s32[1024]{0:T(1024)} %bitcast.28, f32[32,56,128]{2,1,0:T(8,128)} %get-tuple-element.22.geo_lo, f32[32,56,128]{2,1,0:T(8,128)} %get-tuple-element.23.geo_hi), custom_call_target="tpu_custom_call" | custom-call | flops 20000000000 | bytes 10000000 | tf_op jit(solution)/shard_map/inner/pallas_call | solution.py:580
  73.1 0.0 copy-done.1
  73.1 15.2 %all-gather = f32[576,256]{1,0:T(8,128)S(1)} all-gather(f32[72,256]{1,0:T(8,128)S(1)} %copy-done.1), channel_id=2, replica_groups=mesh['group'=4,'sub'=8] {'sub'}, dimensions={0}, use_global_device_ids=true | all-gather | bytes 663552 | tf_op jit(solution)/shard_map/all_gather | solution.py:568
  88.3 0.0 copy-start
  88.3 9.4 %all-gather.1 = f32[128,256]{1,0:T(8,128)} all-gather(f32[32,256]{1,0:T(8,128)S(1)} %slice_reduce_fusion), channel_id=3, replica_groups=mesh['group'=4,'sub'=8] {'group'}, dimensions={0}, use_global_device_ids=true | all-gather | bytes 163840 | tf_op jit(solution)/shard_map/all_gather | solution.py:596
  97.7 0.0 collective-permute-done.left
  97.7 0.0 copy-start.2
  97.7 0.0 collective-permute-done.1.right
  97.7 0.0 copy-start.3
  97.8 1.0 copy-done.2
  98.7 0.2 copy-done.3
  98.9 22.4 %outer.1 = (f32[65,32,128]{2,1,0:T(8,128)}, f32[65,64,128]{2,1,0:T(8,128)}) custom-call(s32[1024]{0:T(1024)} %bitcast.25, s32[1024]{0:T(1024)} %bitcast.26, f32[8,128]{1,0:T(8,128)} %get-tuple-element.28.origin, f32[32,56,128]{2,1,0:T(8,128)} %copy-done.2, f32[32,56,128]{2,1,0:T(8,128)} %copy-done.3, bf16[65,64,128]{2,1,0:T(8,128)(2,1)} %get-tuple-element.29.tgt, ...), custom_call_target="tpu_custom_call" | custom-call | flops 10000000000 | bytes 10000000 | tf_op jit(solution)/shard_map/outer/pallas_call | solution.py:597
  121.4 0.0 copy-done
  121.4 35.8 %finish.1 = f32[32,8192]{1,0:T(8,128)} custom-call(s32[8192]{0:T(1024)} %morton.3, s32[4,8]{1,0:T(4,128)} %bitcast.23, s32[4]{0:T(128)} %bitcast.24, f32[65,32,128]{2,1,0:T(8,128)} %get-tuple-element.24.near_own, f32[65,64,128]{2,1,0:T(8,128)} %get-tuple-element.25.far_own, f32[65,32,128]{2,1,0:T(8,128)} %get-tuple-element.31.near, ...), custom_call_target="tpu_custom_call" | custom-call | tf_op jit(solution)/shard_map/finish/pallas_call | solution.py:608
  (1 shorter events, 0.0 us)
Async XLA Ops:
  18.7 79.0 %collective-permute-start = (f32[32,56,128]{2,1,0:T(8,128)}, f32[32,56,128]{2,1,0:T(8,128)S(1)}, u32[]{:S(2)}, u32[]{:S(2)}) collective-permute-start(f32[32,56,128]{2,1,0:T(8,128)} %get-tuple-element.23.geo_hi), channel_id=1, source_target_pairs={{0,1},{1,2},{2,3},{3,4},{4,5},{5,6},{6,7},{7,8},{8,9},{9,10},{10,1... | collective-permute-start | bytes 2752520 | tf_op jit(solution)/shard_map/ppermute | solution.py:566
  20.7 77.1 %collective-permute-start.1 = (f32[32,56,128]{2,1,0:T(8,128)}, f32[32,56,128]{2,1,0:T(8,128)S(1)}, u32[]{:S(2)}, u32[]{:S(2)}) collective-permute-start(f32[32,56,128]{2,1,0:T(8,128)} %get-tuple-element.22.geo_lo), channel_id=1, source_target_pairs={{1,0},{2,1},{3,2},{4,3},{5,4},{6,5},{7,6},{8,7},{9,8},{10,9},{11,1... | collective-permute-start | bytes 2752520 | tf_op jit(solution)/shard_map/ppermute | solution.py:567
  27.9 45.2 %copy-start.1 = (f32[72,256]{1,0:T(8,128)S(1)}, f32[72,256]{1,0:T(8,128)}, u32[]{:S(2)}) copy-start(f32[72,256]{1,0:T(8,128)} %get-tuple-element.34) | copy-start | bytes 221188
  88.3 33.1 %copy-start = (f32[576,256]{1,0:T(8,128)}, f32[576,256]{1,0:T(8,128)S(1)}, u32[]{:S(2)}) copy-start(f32[576,256]{1,0:T(8,128)S(1)} %all-gather) | copy-start | bytes 1769476
  97.7 1.0 copy-start.2
  97.7 1.2 copy-start.3

commit v4 on v3

--- a/solution.py
+++ b/solution.py
@@ -19,7 +19,6 @@
 NEAR_BATCH = 16
 FAR_BATCH = 14
 
-highest = lax.Precision.HIGHEST
 scale = math.sqrt(3.0) / 12.0
 soft = 0.0001 * scale * scale
 log2e = math.log2(math.e)
@@ -28,12 +27,40 @@
 NT = (((1,), (1,)), ((), ()))
 
 
+def halves(k):
+    hi = k.astype(bf16)
+    return hi, (k - hi.astype(f32)).astype(bf16)
+
+
 def hdot(a, b):
-    return jnp.dot(a, b, precision=highest, preferred_element_type=f32)
+    ah, al = halves(a)
+    bh, bl = halves(b)
+    return jnp.dot(
+        jnp.concatenate([ah, al, ah], axis=1),
+        jnp.concatenate([bh, bh, bl], axis=0),
+        preferred_element_type=f32,
+    )
 
 
 def hdot_nt(a, b):
-    return lax.dot_general(a, b, NT, precision=highest, preferred_element_type=f32)
+    ah, al = halves(a)
+    bh, bl = halves(b)
+    return lax.dot_general(
+        jnp.concatenate([ah, al, ah], axis=1),
+        jnp.concatenate([bh, bh, bl], axis=1),
+        NT,
+        preferred_element_type=f32,
+    )
+
+
+def weigh(q, k):
+    n = k.shape[1]
+    both = jnp.dot(
+        jnp.concatenate(halves(q), axis=0),
+        jnp.concatenate(halves(k), axis=1),
+        preferred_element_type=f32,
+    )
+    return both[0:32, 0:n] + both[0:32, n:] + both[32:64, 0:n]
 
 
 def profile(squared):
@@ -286,11 +313,6 @@
     lax.fori_loop(0, trips, one, tuple(start() for start, _, _ in streams))
 
 
-def halves(k):
-    hi = k.astype(bf16)
-    return hi, (k - hi.astype(f32)).astype(bf16)
-
-
 def near_pass(ids, src, tgt, xw, out, dist):
     def first(j, at):
         leaf, a, b = at
@@ -326,6 +348,18 @@
         )
 
     return stream(ids, tgt.shape[0] - 1, FAR_BATCH, out, first, part)
+
+
+def centred(block, centre):
+    return augmented(coords(block, centre))
+
+
+def distances(source8, target8):
+    return jnp.dot(
+        source_rows(source8).T.astype(bf16),
+        target_rows(target8).astype(bf16),
+        preferred_element_type=f32,
+    )
 
 
 def inner_kernel(
@@ -358,10 +392,36 @@
 
 
 def outer_kernel(
-    near_ids, far_ids, origin, left, right, tgt, tgt_far,
-    near_out, far_out,
-    src, xw, src_lo, src_hi, qw, near_dist, far_dist,
+    near_ids, far_ids, box_far, origin, left, right, tgt, tgt_far, q1, box_skel3,
+    near_out, far_out, z1,
+    src, xw, src_lo, src_hi, qw, near_dist, far_dist, box_skel,
 ):
+    boxes, box_width = q1.shape[0], box_far.shape[0]
+    device = lax.axis_index("group") * lax.axis_size("sub") + lax.axis_index("sub")
+    box_skel[...] = jnp.zeros_like(box_skel)
+    for b in range(boxes):
+        for c in range(3):
+            box_skel[b, c : c + 1, :] = box_skel3[c, b : b + 1, :]
+
+    def box_level(b):
+        mine = box_skel[b]
+        centre = mine[:, 0:1]
+        blocks, weights = [], []
+        for j in range(box_width):
+            entry = box_far[j, b]
+            m = jnp.maximum(entry - device * boxes, 0)
+            blocks.append(box_skel[m])
+            weights.append(jnp.where(entry >= 0, q1[m], 0.0))
+        source = centred(jnp.concatenate(blocks, axis=1), centre)[0]
+        k = distances(source, centred(mine, centre)[1])
+        z1[b] = weigh(jnp.concatenate(weights, axis=1), profile(k))
+
+    def two_levels(g, c):
+        box_level(2 * g)
+        box_level(2 * g + 1)
+        return c
+
+    lax.fori_loop(0, boxes // 2, two_levels, 0)
     first = origin[:, 0:1]
     centre_sk = jnp.concatenate([first[3:8], first[0:3]], axis=0)
     sources = (src, xw, src_lo, src_hi, qw)
@@ -381,53 +441,36 @@
     )
 
 
-def centred(block, centre):
-    return augmented(coords(block, centre))
-
-
 def finish_kernel(
-    morton, box_far, sub_far, near_own, far_own, near, far,
-    q1, family, tops, box_skel3, group_skel3, basis_hbm, leaf_hbm, box_hbm, sub_hbm,
+    morton, sub_far, near_own, far_own, near, far,
+    z1, gathered, group_skel3, basis_hbm, leaf_hbm, box_hbm, sub_hbm,
     out,
-    box_skel, group_skel, rows, pad, tall, tall_too, l1s, basis, leaf_tr, box_tr, sub_tr, sems,
-    *, groups, box_width, sub_width, near_factor, f0, f1, f2, f3,
+    group_skel, rows, pad, tall, tall_too, l1s, basis, leaf_tr, box_tr, sub_tr, sems,
+    *, groups, sub_width, near_factor, f0, f1, f2, f3,
 ):
     copies = fetch(
         ((basis_hbm, basis), (leaf_hbm, leaf_tr), (box_hbm, box_tr), (sub_hbm, sub_tr)), sems
     )
-    boxes = q1.shape[0]
+    boxes = z1.shape[0]
     leaves = near.shape[0] - 1
     group = lax.axis_index("group")
-    sub = lax.axis_index("sub")
     subs = lax.axis_size("sub")
-    device = group * subs + sub
-    for ref, ref3 in ((box_skel, box_skel3), (group_skel, group_skel3)):
-        ref[...] = jnp.zeros_like(ref)
-        for b in range(ref.shape[0]):
-            for c in range(3):
-                ref[b, c : c + 1, :] = ref3[c, b : b + 1, :]
-    for copy in copies:
-        copy.wait()
-
-    def tile(source8, target8):
-        return profile(
-            jnp.dot(
-                source_rows(source8).T.astype(bf16),
-                target_rows(target8).astype(bf16),
-                preferred_element_type=f32,
-            )
-        )
-
-    own = family[sub, 64:72, :]
+    device = group * subs + lax.axis_index("sub")
+    group_skel[...] = jnp.zeros_like(group_skel)
+    for b in range(groups):
+        for c in range(3):
+            group_skel[b, c : c + 1, :] = group_skel3[c, b : b + 1, :]
+
+    own = gathered[device, 64:72, :]
     centre = own[:, 0:1]
     target = centred(own, centre)[1]
 
     def sub_term(j, acc):
         entry = sub_far[j]
-        m = jnp.maximum(entry - group * subs, 0)
-        source = centred(family[m, 64:72, :], centre)[0]
-        term = hdot(family[m, 0:32, :], tile(source, target))
-        return acc + jnp.where(entry >= 0, term, 0.0)
+        m = jnp.maximum(entry, 0)
+        source = centred(gathered[m, 64:72, :], centre)[0]
+        q2 = jnp.where(entry >= 0, gathered[m, 0:32, :], 0.0)
+        return acc + weigh(q2, profile(distances(source, target)))
 
     many = 4 if sub_width % 4 == 0 else 1
 
@@ -436,43 +479,28 @@
             acc = sub_term(g * many + j, acc)
         return acc
 
-    z2 = lax.fori_loop(0, sub_width // many, sub_terms, jnp.zeros((32, family.shape[2]), f32))
+    none = jnp.zeros((32, gathered.shape[2]), f32)
+    z2 = lax.fori_loop(0, sub_width // many, sub_terms, none)
     g_own = group_skel[group]
     g_centre = g_own[:, 0:1]
     g_target = centred(g_own, g_centre)[1]
-
-    def group_term(h, acc):
+    z3 = none
+    for step in range(1, groups):
+        h = lax.rem(group + step, groups)
+
+        def eight(s, t):
+            for k in range(8):
+                t = t + gathered[h * subs + s * 8 + k, 32:64, :]
+            return t
+
+        q3 = lax.fori_loop(0, subs // 8, eight, none)
         source = centred(group_skel[h], g_centre)[0]
-        return acc + jnp.where(h != group, hdot(tops[h], tile(source, g_target)), 0.0)
-
-    z3 = jnp.zeros(z2.shape, f32)
-    for h in range(groups):
-        z3 = group_term(h, z3)
+        z3 = z3 + weigh(q3, profile(distances(source, g_target)))
+    for copy in copies:
+        copy.wait()
     l2 = z2 * f2 + hdot_nt(z3 * f3, sub_tr[0])
-
-    def box_level(b, c):
-        mine = box_skel[b]
-        b_centre = mine[:, 0:1]
-        b_target = centred(mine, b_centre)[1]
-
-        def box_term(j, acc):
-            entry = box_far[j, b]
-            m = jnp.maximum(entry - device * boxes, 0)
-            source = centred(box_skel[m], b_centre)[0]
-            return acc + jnp.where(entry >= 0, hdot(q1[m], tile(source, b_target)), 0.0)
-
-        z1 = jnp.zeros((32, P_SIZE), f32)
-        for j in range(box_width):
-            z1 = box_term(j, z1)
-        l1s[b] = z1 * f1 + hdot_nt(l2, box_tr[b])
-        return c
-
-    def box_pair(g, c):
-        for j in range(2):
-            box_level(2 * g + j, c)
-        return c
-
-    lax.fori_loop(0, boxes // 2, box_pair, 0)
+    for b in range(boxes):
+        l1s[b] = z1[b] * f1 + hdot_nt(l2, box_tr[b])
 
     def down(b, into):
         l1 = l1s[b]
@@ -565,7 +593,7 @@
     ends = subs * groups - 1
     left = lax.ppermute(geo_hi, both, [(i, i + 1) for i in range(ends)])
     right = lax.ppermute(geo_lo, both, [(i + 1, i) for i in range(ends)])
-    family = lax.all_gather(packed, "sub", axis=0)
+    gathered = lax.all_gather(packed, both, axis=0)
 
     acc_shapes = ((leaves + 1, nv, P_SIZE), (leaves + 1, r0, P_SIZE))
     tables = [
@@ -593,23 +621,26 @@
         name="inner",
     )(near_ids.reshape(-1), far_ids.reshape(-1), geo_lo, geo_hi)
 
-    tops = lax.all_gather(jnp.sum(family[:, nv : 2 * nv, :], axis=0), "group", axis=0)
-    near_halo, far_halo = pl.pallas_call(
+    near_halo, far_halo, z1 = pl.pallas_call(
         outer_kernel,
-        out_shape=tuple(jax.ShapeDtypeStruct(a, f32) for a in acc_shapes),
-        in_specs=[SMEM] * 2 + [VMEM] * 5,
-        out_specs=(VMEM,) * 2,
-        scratch_shapes=tables,
+        out_shape=tuple(
+            jax.ShapeDtypeStruct(a, f32) for a in acc_shapes + ((boxes, nv, r1),)
+        ),
+        in_specs=[SMEM] * 3 + [VMEM] * 7,
+        out_specs=(VMEM,) * 3,
+        scratch_shapes=tables + [pltpu.VMEM((boxes, 8, r1), f32)],
         compiler_params=params,
         cost_estimate=pl.CostEstimate(flops=10**10, bytes_accessed=10**7, transcendentals=3 * 10**7),
         name="outer",
-    )(near_ids_out.reshape(-1), far_ids_out.reshape(-1), origin, left, right, tgt, tgt_far)
+    )(
+        near_ids_out.reshape(-1), far_ids_out.reshape(-1), box_far.T,
+        origin, left, right, tgt, tgt_far, q1, front(box_skeleton),
+    )
 
     return pl.pallas_call(
         functools.partial(
             finish_kernel,
             groups=groups,
-            box_width=box_far.shape[1],
             sub_width=subtree_far.shape[1],
             near_factor=(P_SIZE * near_list.shape[1]) ** -0.5,
             f0=(r0 * leaf_far.shape[1]) ** -0.5,
@@ -618,10 +649,9 @@
             f3=r3**-0.5,
         ),
         out_shape=jax.ShapeDtypeStruct((nv, count), f32),
-        in_specs=[SMEM] * 3 + [VMEM] * 9 + [ANY] * 4,
+        in_specs=[SMEM] * 2 + [VMEM] * 7 + [ANY] * 4,
         out_specs=VMEM,
         scratch_shapes=[
-            pltpu.VMEM((boxes, 8, r1), f32),
             pltpu.VMEM((groups, 8, r3), f32),
             pltpu.VMEM((count, P_SIZE), f32),
             pltpu.VMEM((CH, P_SIZE, P_SIZE), f32),
@@ -634,8 +664,8 @@
         compiler_params=params,
         name="finish",
     )(
-        morton, box_far.T, subtree_far.reshape(-1), near, far, near_halo, far_halo,
-        q1, family, tops, front(box_skeleton), front(group_skeleton), *bases,
+        morton, subtree_far.reshape(-1), near, far, near_halo, far_halo,
+        z1, gathered, front(group_skeleton), *bases,
     )
 
 

time: 157 us -> 132 us (0.84)
  blocking collectives: 24.6 us -> 0 us
  Pallas kernels: 122 us -> 108 us
  between operations: 0.23 us -> 13.5 us
    all_gather x2 -> x0, blocking collectives: 24.6 us -> none  [the longest x1 15.2 us: body(): family = lax.all_gather(packed, 'sub', axis=0)]
    pallas_call x1, Pallas kernels: 35.8 us -> 23.6 us  [body(): pl.pallas_call(functools.partial(finish_kernel, groups=groups, sub_width=...]
    pallas_call x1, Pallas kernels: 18.7 us -> 14.2 us  [body(): pl.pallas_call(arrange_kernel, out_shape=(jax.ShapeDtypeStruct((leaves //...]
    pallas_call x1, Pallas kernels: 22.4 us -> 25.2 us  [body(): pl.pallas_call(outer_kernel, out_shape=tuple((jax.ShapeDtypeStruct(a, f32...]
  transfers between devices with their start and end apart: 2 -> 3, of which waited for: 0 -> 0; matrix products, arithmetic and copies ran while one was open for 0% -> 0% of each run, Pallas kernels for 29% -> 53%
where the time goes in v4:
time: 132 us
  Pallas kernels  108 us (82%)
  between operations  13.5 us (10%)
  starting transfers between devices  9.16 us (7%)
    pallas_call x1, Pallas kernels, body(): pl.pallas_call(inner_kernel, out_shape=tuple((jax.ShapeDtypeStruct(a, f32...  45.3 us
    pallas_call x1, Pallas kernels, body(): pl.pallas_call(outer_kernel, out_shape=tuple((jax.ShapeDtypeStruct(a, f32...  25.2 us
    pallas_call x1, Pallas kernels, body(): pl.pallas_call(functools.partial(finish_kernel, groups=groups, sub_width=...  23.6 us
    pallas_call x1, Pallas kernels, body(): pl.pallas_call(arrange_kernel, out_shape=(jax.ShapeDtypeStruct((leaves //...  14.2 us
    ppermute x1, starting transfers between devices, body(): right = lax.ppermute(geo_lo, both, [(i + 1, i) for i in range(ends)])  7.24 us
  transfers between devices with their start and end apart: 3, of which 0 were waited for; matrix products, arithmetic and copies ran while one was open for 0% of the time, Pallas kernels for 53%

profile of v4, /device:TPU:4, one launch (start us, length us, event | category | flops | bytes accessed | tf_op | source)
XLA Modules:
  0.0 132.1 jit_solution(8444784243134713051)
XLA Ops:
  6.5 0.0 all-gather.3.cloned.1.call-start
  6.5 14.2 %arrange.1 = (f32[32,56,128]{2,1,0:T(8,128)}, f32[32,56,128]{2,1,0:T(8,128)}, s32[8,128]{1,0:T(8,128)}, s32[8,128]{1,0:T(8,128)}, s32[8,128]{1,0:T(8,128)}, /*in...) custom-call(s32[8192]{0:T(1024)} %morton.3, s32[27,64]{1,0:T(8,128)} %bitcast.15, s32[24,64]{1,0:T(8,128)} %bitcast.16, ...), custom_call_target="tpu_custom_call" | custom-call | tf_op jit(solution)/shard_map/arrange/pallas_call | solution.py:566
  20.8 0.0 all-gather.3.cloned.1.call-update
  20.8 1.9 %collective-permute-start = (f32[32,56,128]{2,1,0:T(8,128)}, f32[32,56,128]{2,1,0:T(8,128)S(1)}, u32[]{:S(2)}, u32[]{:S(2)}) collective-permute-start(f32[32,56,128]{2,1,0:T(8,128)} %get-tuple-element.24.geo_hi), channel_id=1, source_target_pairs={{0,1},{1,2},{2,3},{3,4},{4,5},{5,6},{6,7},{7,8},{8,9},{9,10},{10,1... | collective-permute-start | bytes 2752520 | tf_op jit(solution)/shard_map/ppermute | solution.py:594
  22.7 7.2 %collective-permute-start.1 = (f32[32,56,128]{2,1,0:T(8,128)}, f32[32,56,128]{2,1,0:T(8,128)S(1)}, u32[]{:S(2)}, u32[]{:S(2)}) collective-permute-start(f32[32,56,128]{2,1,0:T(8,128)} %get-tuple-element.23.geo_lo), channel_id=1, source_target_pairs={{1,0},{2,1},{3,2},{4,3},{5,4},{6,5},{7,6},{8,7},{9,8},{10,9},{11,1... | collective-permute-start | bytes 2752520 | tf_op jit(solution)/shard_map/ppermute | solution.py:595
  30.0 45.3 %inner.1 = (f32[65,32,128]{2,1,0:T(8,128)}, f32[65,64,128]{2,1,0:T(8,128)}, bf16[65,64,128]{2,1,0:T(8,128)(2,1)}, bf16[65,64,128]{2,1,0:T(8,128)(2,1)}, f32[8,128]{1,0:T(8,128)}) custom-call(s32[1024]{0:T(1024)} %bitcast.23, s32[1024]{0:T(1024)} %bitcast.24, f32[32,56,128]{2,1,0:T(8,128)} %get-tuple-element.23.geo_lo, f32[32,56,128]{2,1,0:T(8,128)} %get-tuple-element.24.geo_hi), custom_call_target="tpu_custom_call" | custom-call | flops 20000000000 | bytes 10000000 | tf_op jit(solution)/shard_map/inner/pallas_call | solution.py:608
  75.3 0.0 collective-permute-done.left
  75.3 0.0 copy-start
  75.3 0.0 collective-permute-done.1.right
  75.3 0.0 copy-start.1
  75.3 0.9 copy-done
  76.3 0.3 copy-done.1
  76.5 25.2 %outer.1 = (f32[65,32,128]{2,1,0:T(8,128)}, f32[65,64,128]{2,1,0:T(8,128)}, f32[8,32,128]{2,1,0:T(8,128)}) custom-call(s32[1024]{0:T(1024)} %bitcast.21, s32[1024]{0:T(1024)} %bitcast.22, s32[4,8]{1,0:T(4,128)} %bitcast.25, f32[8,128]{1,0:T(8,128)} %get-tuple-element.29.origin, f32[32,56,128]{2,1,0:T(8,128)} %copy-done, f32[32,56,128]{2,1,0:T(8,128)} %copy-done.1, ...), custom_call_target="tpu_custom_call" | custom-call | flops 10000000000 | bytes 10000000 | tf_op jit(solution)/shard_map/outer/pallas_call | solution.py:624
  101.7 0.0 all-gather.3.cloned.1.call-done
  101.7 23.6 %finish.1 = f32[32,8192]{1,0:T(8,128)} custom-call(s32[8192]{0:T(1024)} %morton.3, s32[4]{0:T(128)} %bitcast.19, f32[65,32,128]{2,1,0:T(8,128)} %get-tuple-element.25.near_own, f32[65,64,128]{2,1,0:T(8,128)} %get-tuple-element.26.far_own, f32[65,32,128]{2,1,0:T(8,128)} %get-tuple-element.33.near, f32[65,64,128]{2,1,0:T(8,128)} %get-tuple-element.34.far, ...), custom_call_target="tpu_custom_call" | custom-call | tf_op jit(solution)/shard_map/finish/pallas_call | solution.py:640
Async XLA Ops:
  6.5 95.2 %all-gather.3.cloned.1.call-start = ((), (), s32[]{:S(2)}) async-start(), calls=%async_computation | async-start | bytes 2433024 | tf_op jit(solution)/shard_map/all_gather | solution.py:596
  20.8 54.5 %collective-permute-start = (f32[32,56,128]{2,1,0:T(8,128)}, f32[32,56,128]{2,1,0:T(8,128)S(1)}, u32[]{:S(2)}, u32[]{:S(2)}) collective-permute-start(f32[32,56,128]{2,1,0:T(8,128)} %get-tuple-element.24.geo_hi), channel_id=1, source_target_pairs={{0,1},{1,2},{2,3},{3,4},{4,5},{5,6},{6,7},{7,8},{8,9},{9,10},{10,1... | collective-permute-start | bytes 2752520 | tf_op jit(solution)/shard_map/ppermute | solution.py:594
  22.7 52.6 %collective-permute-start.1 = (f32[32,56,128]{2,1,0:T(8,128)}, f32[32,56,128]{2,1,0:T(8,128)S(1)}, u32[]{:S(2)}, u32[]{:S(2)}) collective-permute-start(f32[32,56,128]{2,1,0:T(8,128)} %get-tuple-element.23.geo_lo), channel_id=1, source_target_pairs={{1,0},{2,1},{3,2},{4,3},{5,4},{6,5},{7,6},{8,7},{9,8},{10,9},{11,1... | collective-permute-start | bytes 2752520 | tf_op jit(solution)/shard_map/ppermute | solution.py:595
  75.3 0.9 copy-start
  75.3 1.2 copy-start.1
Sparse Core Ops, SparseCore 0:
  20.9 64.7 all-gather.2

commit v5 on v4

--- a/solution.py
+++ b/solution.py
@@ -542,7 +542,7 @@
 VMEM = pl.BlockSpec(memory_space=pltpu.VMEM)
 SMEM = pl.BlockSpec(memory_space=pltpu.SMEM)
 ANY = pl.BlockSpec(memory_space=pl.ANY)
-params = pltpu.CompilerParams(vmem_limit_bytes=56 * 2**20)
+params = pltpu.CompilerParams(vmem_limit_bytes=36 * 2**20)
 
 
 def body(

time: 132 us -> 151 us (1.14); the launches traced: 132 us -> 148 us
  local copies, waits for them, and re-layouts: 1.2 us -> 27.6 us
  Pallas kernels: 108 us -> 97.8 us
    unnamed x4 -> x70, local copies, waits for them, and re-layouts: 1.2 us -> 27.6 us
    pallas_call x1, Pallas kernels: 25.2 us -> 20.8 us  [body(): pl.pallas_call(outer_kernel, out_shape=tuple((jax.ShapeDtypeStruct(a, f32...]
    pallas_call x1, Pallas kernels: 23.6 us -> 20 us  [body(): pl.pallas_call(functools.partial(finish_kernel, groups=groups, sub_width=...]
    pallas_call x1, Pallas kernels: 45.3 us -> 42.6 us  [body(): pl.pallas_call(inner_kernel, out_shape=tuple((jax.ShapeDtypeStruct(a, f32...]
  transfers between devices with their start and end apart: 3 -> 3, of which waited for: 0 -> 0; matrix products, arithmetic and copies ran while one was open for 0% -> 0% of each run, Pallas kernels for 53% -> 43%
where the time goes in v5:
time: 151 us; the launch traced here: 148 us
  Pallas kernels  97.8 us (65%)
  local copies, waits for them, and re-layouts  27.6 us (18%)
  between operations  13.6 us (9%)
  starting transfers between devices  9.16 us (6%)
    pallas_call x1, Pallas kernels, body(): pl.pallas_call(inner_kernel, out_shape=tuple((jax.ShapeDtypeStruct(a, f32...  42.6 us
    unnamed x70, local copies, waits for them, and re-layouts  27.6 us
    pallas_call x1, Pallas kernels, body(): pl.pallas_call(outer_kernel, out_shape=tuple((jax.ShapeDtypeStruct(a, f32...  20.8 us
    pallas_call x1, Pallas kernels, body(): pl.pallas_call(functools.partial(finish_kernel, groups=groups, sub_width=...  20 us
    pallas_call x1, Pallas kernels, body(): pl.pallas_call(arrange_kernel, out_shape=(jax.ShapeDtypeStruct((leaves //...  14.3 us
    ppermute x1, starting transfers between devices, body(): right = lax.ppermute(geo_lo, both, [(i + 1, i) for i in range(ends)])  7.24 us
  transfers between devices with their start and end apart: 3, of which 0 were waited for; matrix products, arithmetic and copies ran while one was open for 0% of the time, Pallas kernels for 43%

profile of v5, /device:TPU:4, one launch (start us, length us, event | category | flops | bytes accessed | tf_op | source)
XLA Modules:
  0.0 148.2 jit_solution(13063894880959730867)
XLA Ops:
  6.5 0.0 all-gather.3.cloned.1.call-start
  6.5 0.0 copy-start
  6.5 1.6 %copy-done = f32[64,64,128]{2,1,0:T(8,128)S(1)} copy-done((f32[64,64,128]{2,1,0:T(8,128)S(1)}, f32[64,64,128]{2,1,0:T(8,128)}, u32[]{:S(2)}) %copy-start) | copy-done | bytes 2097176
  8.1 0.0 copy-start.2
  8.1 1.6 %copy-done.2 = f32[64,64,128]{2,1,0:T(8,128)S(1)} copy-done((f32[64,64,128]{2,1,0:T(8,128)S(1)}, f32[64,64,128]{2,1,0:T(8,128)}, u32[]{:S(2)}) %copy-start.2) | copy-done | bytes 2097176
  9.7 0.0 copy-start.4
  9.7 1.2 copy-done.4
  10.9 0.0 copy-start.15
  10.9 0.9 copy-done.15
  11.9 0.0 copy-start.17
  11.9 1.2 copy-done.17
  13.1 0.8 copy-done.18
  13.9 0.9 copy-done.20
  14.8 0.9 copy-done.21
  15.7 0.7 copy-done.22
  16.4 0.7 copy-done.23
  17.1 0.7 copy-done.25
  17.8 14.3 %arrange.1 = (f32[32,56,128]{2,1,0:T(8,128)S(1)}, f32[32,56,128]{2,1,0:T(8,128)S(1)}, s32[8,128]{1,0:T(8,128)S(1)}, s32[8,128]{1,0:T(8,128)S(1)}, s32[8,128]{1,0...) custom-call(s32[8192]{0:T(1024)S(1)} %copy-done.18, s32[27,64]{1,0:T(8,128)S(1)} %bitcast.15, ...), custom_call_target="tpu_custom_call" | custom-call | tf_op jit(solution)/shard_map/arrange/pallas_call | solution.py:566
  32.1 0.0 copy-start.27
  32.1 0.6 copy-done.27
  32.8 0.6 copy-done.30
  33.4 0.6 copy-done.32
  34.0 0.0 all-gather.3.cloned.1.call-update
  34.0 1.9 %collective-permute-start = (f32[32,56,128]{2,1,0:T(8,128)S(1)}, f32[32,56,128]{2,1,0:T(8,128)S(1)}, u32[]{:S(2)}, u32[]{:S(2)}) collective-permute-start(f32[32,56,128]{2,1,0:T(8,128)S(1)} %get-tuple-element.24.geo_hi), channel_id=1, source_target_pairs={{0,1},{1,2},{2,3},{3,4},{4,5},{5,6},{6,7},{7,8},{8,9},{9,10},{10,1... | collective-permute-start | bytes 2752520 | tf_op jit(solution)/shard_map/ppermute | solution.py:594
  35.9 7.2 %collective-permute-start.1 = (f32[32,56,128]{2,1,0:T(8,128)S(1)}, f32[32,56,128]{2,1,0:T(8,128)S(1)}, u32[]{:S(2)}, u32[]{:S(2)}) collective-permute-start(f32[32,56,128]{2,1,0:T(8,128)S(1)} %get-tuple-element.23.geo_lo), channel_id=1, source_target_pairs={{1,0},{2,1},{3,2},{4,3},{5,4},{6,5},{7,6},{8,7},{9,8},{10,9},{11,1... | collective-permute-start | bytes 2752520 | tf_op jit(solution)/shard_map/ppermute | solution.py:595
  43.2 0.0 copy-start.28
  43.2 0.0 copy-start.29
  43.2 0.0 copy-start.31
  43.2 0.0 copy-start.33
  43.2 0.0 copy-start.34
  43.2 42.6 %inner.1 = (f32[65,32,128]{2,1,0:T(8,128)S(1)}, f32[65,64,128]{2,1,0:T(8,128)S(1)}, bf16[65,64,128]{2,1,0:T(8,128)(2,1)S(1)}, bf16[65,64,128]{2,1,0:T(8,128)(2,1)S(1)}, f32[8,128]{1,0:T(8,128)S(1)}) custom-call(s32[1024]{0:T(1024)S(1)} %bitcast.23, s32[1024]{0:T(1024)S(1)} %bitcast.24, f32[32,56,128]{2,1,0:T(8,128)S(1)} %get-tuple-element.23.geo_lo, ...), custom_call_target="tpu_custom_call" | custom-call | flops 20000000000 | bytes 10000000 | tf_op jit(solution)/shard_map/inner/pallas_call | solution.py:608
  85.8 0.0 copy-start.7
  85.8 1.4 copy-done.7
  87.2 1.0 copy-done.11
  88.2 0.0 collective-permute-done.left
  88.2 0.0 collective-permute-done.1.right
  88.2 0.0 copy-done.28
  88.2 0.0 copy-done.29
  88.2 0.0 copy-done.31
  88.2 0.0 copy-done.33
  88.2 0.0 copy-done.34
  88.2 0.0 copy-start.1
  88.3 0.0 copy-start.5
  88.3 0.0 copy-start.16
  88.3 0.0 copy-start.24
  88.3 0.0 copy-start.26
  88.3 20.8 %outer.1 = (f32[65,32,128]{2,1,0:T(8,128)S(1)}, f32[65,64,128]{2,1,0:T(8,128)S(1)}, f32[8,32,128]{2,1,0:T(8,128)S(1)}) custom-call(s32[1024]{0:T(1024)S(1)} %bitcast.21, s32[1024]{0:T(1024)S(1)} %bitcast.22, s32[4,8]{1,0:T(4,128)S(1)} %bitcast.25, f32[8,128]{1,0:T(8,128)S(1)} %get-tuple-element.29.origin, f32[32,56,128]{2,1,0:T(8,128)S(1)} %collective-permute-done.left, ...), custom_call_target="tpu_custom_call" | custom-call | flops 10000000000 | bytes 10000000 | tf_op jit(solution)/shard_map/outer/pallas_call | solution.py:624
  109.1 0.0 copy-start.9
  109.1 1.4 copy-done.9
  110.5 1.1 copy-done.13
  111.6 0.0 copy-done.1
  111.6 0.0 copy-done.5
  111.6 0.0 copy-done.16
  111.6 0.0 copy-done.24
  111.6 0.0 copy-done.26
  111.6 0.0 copy-start.3
  111.6 1.6 %copy-done.3 = f32[64,64,128]{2,1,0:T(8,128)S(1)} copy-done((f32[64,64,128]{2,1,0:T(8,128)S(1)}, f32[64,64,128]{2,1,0:T(8,128)}, u32[]{:S(2)}) %copy-start.3) | copy-done | bytes 2097176
  113.2 1.7 %copy-done.6 = f32[2304,256]{1,0:T(8,128)S(1)} copy-done((f32[2304,256]{1,0:T(8,128)S(1)}, f32[2304,256]{1,0:T(8,128)}, u32[]{:S(2)}) %copy-start.6) | copy-done | bytes 2359320
  114.8 1.6 %copy-done.8 = f32[65,64,128]{2,1,0:T(8,128)S(1)} copy-done((f32[65,64,128]{2,1,0:T(8,128)S(1)}, f32[65,64,128]{2,1,0:T(8,128)}, u32[]{:S(2)}) %copy-start.8) | copy-done | bytes 2129944
  116.4 1.6 %copy-done.10 = f32[65,64,128]{2,1,0:T(8,128)S(1)} copy-done((f32[65,64,128]{2,1,0:T(8,128)S(1)}, f32[65,64,128]{2,1,0:T(8,128)}, u32[]{:S(2)}) %copy-start.10) | copy-done | bytes 2129944
  118.0 1.2 copy-done.12
  119.3 1.2 copy-done.14
  120.5 0.8 copy-done.19
  121.3 20.0 %finish.1 = f32[32,8192]{1,0:T(8,128)} custom-call(s32[8192]{0:T(1024)S(1)} %copy-done.19, s32[4]{0:T(128)S(1)} %bitcast.19, f32[65,32,128]{2,1,0:T(8,128)S(1)} %copy-done.12, f32[65,64,128]{2,1,0:T(8,128)S(1)} %copy-done.8, f32[65,32,128]{2,1,0:T(8,128)S(1)} %copy-done.14, f32[65,64,128]{2,1,0:T(8,128)S(1)} %copy-done.10, ...), custom_call_target="tpu_custom_call" | custom-call | tf_op jit(solution)/shard_map/finish/pallas_call | solution.py:640
  (17 shorter events, 0.0 us)
Async XLA Ops:
  6.5 105.0 %all-gather.3.cloned.1.call-start = ((), (), s32[]{:S(2)}) async-start(), calls=%async_computation | async-start | bytes 2433024 | tf_op jit(solution)/shard_map/all_gather | solution.py:596
  6.5 1.6 %copy-start = (f32[64,64,128]{2,1,0:T(8,128)S(1)}, f32[64,64,128]{2,1,0:T(8,128)}, u32[]{:S(2)}) copy-start(f32[64,64,128]{2,1,0:T(8,128)} %basis_hbm.3) | copy-start | bytes 6291460
  8.1 1.6 %copy-start.2 = (f32[64,64,128]{2,1,0:T(8,128)S(1)}, f32[64,64,128]{2,1,0:T(8,128)}, u32[]{:S(2)}) copy-start(f32[64,64,128]{2,1,0:T(8,128)} %leaf_hbm.3) | copy-start | bytes 6291460
  9.7 1.2 copy-start.4
  10.9 0.9 copy-start.15
  11.9 1.2 copy-start.17
  13.1 0.8 copy-start.18
  13.9 0.9 copy-start.20
  14.8 0.9 copy-start.21
  15.7 0.7 copy-start.22
  16.4 0.7 copy-start.23
  17.1 0.7 copy-start.25
  32.1 0.7 copy-start.27
  32.8 0.6 copy-start.30
  33.4 0.6 copy-start.32
  34.0 54.2 %collective-permute-start = (f32[32,56,128]{2,1,0:T(8,128)S(1)}, f32[32,56,128]{2,1,0:T(8,128)S(1)}, u32[]{:S(2)}, u32[]{:S(2)}) collective-permute-start(f32[32,56,128]{2,1,0:T(8,128)S(1)} %get-tuple-element.24.geo_hi), channel_id=1, source_target_pairs={{0,1},{1,2},{2,3},{3,4},{4,5},{5,6},{6,7},{7,8},{8,9},{9,10},{10,1... | collective-permute-start | bytes 2752520 | tf_op jit(solution)/shard_map/ppermute | solution.py:594
  35.9 52.3 %collective-permute-start.1 = (f32[32,56,128]{2,1,0:T(8,128)S(1)}, f32[32,56,128]{2,1,0:T(8,128)S(1)}, u32[]{:S(2)}, u32[]{:S(2)}) collective-permute-start(f32[32,56,128]{2,1,0:T(8,128)S(1)} %get-tuple-element.23.geo_lo), channel_id=1, source_target_pairs={{1,0},{2,1},{3,2},{4,3},{5,4},{6,5},{7,6},{8,7},{9,8},{10,9},{11,1... | collective-permute-start | bytes 2752520 | tf_op jit(solution)/shard_map/ppermute | solution.py:595
  43.2 45.0 %copy-start.28 = (f32[8,32,128]{2,1,0:T(8,128)S(1)}, f32[8,32,128]{2,1,0:T(8,128)}, u32[]{:S(2)}) copy-start(f32[8,32,128]{2,1,0:T(8,128)} %copy-done.27) | copy-start | bytes 393220
  43.2 45.0 %copy-start.29 = (f32[8,3,128]{2,0,1:T(8,128)S(1)}, f32[8,3,128]{2,0,1:T(8,128)}, u32[]{:S(2)}) copy-start(f32[8,3,128]{2,0,1:T(8,128)} %param.23) | copy-start | bytes 36868
  43.2 45.0 %copy-start.31 = (s32[8,128]{1,0:T(8,128)S(1)}, s32[8,128]{1,0:T(8,128)}, u32[]{:S(2)}) copy-start(s32[8,128]{1,0:T(8,128)} %copy-done.30) | copy-start | bytes 12292
  43.2 45.0 %copy-start.33 = (s32[8,128]{1,0:T(8,128)S(1)}, s32[8,128]{1,0:T(8,128)}, u32[]{:S(2)}) copy-start(s32[8,128]{1,0:T(8,128)} %copy-done.32) | copy-start | bytes 12292
  43.2 45.0 %copy-start.34 = (s32[8,4]{0,1:T(4,128)S(1)}, s32[8,4]{0,1:T(4,128)}, u32[]{:S(2)}) copy-start(s32[8,4]{0,1:T(4,128)} %param.20) | copy-start | bytes 388
  85.8 1.4 copy-start.7
  87.2 1.0 copy-start.11
  88.2 23.3 %copy-start.1 = (f32[64,64,128]{2,1,0:T(8,128)S(1)}, f32[64,64,128]{2,1,0:T(8,128)}, u32[]{:S(2)}) copy-start(f32[64,64,128]{2,1,0:T(8,128)} %basis_hbm.3) | copy-start | bytes 6291460
  88.3 23.3 %copy-start.5 = (f32[8,128,256]{2,1,0:T(8,128)S(1)}, f32[8,128,256]{2,1,0:T(8,128)}, u32[]{:S(2)}) copy-start(f32[8,128,256]{2,1,0:T(8,128)} %box_hbm.3) | copy-start | bytes 3145732
  88.3 23.3 %copy-start.16 = (f32[1,256,256]{2,1,0:T(8,128)S(1)}, f32[1,256,256]{2,1,0:T(8,128)}, u32[]{:S(2)}) copy-start(f32[1,256,256]{2,1,0:T(8,128)} %sub_hbm.3) | copy-start | bytes 786436
  88.3 23.3 %copy-start.24 = (f32[4,3,256]{2,0,1:T(4,128)S(1)}, f32[4,3,256]{2,0,1:T(4,128)}, u32[]{:S(2)}) copy-start(f32[4,3,256]{2,0,1:T(4,128)} %param.25) | copy-start | bytes 36868
  88.3 23.3 %copy-start.26 = (s32[1,4]{1,0:T(1,128)S(1)}, s32[1,4]{1,0:T(1,128)}, u32[]{:S(2)}) copy-start(s32[1,4]{1,0:T(1,128)} %param.21) | copy-start | bytes 52
  109.1 1.4 copy-start.9
  110.5 1.1 copy-start.13
  111.6 1.6 %copy-start.3 = (f32[64,64,128]{2,1,0:T(8,128)S(1)}, f32[64,64,128]{2,1,0:T(8,128)}, u32[]{:S(2)}) copy-start(f32[64,64,128]{2,1,0:T(8,128)} %leaf_hbm.3) | copy-start | bytes 6291460
  113.2 1.7 %copy-start.6 = (f32[2304,256]{1,0:T(8,128)S(1)}, f32[2304,256]{1,0:T(8,128)}, u32[]{:S(2)}) copy-start(f32[2304,256]{1,0:T(8,128)} %all-gather.3.cloned.1.call-done) | copy-start | bytes 7077892
  114.8 1.6 %copy-start.8 = (f32[65,64,128]{2,1,0:T(8,128)S(1)}, f32[65,64,128]{2,1,0:T(8,128)}, u32[]{:S(2)}) copy-start(f32[65,64,128]{2,1,0:T(8,128)} %copy-done.7) | copy-start | bytes 6389764
  116.4 1.6 %copy-start.10 = (f32[65,64,128]{2,1,0:T(8,128)S(1)}, f32[65,64,128]{2,1,0:T(8,128)}, u32[]{:S(2)}) copy-start(f32[65,64,128]{2,1,0:T(8,128)} %copy-done.9) | copy-start | bytes 6389764
  118.0 1.2 copy-start.12
  119.3 1.2 copy-start.14
  120.5 0.8 copy-start.19
Sparse Core Ops, SparseCore 0:
  34.1 64.6 all-gather.2

commit v6 on v4

--- a/solution.py
+++ b/solution.py
@@ -203,21 +203,18 @@
     for copy in copies:
         copy.wait()
 
-    def gather(b, into):
-        for j in range(CH):
-            for k in range(P_SIZE):
-                into[j, k : k + 1, :] = rows[pl.ds(row_of(morton, b, j * P_SIZE + k), 1), :]
-
-    def combine(b, start, held, geo):
-        turned = [held[j].T for j in range(CH)]
+    def work(b, start, held, geo, new, into):
         parts = []
         for j in range(CH):
             i = b * CH + j
             at = i - start
-            geo[at, 0:40, :] = turned[j][0:40]
+            turned = held[j].T
+            for k in range(P_SIZE if into is not None else 0):
+                into[j, k : k + 1, :] = rows[pl.ds(row_of(morton, new, j * P_SIZE + k), 1), :]
+            geo[at, 0:40, :] = turned[0:40]
             for c in range(3):
                 geo[at, 35 + c : 36 + c, 0:64] = skel[c, pl.ds(i, 1), :]
-            q0 = hdot_nt(turned[j][0:32], basis[i])
+            q0 = hdot_nt(turned[0:32], basis[i])
             geo[at, 40:56, 0:64] = q0[0:16]
             geo[at, 40:56, 64:128] = q0[16:32]
             parts.append(q0)
@@ -229,13 +226,11 @@
         return hdot(q1, box_tr[b])
 
     def two_boxes(g, q2):
-        gather(g, got)
-        late = combine(middle + jnp.maximum(g - 1, 0), half, got_too, geo_hi)
-        gather(middle + g, got_too)
-        return q2 + jnp.where(g > 0, late, 0.0) + combine(g, 0, got, geo_lo)
+        late = work(middle + jnp.maximum(g - 1, 0), half, got_too, geo_hi, g, got)
+        return q2 + jnp.where(g > 0, late, 0.0) + work(g, 0, got, geo_lo, middle + g, got_too)
 
     q2 = lax.fori_loop(0, middle, two_boxes, jnp.zeros((32, packed.shape[1]), f32))
-    q2 = q2 + combine(2 * middle - 1, half, got_too, geo_hi)
+    q2 = q2 + work(2 * middle - 1, half, got_too, geo_hi, None, None)
     packed[0:32, :] = q2
     packed[32:64, :] = hdot(q2, sub_tr[0])
     packed[64:72, :] = jnp.zeros((8, packed.shape[1]), f32)
@@ -376,13 +371,13 @@
 
     def load(g, c):
         for geo, start in ((geo_lo, 0), (geo_hi, half)):
-            for j in range(4):
-                i = g * 4 + j
+            for j in range(8):
+                i = g * 8 + j
                 t8, kt8 = prepare_source(geo[i], i + start, first, centre_sk, *sources)
                 prepare_target(t8, kt8, i + start, tgt, tgt_far)
         return c
 
-    lax.fori_loop(0, half // 4, load, 0)
+    lax.fori_loop(0, half // 8, load, 0)
     clear(sources, NONE)
     clear((tgt, tgt_far), leaves)
     run(
@@ -428,12 +423,12 @@
 
     def load(g, c):
         for block, start in ((left, 0), (right, HALO)):
-            for j in range(4):
-                i = g * 4 + j
+            for j in range(8):
+                i = g * 8 + j
                 prepare_source(block[i], i + start, first, centre_sk, *sources)
         return c
 
-    lax.fori_loop(0, HALO // 4, load, 0)
+    lax.fori_loop(0, HALO // 8, load, 0)
     clear(sources, NONE)
     run(
         near_pass(near_ids, src, tgt, xw, near_out, near_dist),
@@ -442,15 +437,14 @@
 
 
 def finish_kernel(
-    morton, sub_far, near_own, far_own, near, far,
-    z1, gathered, group_skel3, basis_hbm, leaf_hbm, box_hbm, sub_hbm,
-    out,
-    group_skel, rows, pad, tall, tall_too, l1s, basis, leaf_tr, box_tr, sub_tr, sems,
-    *, groups, sub_width, near_factor, f0, f1, f2, f3,
+    morton, sub_far, z1, gathered, group_skel3, *rest,
+    groups, sub_width, near_factor, f0, f1, f2, f3,
 ):
-    copies = fetch(
-        ((basis_hbm, basis), (leaf_hbm, leaf_tr), (box_hbm, box_tr), (sub_hbm, sub_tr)), sems
-    )
+    fetched = rest[:8]
+    out, group_skel, rows, pad, tall, tall_too, l1s = rest[8:15]
+    held, sems = rest[15:23], rest[23]
+    near_own, far_own, near, far, basis, leaf_tr, box_tr, sub_tr = held
+    copies = fetch(tuple(zip(fetched, held))[::-1], sems)
     boxes = z1.shape[0]
     leaves = near.shape[0] - 1
     group = lax.axis_index("group")
@@ -502,14 +496,15 @@
     for b in range(boxes):
         l1s[b] = z1[b] * f1 + hdot_nt(l2, box_tr[b])
 
-    def down(b, into):
+    def work(b, into, old, held):
         l1 = l1s[b]
         for j in range(CH):
+            for k in range(P_SIZE):
+                rows[pl.ds(row_of(morton, old, j * P_SIZE + k), 1), :] = held[j, k : k + 1, :]
             i = b * CH + j
             turned = (far_own[i] + far[i]).T
             l0 = (turned[0:32] + turned[32:64]) * f0 + hdot_nt(l1, leaf_tr[i])
             pad[j, 0:32, :] = (near_own[i] + near[i]) * near_factor + hdot(l0, basis[i])
-        for j in range(CH):
             into[j] = pad[j].T
 
     def scatter(b, held):
@@ -521,10 +516,8 @@
     tall_too[...] = jnp.zeros_like(tall_too)
 
     def two_boxes(g, c):
-        scatter(jnp.maximum(2 * g - 1, 1), tall_too)
-        down(2 * g, tall)
-        scatter(2 * g, tall)
-        down(2 * g + 1, tall_too)
+        work(2 * g, tall, jnp.maximum(2 * g - 1, 1), tall_too)
+        work(2 * g + 1, tall_too, 2 * g, tall)
         return c
 
     lax.fori_loop(0, boxes // 2, two_boxes, 0)
@@ -649,7 +642,7 @@
             f3=r3**-0.5,
         ),
         out_shape=jax.ShapeDtypeStruct((nv, count), f32),
-        in_specs=[SMEM] * 2 + [VMEM] * 7 + [ANY] * 4,
+        in_specs=[SMEM] * 2 + [VMEM] * 3 + [ANY] * 8,
         out_specs=VMEM,
         scratch_shapes=[
             pltpu.VMEM((groups, 8, r3), f32),
@@ -659,13 +652,14 @@
             pltpu.VMEM((CH, P_SIZE, P_SIZE), f32),
             pltpu.VMEM((boxes, nv, P_SIZE), f32),
         ]
+        + [pltpu.VMEM(a, f32) for a in acc_shapes * 2]
         + held
-        + [sems],
+        + [pltpu.SemaphoreType.DMA((8,))],
         compiler_params=params,
         name="finish",
     )(
-        morton, subtree_far.reshape(-1), near, far, near_halo, far_halo,
-        z1, gathered, front(group_skeleton), *bases,
+        morton, subtree_far.reshape(-1), z1, gathered, front(group_skeleton),
+        near, far, near_halo, far_halo, *bases,
     )
 
 

time: 132 us -> 133 us (level)
  no operation moved by 1% of the time
where the time goes in v6:
time: 133 us; the launch traced here: 132 us
  Pallas kernels  108 us (81%)
  between operations  13.5 us (10%)
  starting transfers between devices  9.16 us (7%)
    pallas_call x1, Pallas kernels, body(): pl.pallas_call(inner_kernel, out_shape=tuple((jax.ShapeDtypeStruct(a, f32...  45.4 us
    pallas_call x1, Pallas kernels, body(): pl.pallas_call(functools.partial(finish_kernel, groups=groups, sub_width=...  24.2 us
    pallas_call x1, Pallas kernels, body(): pl.pallas_call(outer_kernel, out_shape=tuple((jax.ShapeDtypeStruct(a, f32...  24.2 us
    pallas_call x1, Pallas kernels, body(): pl.pallas_call(arrange_kernel, out_shape=(jax.ShapeDtypeStruct((leaves //...  14.2 us
    ppermute x1, starting transfers between devices, body(): right = lax.ppermute(geo_lo, both, [(i + 1, i) for i in range(ends)])  7.24 us
  transfers between devices with their start and end apart: 3, of which 0 were waited for; matrix products, arithmetic and copies ran while one was open for 0% of the time, Pallas kernels for 53%

profile of v6, /device:TPU:4, one launch (start us, length us, event | category | flops | bytes accessed | tf_op | source)
XLA Modules:
  0.0 131.9 jit_solution(448985445607180264)
XLA Ops:
  6.5 0.0 all-gather.3.cloned.1.call-start
  6.5 14.2 %arrange.1 = (f32[32,56,128]{2,1,0:T(8,128)}, f32[32,56,128]{2,1,0:T(8,128)}, s32[8,128]{1,0:T(8,128)}, s32[8,128]{1,0:T(8,128)}, s32[8,128]{1,0:T(8,128)}, /*in...) custom-call(s32[8192]{0:T(1024)} %morton.3, s32[27,64]{1,0:T(8,128)} %bitcast.15, s32[24,64]{1,0:T(8,128)} %bitcast.16, ...), custom_call_target="tpu_custom_call" | custom-call | tf_op jit(solution)/shard_map/arrange/pallas_call | solution.py:559
  20.8 0.0 all-gather.3.cloned.1.call-update
  20.8 1.9 %collective-permute-start = (f32[32,56,128]{2,1,0:T(8,128)}, f32[32,56,128]{2,1,0:T(8,128)S(1)}, u32[]{:S(2)}, u32[]{:S(2)}) collective-permute-start(f32[32,56,128]{2,1,0:T(8,128)} %get-tuple-element.26.geo_hi), channel_id=1, source_target_pairs={{0,1},{1,2},{2,3},{3,4},{4,5},{5,6},{6,7},{7,8},{8,9},{9,10},{10,1... | collective-permute-start | bytes 2752520 | tf_op jit(solution)/shard_map/ppermute | solution.py:587
  22.7 7.2 %collective-permute-start.1 = (f32[32,56,128]{2,1,0:T(8,128)}, f32[32,56,128]{2,1,0:T(8,128)S(1)}, u32[]{:S(2)}, u32[]{:S(2)}) collective-permute-start(f32[32,56,128]{2,1,0:T(8,128)} %get-tuple-element.25.geo_lo), channel_id=1, source_target_pairs={{1,0},{2,1},{3,2},{4,3},{5,4},{6,5},{7,6},{8,7},{9,8},{10,9},{11,1... | collective-permute-start | bytes 2752520 | tf_op jit(solution)/shard_map/ppermute | solution.py:588
  30.0 45.4 %inner.1 = (f32[65,32,128]{2,1,0:T(8,128)}, f32[65,64,128]{2,1,0:T(8,128)}, bf16[65,64,128]{2,1,0:T(8,128)(2,1)}, bf16[65,64,128]{2,1,0:T(8,128)(2,1)}, f32[8,128]{1,0:T(8,128)}) custom-call(s32[1024]{0:T(1024)} %bitcast.23, s32[1024]{0:T(1024)} %bitcast.24, f32[32,56,128]{2,1,0:T(8,128)} %get-tuple-element.25.geo_lo, f32[32,56,128]{2,1,0:T(8,128)} %get-tuple-element.26.geo_hi), custom_call_target="tpu_custom_call" | custom-call | flops 20000000000 | bytes 10000000 | tf_op jit(solution)/shard_map/inner/pallas_call | solution.py:601
  75.4 0.0 collective-permute-done.left
  75.4 0.0 copy-start
  75.4 0.0 collective-permute-done.1.right
  75.4 0.0 copy-start.1
  75.4 0.9 copy-done
  76.3 0.3 copy-done.1
  76.6 24.2 %outer.1 = (f32[65,32,128]{2,1,0:T(8,128)}, f32[65,64,128]{2,1,0:T(8,128)}, f32[8,32,128]{2,1,0:T(8,128)}) custom-call(s32[1024]{0:T(1024)} %bitcast.21, s32[1024]{0:T(1024)} %bitcast.22, s32[4,8]{1,0:T(4,128)} %bitcast.25, f32[8,128]{1,0:T(8,128)} %get-tuple-element.27.origin, f32[32,56,128]{2,1,0:T(8,128)} %copy-done, f32[32,56,128]{2,1,0:T(8,128)} %copy-done.1, ...), custom_call_target="tpu_custom_call" | custom-call | flops 10000000000 | bytes 10000000 | tf_op jit(solution)/shard_map/outer/pallas_call | solution.py:617
  100.8 0.0 all-gather.3.cloned.1.call-done
  100.8 24.2 %finish.1 = f32[32,8192]{1,0:T(8,128)} custom-call(s32[8192]{0:T(1024)} %morton.3, s32[4]{0:T(128)} %bitcast.19, f32[8,32,128]{2,1,0:T(8,128)} %get-tuple-element.31.z1, f32[32,72,256]{2,1,0:T(8,128)} %bitcast.13, f32[3,4,256]{2,1,0:T(4,128)} %bitcast.17, f32[65,32,128]{2,1,0:T(8,128)} %get-tuple-element.33.rest_0_, ...), custom_call_target="tpu_custom_call" | custom-call | tf_op jit(solution)/shard_map/finish/pallas_call | solution.py:633
Async XLA Ops:
  6.5 94.2 %all-gather.3.cloned.1.call-start = ((), (), s32[]{:S(2)}) async-start(), calls=%async_computation | async-start | bytes 2433024 | tf_op jit(solution)/shard_map/all_gather | solution.py:589
  20.8 54.6 %collective-permute-start = (f32[32,56,128]{2,1,0:T(8,128)}, f32[32,56,128]{2,1,0:T(8,128)S(1)}, u32[]{:S(2)}, u32[]{:S(2)}) collective-permute-start(f32[32,56,128]{2,1,0:T(8,128)} %get-tuple-element.26.geo_hi), channel_id=1, source_target_pairs={{0,1},{1,2},{2,3},{3,4},{4,5},{5,6},{6,7},{7,8},{8,9},{9,10},{10,1... | collective-permute-start | bytes 2752520 | tf_op jit(solution)/shard_map/ppermute | solution.py:587
  22.7 52.6 %collective-permute-start.1 = (f32[32,56,128]{2,1,0:T(8,128)}, f32[32,56,128]{2,1,0:T(8,128)S(1)}, u32[]{:S(2)}, u32[]{:S(2)}) collective-permute-start(f32[32,56,128]{2,1,0:T(8,128)} %get-tuple-element.25.geo_lo), channel_id=1, source_target_pairs={{1,0},{2,1},{3,2},{4,3},{5,4},{6,5},{7,6},{8,7},{9,8},{10,9},{11,1... | collective-permute-start | bytes 2752520 | tf_op jit(solution)/shard_map/ppermute | solution.py:588
  75.4 0.9 copy-start
  75.4 1.2 copy-start.1
Sparse Core Ops, SparseCore 0:
  20.9 64.7 all-gather.2

commit v7 on v6

--- a/solution.py
+++ b/solution.py
@@ -388,9 +388,13 @@
 
 def outer_kernel(
     near_ids, far_ids, box_far, origin, left, right, tgt, tgt_far, q1, box_skel3,
-    near_out, far_out, z1,
+    near_hbm, far_hbm,
+    near_sum, far_sum, z1,
     src, xw, src_lo, src_hi, qw, near_dist, far_dist, box_skel,
+    near_out, far_out, near_own, far_own, sems,
+    *, near_factor, f0,
 ):
+    copies = fetch(((near_hbm, near_own), (far_hbm, far_own)), sems)
     boxes, box_width = q1.shape[0], box_far.shape[0]
     device = lax.axis_index("group") * lax.axis_size("sub") + lax.axis_index("sub")
     box_skel[...] = jnp.zeros_like(box_skel)
@@ -434,19 +438,34 @@
         near_pass(near_ids, src, tgt, xw, near_out, near_dist),
         far_pass(far_ids, src_lo, src_hi, tgt_far, qw, far_out, far_dist),
     )
+    for copy in copies:
+        copy.wait()
+
+    def combine(g, c):
+        for j in range(4):
+            parts = []
+            for half in range(2):
+                i = 8 * g + 2 * j + half
+                near_sum[i] = (near_own[i] + near_out[i]) * near_factor
+                turned = (far_own[i] + far_out[i]).T
+                parts.append((turned[0:32] + turned[32:64]) * f0)
+            far_sum[4 * g + j] = jnp.concatenate(parts, axis=1)
+        return c
+
+    lax.fori_loop(0, near_sum.shape[0] // 8, combine, 0)
 
 
 def finish_kernel(
-    morton, sub_far, z1, gathered, group_skel3, *rest,
-    groups, sub_width, near_factor, f0, f1, f2, f3,
+    morton, sub_far, near, far, z1, gathered, group_skel3, *rest,
+    groups, sub_width, f1, f2, f3,
 ):
-    fetched = rest[:8]
-    out, group_skel, rows, pad, tall, tall_too, l1s = rest[8:15]
-    held, sems = rest[15:23], rest[23]
-    near_own, far_own, near, far, basis, leaf_tr, box_tr, sub_tr = held
+    fetched = rest[:4]
+    out, group_skel, rows, pad, tall, tall_too, l1s = rest[4:11]
+    held, sems = rest[11:15], rest[15]
+    basis, leaf_tr, box_tr, sub_tr = held
     copies = fetch(tuple(zip(fetched, held))[::-1], sems)
     boxes = z1.shape[0]
-    leaves = near.shape[0] - 1
+    leaves = near.shape[0]
     group = lax.axis_index("group")
     subs = lax.axis_size("sub")
     device = group * subs + lax.axis_index("sub")
@@ -502,9 +521,9 @@
             for k in range(P_SIZE):
                 rows[pl.ds(row_of(morton, old, j * P_SIZE + k), 1), :] = held[j, k : k + 1, :]
             i = b * CH + j
-            turned = (far_own[i] + far[i]).T
-            l0 = (turned[0:32] + turned[32:64]) * f0 + hdot_nt(l1, leaf_tr[i])
-            pad[j, 0:32, :] = (near_own[i] + near[i]) * near_factor + hdot(l0, basis[i])
+            side = 64 * (j % 2)
+            l0 = far[b * (CH // 2) + j // 2, :, side : side + 64] + hdot_nt(l1, leaf_tr[i])
+            pad[j, 0:32, :] = near[i] + hdot(l0, basis[i])
             into[j] = pad[j].T
 
     def scatter(b, held):
@@ -614,20 +633,29 @@
         name="inner",
     )(near_ids.reshape(-1), far_ids.reshape(-1), geo_lo, geo_hi)
 
-    near_halo, far_halo, z1 = pl.pallas_call(
-        outer_kernel,
-        out_shape=tuple(
-            jax.ShapeDtypeStruct(a, f32) for a in acc_shapes + ((boxes, nv, r1),)
+    near, far, z1 = pl.pallas_call(
+        functools.partial(
+            outer_kernel,
+            near_factor=(P_SIZE * near_list.shape[1]) ** -0.5,
+            f0=(r0 * leaf_far.shape[1]) ** -0.5,
         ),
-        in_specs=[SMEM] * 3 + [VMEM] * 7,
+        out_shape=(
+            jax.ShapeDtypeStruct((leaves, nv, P_SIZE), f32),
+            jax.ShapeDtypeStruct((leaves // 2, nv, 2 * r0), f32),
+            jax.ShapeDtypeStruct((boxes, nv, r1), f32),
+        ),
+        in_specs=[SMEM] * 3 + [VMEM] * 7 + [ANY] * 2,
         out_specs=(VMEM,) * 3,
-        scratch_shapes=tables + [pltpu.VMEM((boxes, 8, r1), f32)],
+        scratch_shapes=tables
+        + [pltpu.VMEM((boxes, 8, r1), f32)]
+        + [pltpu.VMEM(a, f32) for a in acc_shapes * 2]
+        + [pltpu.SemaphoreType.DMA((2,))],
         compiler_params=params,
         cost_estimate=pl.CostEstimate(flops=10**10, bytes_accessed=10**7, transcendentals=3 * 10**7),
         name="outer",
     )(
         near_ids_out.reshape(-1), far_ids_out.reshape(-1), box_far.T,
-        origin, left, right, tgt, tgt_far, q1, front(box_skeleton),
+        origin, left, right, tgt, tgt_far, q1, front(box_skeleton), near, far,
     )
 
     return pl.pallas_call(
@@ -635,14 +663,12 @@
             finish_kernel,
             groups=groups,
             sub_width=subtree_far.shape[1],
-            near_factor=(P_SIZE * near_list.shape[1]) ** -0.5,
-            f0=(r0 * leaf_far.shape[1]) ** -0.5,
             f1=(r1 * box_far.shape[1]) ** -0.5,
             f2=(r2 * subtree_far.shape[1]) ** -0.5,
             f3=r3**-0.5,
         ),
         out_shape=jax.ShapeDtypeStruct((nv, count), f32),
-        in_specs=[SMEM] * 2 + [VMEM] * 3 + [ANY] * 8,
+        in_specs=[SMEM] * 2 + [VMEM] * 5 + [ANY] * 4,
         out_specs=VMEM,
         scratch_shapes=[
             pltpu.VMEM((groups, 8, r3), f32),
@@ -652,14 +678,12 @@
             pltpu.VMEM((CH, P_SIZE, P_SIZE), f32),
             pltpu.VMEM((boxes, nv, P_SIZE), f32),
         ]
-        + [pltpu.VMEM(a, f32) for a in acc_shapes * 2]
         + held
-        + [pltpu.SemaphoreType.DMA((8,))],
+        + [sems],
         compiler_params=params,
         name="finish",
     )(
-        morton, subtree_far.reshape(-1), z1, gathered, front(group_skeleton),
-        near, far, near_halo, far_halo, *bases,
+        morton, subtree_far.reshape(-1), near, far, z1, gathered, front(group_skeleton), *bases,
     )
 
 

time: 133 us -> 133 us (level)
    pallas_call x1, Pallas kernels: 45.4 us -> 42.9 us  [body(): pl.pallas_call(inner_kernel, out_shape=tuple((jax.ShapeDtypeStruct(a, f32...]
    pallas_call x1, Pallas kernels: 24.2 us -> 25.8 us  [body(): pl.pallas_call(functools.partial(outer_kernel, near_factor=(P_SIZE * near...]
  transfers between devices with their start and end apart: 3 -> 3, of which waited for: 0 -> 0; matrix products, arithmetic and copies ran while one was open for 0% -> 0% of each run, Pallas kernels for 53% -> 52%
where the time goes in v7:
time: 133 us; the launch traced here: 132 us
  Pallas kernels  108 us (81%)
  between operations  13.5 us (10%)
  starting transfers between devices  9.16 us (7%)
    pallas_call x1, Pallas kernels, body(): pl.pallas_call(inner_kernel, out_shape=tuple((jax.ShapeDtypeStruct(a, f32...  42.9 us
    pallas_call x1, Pallas kernels, body(): pl.pallas_call(functools.partial(outer_kernel, near_factor=(P_SIZE * near...  25.8 us
    pallas_call x1, Pallas kernels, body(): pl.pallas_call(functools.partial(finish_kernel, groups=groups, sub_width=...  24.8 us
    pallas_call x1, Pallas kernels, body(): pl.pallas_call(arrange_kernel, out_shape=(jax.ShapeDtypeStruct((leaves //...  14.3 us
    ppermute x1, starting transfers between devices, body(): right = lax.ppermute(geo_lo, both, [(i + 1, i) for i in range(ends)])  7.24 us
  transfers between devices with their start and end apart: 3, of which 0 were waited for; matrix products, arithmetic and copies ran while one was open for 0% of the time, Pallas kernels for 52%

profile of v7, /device:TPU:4, one launch (start us, length us, event | category | flops | bytes accessed | tf_op | source)
XLA Modules:
  0.0 131.6 jit_solution(10741554809559581170)
XLA Ops:
  6.5 0.0 all-gather.3.cloned.1.call-start
  6.5 14.3 %arrange.1 = (f32[32,56,128]{2,1,0:T(8,128)}, f32[32,56,128]{2,1,0:T(8,128)}, s32[8,128]{1,0:T(8,128)}, s32[8,128]{1,0:T(8,128)}, s32[8,128]{1,0:T(8,128)}, /*in...) custom-call(s32[8192]{0:T(1024)} %morton.3, s32[27,64]{1,0:T(8,128)} %bitcast.15, s32[24,64]{1,0:T(8,128)} %bitcast.16, ...), custom_call_target="tpu_custom_call" | custom-call | tf_op jit(solution)/shard_map/arrange/pallas_call | solution.py:578
  20.8 0.0 all-gather.3.cloned.1.call-update
  20.8 1.9 %collective-permute-start = (f32[32,56,128]{2,1,0:T(8,128)}, f32[32,56,128]{2,1,0:T(8,128)S(1)}, u32[]{:S(2)}, u32[]{:S(2)}) collective-permute-start(f32[32,56,128]{2,1,0:T(8,128)} %get-tuple-element.26.geo_hi), channel_id=1, source_target_pairs={{0,1},{1,2},{2,3},{3,4},{4,5},{5,6},{6,7},{7,8},{8,9},{9,10},{10,1... | collective-permute-start | bytes 2752520 | tf_op jit(solution)/shard_map/ppermute | solution.py:606
  22.8 7.2 %collective-permute-start.1 = (f32[32,56,128]{2,1,0:T(8,128)}, f32[32,56,128]{2,1,0:T(8,128)S(1)}, u32[]{:S(2)}, u32[]{:S(2)}) collective-permute-start(f32[32,56,128]{2,1,0:T(8,128)} %get-tuple-element.25.geo_lo), channel_id=1, source_target_pairs={{1,0},{2,1},{3,2},{4,3},{5,4},{6,5},{7,6},{8,7},{9,8},{10,9},{11,1... | collective-permute-start | bytes 2752520 | tf_op jit(solution)/shard_map/ppermute | solution.py:607
  30.0 42.9 %inner.1 = (f32[65,32,128]{2,1,0:T(8,128)}, f32[65,64,128]{2,1,0:T(8,128)}, bf16[65,64,128]{2,1,0:T(8,128)(2,1)}, bf16[65,64,128]{2,1,0:T(8,128)(2,1)}, f32[8,128]{1,0:T(8,128)}) custom-call(s32[1024]{0:T(1024)} %bitcast.23, s32[1024]{0:T(1024)} %bitcast.24, f32[32,56,128]{2,1,0:T(8,128)} %get-tuple-element.25.geo_lo, f32[32,56,128]{2,1,0:T(8,128)} %get-tuple-element.26.geo_hi), custom_call_target="tpu_custom_call" | custom-call | flops 20000000000 | bytes 10000000 | tf_op jit(solution)/shard_map/inner/pallas_call | solution.py:620
  72.9 0.0 collective-permute-done.left
  72.9 0.0 copy-start
  72.9 0.0 collective-permute-done.1.right
  72.9 0.0 copy-start.1
  72.9 1.0 copy-done
  73.9 0.2 copy-done.1
  74.1 25.8 %outer.1 = (f32[64,32,128]{2,1,0:T(8,128)}, f32[32,32,128]{2,1,0:T(8,128)}, f32[8,32,128]{2,1,0:T(8,128)}) custom-call(s32[1024]{0:T(1024)} %bitcast.21, s32[1024]{0:T(1024)} %bitcast.22, s32[4,8]{1,0:T(4,128)} %bitcast.25, f32[8,128]{1,0:T(8,128)} %get-tuple-element.27.origin, f32[32,56,128]{2,1,0:T(8,128)} %copy-done, f32[32,56,128]{2,1,0:T(8,128)} %copy-done.1, ...), custom_call_target="tpu_custom_call" | custom-call | flops 10000000000 | bytes 10000000 | tf_op jit(solution)/shard_map/outer/pallas_call | solution.py:636
  99.9 0.0 all-gather.3.cloned.1.call-done
  99.9 24.8 %finish.1 = f32[32,8192]{1,0:T(8,128)} custom-call(s32[8192]{0:T(1024)} %morton.3, s32[4]{0:T(128)} %bitcast.19, f32[64,32,128]{2,1,0:T(8,128)} %get-tuple-element.33.near, f32[32,32,128]{2,1,0:T(8,128)} %get-tuple-element.34.far, f32[8,32,128]{2,1,0:T(8,128)} %get-tuple-element.35.z1, f32[32,72,256]{2,1,0:T(8,128)} %bitcast.13, f32[3,4,256]{2,1,0:T(4,128)} %bitcast.17, ...), custom_call_target="tpu_custom_call" | custom-call | tf_op jit(solution)/shard_map/finish/pallas_call | solution.py:661
Async XLA Ops:
  6.5 93.4 %all-gather.3.cloned.1.call-start = ((), (), s32[]{:S(2)}) async-start(), calls=%async_computation | async-start | bytes 2433024 | tf_op jit(solution)/shard_map/all_gather | solution.py:608
  20.8 52.0 %collective-permute-start = (f32[32,56,128]{2,1,0:T(8,128)}, f32[32,56,128]{2,1,0:T(8,128)S(1)}, u32[]{:S(2)}, u32[]{:S(2)}) collective-permute-start(f32[32,56,128]{2,1,0:T(8,128)} %get-tuple-element.26.geo_hi), channel_id=1, source_target_pairs={{0,1},{1,2},{2,3},{3,4},{4,5},{5,6},{6,7},{7,8},{8,9},{9,10},{10,1... | collective-permute-start | bytes 2752520 | tf_op jit(solution)/shard_map/ppermute | solution.py:606
  22.8 50.1 %collective-permute-start.1 = (f32[32,56,128]{2,1,0:T(8,128)}, f32[32,56,128]{2,1,0:T(8,128)S(1)}, u32[]{:S(2)}, u32[]{:S(2)}) collective-permute-start(f32[32,56,128]{2,1,0:T(8,128)} %get-tuple-element.25.geo_lo), channel_id=1, source_target_pairs={{1,0},{2,1},{3,2},{4,3},{5,4},{6,5},{7,6},{8,7},{9,8},{10,9},{11,1... | collective-permute-start | bytes 2752520 | tf_op jit(solution)/shard_map/ppermute | solution.py:607
  72.9 1.0 copy-start
  72.9 1.2 copy-start.1
Sparse Core Ops, SparseCore 0:
  21.0 64.6 all-gather.2

commit v8 on v4

--- a/solution.py
+++ b/solution.py
@@ -376,13 +376,13 @@
 
     def load(g, c):
         for geo, start in ((geo_lo, 0), (geo_hi, half)):
-            for j in range(4):
-                i = g * 4 + j
+            for j in range(8):
+                i = g * 8 + j
                 t8, kt8 = prepare_source(geo[i], i + start, first, centre_sk, *sources)
                 prepare_target(t8, kt8, i + start, tgt, tgt_far)
         return c
 
-    lax.fori_loop(0, half // 4, load, 0)
+    lax.fori_loop(0, half // 8, load, 0)
     clear(sources, NONE)
     clear((tgt, tgt_far), leaves)
     run(
@@ -428,12 +428,12 @@
 
     def load(g, c):
         for block, start in ((left, 0), (right, HALO)):
-            for j in range(4):
-                i = g * 4 + j
+            for j in range(8):
+                i = g * 8 + j
                 prepare_source(block[i], i + start, first, centre_sk, *sources)
         return c
 
-    lax.fori_loop(0, HALO // 4, load, 0)
+    lax.fori_loop(0, HALO // 8, load, 0)
     clear(sources, NONE)
     run(
         near_pass(near_ids, src, tgt, xw, near_out, near_dist),

time: 132 us -> 130 us (0.985); the launches traced: 132 us -> 129 us
  Pallas kernels: 108 us -> 105 us
    pallas_call x1, Pallas kernels: 25.2 us -> 23 us  [body(): pl.pallas_call(outer_kernel, out_shape=tuple((jax.ShapeDtypeStruct(a, f32...]
  transfers between devices with their start and end apart: 3 -> 3, of which waited for: 0 -> 0; matrix products, arithmetic and copies ran while one was open for 0% -> 0% of each run, Pallas kernels for 53% -> 52%
where the time goes in v8:
time: 130 us; the launch traced here: 129 us
  Pallas kernels  105 us (81%)
  between operations  13.5 us (10%)
  starting transfers between devices  9.16 us (7%)
    pallas_call x1, Pallas kernels, body(): pl.pallas_call(inner_kernel, out_shape=tuple((jax.ShapeDtypeStruct(a, f32...  44.1 us
    pallas_call x1, Pallas kernels, body(): pl.pallas_call(functools.partial(finish_kernel, groups=groups, sub_width=...  23.6 us
    pallas_call x1, Pallas kernels, body(): pl.pallas_call(outer_kernel, out_shape=tuple((jax.ShapeDtypeStruct(a, f32...  23 us
    pallas_call x1, Pallas kernels, body(): pl.pallas_call(arrange_kernel, out_shape=(jax.ShapeDtypeStruct((leaves //...  14.2 us
    ppermute x1, starting transfers between devices, body(): right = lax.ppermute(geo_lo, both, [(i + 1, i) for i in range(ends)])  7.24 us
  transfers between devices with their start and end apart: 3, of which 0 were waited for; matrix products, arithmetic and copies ran while one was open for 0% of the time, Pallas kernels for 52%

profile of v8, /device:TPU:4, one launch (start us, length us, event | category | flops | bytes accessed | tf_op | source)
XLA Modules:
  0.0 128.8 jit_solution(12013463660029947371)
XLA Ops:
  6.5 0.0 all-gather.3.cloned.1.call-start
  6.5 14.2 %arrange.1 = (f32[32,56,128]{2,1,0:T(8,128)}, f32[32,56,128]{2,1,0:T(8,128)}, s32[8,128]{1,0:T(8,128)}, s32[8,128]{1,0:T(8,128)}, s32[8,128]{1,0:T(8,128)}, /*in...) custom-call(s32[8192]{0:T(1024)} %morton.3, s32[27,64]{1,0:T(8,128)} %bitcast.15, s32[24,64]{1,0:T(8,128)} %bitcast.16, ...), custom_call_target="tpu_custom_call" | custom-call | tf_op jit(solution)/shard_map/arrange/pallas_call | solution.py:566
  20.8 0.0 all-gather.3.cloned.1.call-update
  20.8 1.9 %collective-permute-start = (f32[32,56,128]{2,1,0:T(8,128)}, f32[32,56,128]{2,1,0:T(8,128)S(1)}, u32[]{:S(2)}, u32[]{:S(2)}) collective-permute-start(f32[32,56,128]{2,1,0:T(8,128)} %get-tuple-element.24.geo_hi), channel_id=1, source_target_pairs={{0,1},{1,2},{2,3},{3,4},{4,5},{5,6},{6,7},{7,8},{8,9},{9,10},{10,1... | collective-permute-start | bytes 2752520 | tf_op jit(solution)/shard_map/ppermute | solution.py:594
  22.7 7.2 %collective-permute-start.1 = (f32[32,56,128]{2,1,0:T(8,128)}, f32[32,56,128]{2,1,0:T(8,128)S(1)}, u32[]{:S(2)}, u32[]{:S(2)}) collective-permute-start(f32[32,56,128]{2,1,0:T(8,128)} %get-tuple-element.23.geo_lo), channel_id=1, source_target_pairs={{1,0},{2,1},{3,2},{4,3},{5,4},{6,5},{7,6},{8,7},{9,8},{10,9},{11,1... | collective-permute-start | bytes 2752520 | tf_op jit(solution)/shard_map/ppermute | solution.py:595
  30.0 44.1 %inner.1 = (f32[65,32,128]{2,1,0:T(8,128)}, f32[65,64,128]{2,1,0:T(8,128)}, bf16[65,64,128]{2,1,0:T(8,128)(2,1)}, bf16[65,64,128]{2,1,0:T(8,128)(2,1)}, f32[8,128]{1,0:T(8,128)}) custom-call(s32[1024]{0:T(1024)} %bitcast.23, s32[1024]{0:T(1024)} %bitcast.24, f32[32,56,128]{2,1,0:T(8,128)} %get-tuple-element.23.geo_lo, f32[32,56,128]{2,1,0:T(8,128)} %get-tuple-element.24.geo_hi), custom_call_target="tpu_custom_call" | custom-call | flops 20000000000 | bytes 10000000 | tf_op jit(solution)/shard_map/inner/pallas_call | solution.py:608
  74.1 0.0 collective-permute-done.left
  74.1 0.0 copy-start
  74.1 0.0 collective-permute-done.1.right
  74.1 0.0 copy-start.1
  74.2 0.9 copy-done
  75.1 0.3 copy-done.1
  75.4 23.0 %outer.1 = (f32[65,32,128]{2,1,0:T(8,128)}, f32[65,64,128]{2,1,0:T(8,128)}, f32[8,32,128]{2,1,0:T(8,128)}) custom-call(s32[1024]{0:T(1024)} %bitcast.21, s32[1024]{0:T(1024)} %bitcast.22, s32[4,8]{1,0:T(4,128)} %bitcast.25, f32[8,128]{1,0:T(8,128)} %get-tuple-element.29.origin, f32[32,56,128]{2,1,0:T(8,128)} %copy-done, f32[32,56,128]{2,1,0:T(8,128)} %copy-done.1, ...), custom_call_target="tpu_custom_call" | custom-call | flops 10000000000 | bytes 10000000 | tf_op jit(solution)/shard_map/outer/pallas_call | solution.py:624
  98.3 0.0 all-gather.3.cloned.1.call-done
  98.3 23.6 %finish.1 = f32[32,8192]{1,0:T(8,128)} custom-call(s32[8192]{0:T(1024)} %morton.3, s32[4]{0:T(128)} %bitcast.19, f32[65,32,128]{2,1,0:T(8,128)} %get-tuple-element.25.near_own, f32[65,64,128]{2,1,0:T(8,128)} %get-tuple-element.26.far_own, f32[65,32,128]{2,1,0:T(8,128)} %get-tuple-element.33.near, f32[65,64,128]{2,1,0:T(8,128)} %get-tuple-element.34.far, ...), custom_call_target="tpu_custom_call" | custom-call | tf_op jit(solution)/shard_map/finish/pallas_call | solution.py:640
Async XLA Ops:
  6.5 91.8 %all-gather.3.cloned.1.call-start = ((), (), s32[]{:S(2)}) async-start(), calls=%async_computation | async-start | bytes 2433024 | tf_op jit(solution)/shard_map/all_gather | solution.py:596
  20.8 53.3 %collective-permute-start = (f32[32,56,128]{2,1,0:T(8,128)}, f32[32,56,128]{2,1,0:T(8,128)S(1)}, u32[]{:S(2)}, u32[]{:S(2)}) collective-permute-start(f32[32,56,128]{2,1,0:T(8,128)} %get-tuple-element.24.geo_hi), channel_id=1, source_target_pairs={{0,1},{1,2},{2,3},{3,4},{4,5},{5,6},{6,7},{7,8},{8,9},{9,10},{10,1... | collective-permute-start | bytes 2752520 | tf_op jit(solution)/shard_map/ppermute | solution.py:594
  22.7 51.4 %collective-permute-start.1 = (f32[32,56,128]{2,1,0:T(8,128)}, f32[32,56,128]{2,1,0:T(8,128)S(1)}, u32[]{:S(2)}, u32[]{:S(2)}) collective-permute-start(f32[32,56,128]{2,1,0:T(8,128)} %get-tuple-element.23.geo_lo), channel_id=1, source_target_pairs={{1,0},{2,1},{3,2},{4,3},{5,4},{6,5},{7,6},{8,7},{9,8},{10,9},{11,1... | collective-permute-start | bytes 2752520 | tf_op jit(solution)/shard_map/ppermute | solution.py:595
  74.1 0.9 copy-start
  74.1 1.2 copy-start.1
Sparse Core Ops, SparseCore 0:
  20.9 64.6 all-gather.2
